TPU v7x, 128 devices: a whole 4x4x4 slice. The times are simulated.
128 devices in a mesh: leaf: 64 (over z, y, x), front: 2 (over core).
Axes of the slice: x: 4, y: 4, z: 4, core: 2. Of those that a mesh axis runs over, the one named last changes fastest.
Arguments:
- rhs_parts: bfloat16 [64, 2, 1152, 256], P('leaf', 'front'), may hold values from -6 to 6
- send_order: int32 [64, 2, 1152], P('leaf', 'front'), may hold values from 0 to 1151, each once within a row
- recv_place: int32 [64, 2, 1152], P('leaf', 'front'), may hold values from 0 to 1151, each once within a row
- sep_rhs: bfloat16 [64, 2, 3, 16, 256], P('leaf', 'front'), may hold values from -6 to 6
- leaf_inv: bfloat16 [64, 2, 1152, 1152], P('leaf', 'front'), as said below
- leaf_panels: bfloat16 [64, 2, 3, 64, 1152], P('leaf', 'front'), may hold values from -0.1875 to 0.1875
- leaf_rows: int32 [64, 2, 3, 64], P('leaf', 'front'), may hold values from 0 to 255, as said below
- sep_inv: bfloat16 [64, 2, 32, 224], P('leaf', 'front'), as said below
- sep_panels: bfloat16 [64, 2, 3, 64, 16], P('leaf', 'front'), may hold values from -1.5 to 1.5
- sep_rows: int32 [64, 2, 3, 64], P('leaf', 'front'), may hold values from 0 to 255, as said below
Outputs:
- leaf_solution: float32 [64, 2, 1152, 256], P('leaf', 'front')
- sep_solution: bfloat16 [64, 2, 3, 16, 256], P('leaf', 'front')
Inputs may be any that keep to these rules, and one draw needn't show every extreme that they name: Each block of leaf_inv is lower triangular with a positive diagonal. Each E_m[g] assembled from sep_inv is lower triangular with a positive diagonal. `leaf_rows`: within one device's block for level m the 64 row numbers are distinct, ascending and below S_m; each block holds row 0 and row S_m - 1. `sep_rows`: within one device's block for pair (m, k) the 64 row numbers are distinct, ascending and below S_k; each block holds row 0 and row S_k - 1.
All inputs are finite; a program needn't handle non-finite values.
Results may differ from a plain program's by a relative error of at most 0.018.
Values may be sent and summed in bfloat16 or wider, within the bound.
No kernel may reach another device: no remote copies, remote signals or barrier semaphores. Data moves between devices by JAX's collectives and lax.ppermute only.
A program may use at most 64 MiB of HBM per device.

v0:
```python
import jax
import jax.numpy as jnp
from jax import lax
from jax.sharding import PartitionSpec as P


def from_partner(block, axis, stride):
    count = lax.axis_size(axis)
    route = []
    for low in range(count):
        high = low | 1 << stride
        if high != low and high < count:
            route += [(low, high), (high, low)]
    return lax.ppermute(block, axis, route)


def ancestor_pairs(levels_n):
    listing = []
    for lower_lvl in range(levels_n):
        for upper_lvl in range(lower_lvl + 1, levels_n):
            listing.append((lower_lvl, upper_lvl))
    return listing


def on_device(
    rhs_parts,
    send_order,
    recv_place,
    sep_rhs,
    leaf_inv,
    leaf_panels,
    leaf_rows,
    sep_inv,
    sep_panels,
    sep_rows,
):
    leaves = lax.axis_size("leaf")
    fronts = lax.axis_size("front")
    leaf_idx = lax.axis_index("leaf")
    front_idx = lax.axis_index("front")
    rhs_rows = rhs_parts[0, 0]
    leaf_len = rhs_rows.shape[0]
    rhs_width = rhs_rows.shape[1]
    levels_n = sep_rhs.shape[2]
    sub_rows = sep_rhs.shape[3]
    block_rows = sub_rows * fronts
    pair_list = ancestor_pairs(levels_n)
    outgoing = rhs_rows[send_order[0, 0]].reshape(leaves, leaf_len // leaves, rhs_width)
    incoming = lax.all_to_all(outgoing, "leaf", split_axis=0, concat_axis=0, tiled=True)
    owned_rows = (
        jnp.zeros((leaf_len, rhs_width), jnp.bfloat16)
        .at[recv_place[0, 0]]
        .set(incoming.reshape(leaf_len, rhs_width))
    )
    factor_leaf = leaf_inv[0, 0]
    leaf_y = jnp.dot(factor_leaf, owned_rows, preferred_element_type=jnp.float32)
    leaf_yb = leaf_y.astype(jnp.bfloat16)
    pending = []
    for height in range(levels_n):
        group_span = 2 ** (height + 1)
        order_sep = group_span * block_rows
        pushed = jnp.dot(leaf_panels[0, 0, height], leaf_yb, preferred_element_type=jnp.float32)
        summed = (
            jnp.zeros((order_sep, rhs_width), jnp.float32).at[leaf_rows[0, 0, height]].add(pushed)
        )
        offset_row = leaf_idx % group_span * block_rows + front_idx * sub_rows
        current = lax.dynamic_slice_in_dim(summed, offset_row, sub_rows, 0)
        summed = lax.dynamic_update_slice_in_dim(
            summed, current - sep_rhs[0, 0, height].astype(jnp.float32), offset_row, 0
        )
        pending.append(summed)
    sep_y = []
    for height in range(levels_n):
        group_span = 2 ** (height + 1)
        part_cols = group_span * sub_rows
        start_col = sub_rows * (group_span - 2)
        factor_blk = sep_inv[0, 0, :, start_col : start_col + part_cols]
        col_block = lax.psum_scatter(pending[height], "front", scatter_dimension=0, tiled=True)
        for bit_idx in range(height + 1):
            col_block = col_block + from_partner(col_block, "leaf", bit_idx)
        right_side = (-col_block).astype(jnp.bfloat16)
        partial_value = jnp.dot(factor_blk, right_side, preferred_element_type=jnp.float32)
        yslice = lax.psum_scatter(partial_value, "front", scatter_dimension=0, tiled=True)
        sep_y.append(yslice)
        rounded = yslice.astype(jnp.bfloat16)
        for pair_idx, (lower_lvl, upper_lvl) in enumerate(pair_list):
            if lower_lvl == height:
                pushed = jnp.dot(
                    sep_panels[0, 0, pair_idx], rounded, preferred_element_type=jnp.float32
                )
                pending[upper_lvl] = pending[upper_lvl].at[sep_rows[0, 0, pair_idx]].add(pushed)
    sep_x = [None] * levels_n
    sep_out = [None] * levels_n
    for height in reversed(range(levels_n)):
        group_span = 2 ** (height + 1)
        part_cols = group_span * sub_rows
        start_col = sub_rows * (group_span - 2)
        factor_blk = sep_inv[0, 0, :, start_col : start_col + part_cols]
        carried = jnp.zeros((sub_rows, rhs_width), jnp.float32)
        for pair_idx, (lower_lvl, upper_lvl) in enumerate(pair_list):
            if lower_lvl == height:
                picked = sep_x[upper_lvl][sep_rows[0, 0, pair_idx]]
                carried = carried + jnp.dot(
                    sep_panels[0, 0, pair_idx].T, picked, preferred_element_type=jnp.float32
                )
        residue = (sep_y[height] - carried).astype(jnp.bfloat16)
        x_block = jnp.dot(
            factor_blk.T,
            lax.all_gather(residue, "front", axis=0, tiled=True),
            preferred_element_type=jnp.float32,
        )
        for bit_idx in range(height + 1):
            x_block = x_block + from_partner(x_block, "leaf", bit_idx)
        whole_x = lax.all_gather(x_block.astype(jnp.bfloat16), "front", axis=0, tiled=True)
        sep_x[height] = whole_x
        offset_row = leaf_idx % group_span * block_rows + front_idx * sub_rows
        sep_out[height] = lax.dynamic_slice_in_dim(whole_x, offset_row, sub_rows, 0)
    carried = jnp.zeros((leaf_len, rhs_width), jnp.float32)
    for height in range(levels_n):
        picked = sep_x[height][leaf_rows[0, 0, height]]
        carried = carried + jnp.dot(
            leaf_panels[0, 0, height].T, picked, preferred_element_type=jnp.float32
        )
    residue = (leaf_y - carried).astype(jnp.bfloat16)
    leaf_solution = jnp.dot(factor_leaf.T, residue, preferred_element_type=jnp.float32)
    sep_solution = jnp.stack(sep_out, axis=0)
    return (leaf_solution[None, None], sep_solution[None, None])


def solution(mesh):
    in_specs = (
        P("leaf", "front", None, None),
        P("leaf", "front", None),
        P("leaf", "front", None),
        P("leaf", "front", None, None, None),
        P("leaf", "front", None, None),
        P("leaf", "front", None, None, None),
        P("leaf", "front", None, None),
        P("leaf", "front", None, None),
        P("leaf", "front", None, None, None),
        P("leaf", "front", None, None),
    )
    out_specs = (P("leaf", "front", None, None), P("leaf", "front", None, None, None))
    return jax.shard_map(
        on_device, mesh=mesh, in_specs=in_specs, out_specs=out_specs, check_vma=False
    )
```

profile of v0, /device:TPU:1, one launch (start us, length us, event | category | flops | bytes accessed | tf_op | source)
XLA Modules:
  0.0 234.1 jit_solution(3228426880737750054)
XLA Ops:
  7.2 0.9 fusion.50
  8.1 4.4 %gather_fusion = bf16[1152,256]{1,0:T(8,128)(2,1)S(1)} fusion(bf16[1152,256]{1,0:T(8,128)(2,1)} %bitcast.148, s32[2048]{0:T(1024)S(1)} %pad_clamp_fusion), kind=kCustom, calls=%fused_computation | custom fusion | bytes 1184256 | tf_op jit(solution)/shard_map/gather | solution.py:48
  12.5 1.1 reshape.240
  13.5 12.1 %all-to-all-start = ((bf16[64,18,256]{2,1,0:T(8,128)(2,1)}), bf16[64,18,256]{2,1,0:T(8,128)(2,1)S(1)}, u32[]{:S(2)}, u32[]{:S(2)}) async-start(bf16[64,18,256]{2,1,0:T(8,128)(2,1)} %reshape.240), calls=%async_computation | async-start | bytes 1572864 | tf_op jit(solution)/shard_map/all_to_all | solution.py:49
  26.3 14.3 %all-to-all-done = bf16[64,18,256]{2,1,0:T(8,128)(2,1)S(1)} async-done(((bf16[64,18,256]{2,1,0:T(8,128)(2,1)}), bf16[64,18,256]{2,1,0:T(8,128)(2,1)S(1)}, u32[]{:S(2)}, u32[]{:S(2)}) %all-to-all-start) | async-done | bytes 589856 | tf_op jit(solution)/shard_map/all_to_all | solution.py:49
  40.6 1.0 reshape.305
  41.6 9.0 %scatter_custom_fusion = bf16[1152,256]{1,0:T(8,128)(2,1)} fusion(s32[1152]{0:T(1024)S(1)} %fusion.49, bf16[1152,256]{1,0:T(8,128)(2,1)} %reshape.305, bf16[]{:T(256)} %constant.54.clone.1), kind=kCustom, calls=%fused_computation.41 | custom fusion | bytes 590336 | tf_op jit(solution)/shard_map/scatter | solution.py:53
  50.5 2.2 fusion.2
  53.0 1.0 convolution_bitcast_fusion.5
  54.3 1.0 scatter_custom_fusion.2
  55.3 1.1 scatter_custom_fusion.1
  56.4 1.3 scatter_custom_fusion.4
  59.1 7.8 %reduce-scatter.9.cloned.1.call-done = f32[32,256]{1,0:T(8,128)} async-done(((f32[64,256]{1,0:T(8,128)}), f32[32,256]{1,0:T(8,128)}) %reduce-scatter.9.cloned.1.call-update) | async-done | bytes 32784 | tf_op jit(solution)/shard_map/reduce_scatter | solution.py:78
  66.9 1.3 collective-permute-start
  68.2 1.7 collective-permute-done
  69.9 1.5 convolution_bitcast_fusion.11
  71.5 1.3 fusion.71
  72.7 11.4 %reduce-scatter.11.cloned.1.call-done = f32[16,256]{1,0:T(8,128)} async-done(((f32[32,256]{1,0:T(8,128)}), f32[16,256]{1,0:T(8,128)}) %reduce-scatter.11.cloned.1.call-update) | async-done | bytes 16400 | tf_op jit(solution)/shard_map/reduce_scatter | solution.py:83
  84.1 0.9 convolution_bitcast_fusion.6
  85.0 1.1 scatter_fusion
  86.9 11.6 %reduce-scatter.13.cloned.1.call-done = f32[64,256]{1,0:T(8,128)} async-done(((f32[128,256]{1,0:T(8,128)}), f32[64,256]{1,0:T(8,128)}) %reduce-scatter.13.cloned.1.call-update) | async-done | bytes 65552 | tf_op jit(solution)/shard_map/reduce_scatter | solution.py:78
  98.6 1.3 collective-permute-start.1
  99.8 2.6 %collective-permute-done.1 = f32[64,256]{1,0:T(8,128)S(1)} collective-permute-done((f32[64,256]{1,0:T(8,128)}, f32[64,256]{1,0:T(8,128)S(1)}, u32[]{:S(2)}, u32[]{:S(2)}) %collective-permute-start.1) | collective-permute-done | bytes 65568 | tf_op jit(solution)/shard_map/ppermute | solution.py:14
  102.4 0.8 add.212
  103.3 2.8 %collective-permute-start.2 = (f32[64,256]{1,0:T(8,128)S(1)}, f32[64,256]{1,0:T(8,128)S(1)}, u32[]{:S(2)}, u32[]{:S(2)}) collective-permute-start(f32[64,256]{1,0:T(8,128)S(1)} %add.212), channel_id=1, source_target_pairs={{0,4},{4,0},{2,6},{6,2},{8,12},{12,8},{10,14},{14,10},{16,20},{20,... | collective-permute-start | bytes 196616 | tf_op jit(solution)/shard_map/ppermute | solution.py:14
  106.1 1.9 collective-permute-done.2
  108.0 1.5 convolution_bitcast_fusion.10
  109.6 0.9 convolution_bitcast_fusion.4
  110.5 1.2 scatter_fusion.1
  111.7 11.2 %reduce-scatter.15.cloned.1.call-done = f32[16,256]{1,0:T(8,128)} async-done(((f32[32,256]{1,0:T(8,128)}), f32[16,256]{1,0:T(8,128)}) %reduce-scatter.15.cloned.1.call-update) | async-done | bytes 16400 | tf_op jit(solution)/shard_map/reduce_scatter | solution.py:83
  122.9 0.9 convolution_bitcast_fusion.3
  123.9 1.1 scatter_fusion.2
  125.7 11.8 %reduce-scatter.17.cloned.1.call-done = f32[128,256]{1,0:T(8,128)} async-done(((f32[256,256]{1,0:T(8,128)}), f32[128,256]{1,0:T(8,128)}) %reduce-scatter.17.cloned.1.call-update) | async-done | bytes 131088 | tf_op jit(solution)/shard_map/reduce_scatter | solution.py:78
  137.5 1.3 collective-permute-start.3
  138.8 4.0 %collective-permute-done.3 = f32[128,256]{1,0:T(8,128)S(1)} collective-permute-done((f32[128,256]{1,0:T(8,128)}, f32[128,256]{1,0:T(8,128)S(1)}, u32[]{:S(2)}, u32[]{:S(2)}) %collective-permute-start.3) | collective-permute-done | bytes 131104 | tf_op jit(solution)/shard_map/ppermute | solution.py:14
  142.8 0.9 add.220
  143.7 2.7 %collective-permute-start.4 = (f32[128,256]{1,0:T(8,128)S(1)}, f32[128,256]{1,0:T(8,128)S(1)}, u32[]{:S(2)}, u32[]{:S(2)}) collective-permute-start(f32[128,256]{1,0:T(8,128)S(1)} %add.220), channel_id=1, source_target_pairs={{0,4},{4,0},{2,6},{6,2},{8,12},{12,8},{10,14},{14,10},{16,20},{20,... | collective-permute-start | bytes 393224 | tf_op jit(solution)/shard_map/ppermute | solution.py:14
  146.4 3.0 %collective-permute-done.4 = f32[128,256]{1,0:T(8,128)S(1)} collective-permute-done((f32[128,256]{1,0:T(8,128)S(1)}, f32[128,256]{1,0:T(8,128)S(1)}, u32[]{:S(2)}, u32[]{:S(2)}) %collective-permute-start.4) | collective-permute-done | bytes 131104 | tf_op jit(solution)/shard_map/ppermute | solution.py:14
  149.5 0.9 collective-permute-start.5
  150.4 3.0 %collective-permute-done.5 = f32[128,256]{1,0:T(8,128)S(1)} collective-permute-done((f32[128,256]{1,0:T(8,128)S(1)}, f32[128,256]{1,0:T(8,128)S(1)}, u32[]{:S(2)}, u32[]{:S(2)}) %collective-permute-start.5) | collective-permute-done | bytes 131104 | tf_op jit(solution)/shard_map/ppermute | solution.py:14
  154.2 14.2 %reduce-scatter.19.cloned.1.call-done = f32[16,256]{1,0:T(8,128)} async-done(((f32[32,256]{1,0:T(8,128)}), f32[16,256]{1,0:T(8,128)}) %reduce-scatter.19.cloned.1.call-update) | async-done | bytes 16400 | tf_op jit(solution)/shard_map/reduce_scatter | solution.py:83
  169.2 1.8 all_gather.18
  171.2 1.4 collective-permute-start.6
  173.1 3.0 %collective-permute-done.6 = f32[128,256]{0,1:T(8,128)S(1)} collective-permute-done((f32[128,256]{0,1:T(8,128)S(1)}, f32[128,256]{0,1:T(8,128)S(1)}, u32[]{:S(2)}, u32[]{:S(2)}) %collective-permute-start.6) | collective-permute-done | bytes 131104 | tf_op jit(solution)/shard_map/ppermute | solution.py:14
  176.2 3.1 %collective-permute-start.7 = (f32[128,256]{0,1:T(8,128)S(1)}, f32[128,256]{0,1:T(8,128)S(1)}, u32[]{:S(2)}, u32[]{:S(2)}) collective-permute-start(f32[128,256]{0,1:T(8,128)S(1)} %add.223), channel_id=1, source_target_pairs={{0,4},{4,0},{2,6},{6,2},{8,12},{12,8},{10,14},{14,10},{16,20},{20,... | collective-permute-start | bytes 393224 | tf_op jit(solution)/shard_map/ppermute | solution.py:14
  179.9 1.9 collective-permute-done.7
  181.8 1.4 collective-permute-start.8
  183.8 1.9 collective-permute-done.8
  185.7 4.8 %all_gather.19 = bf16[256,256]{0,1:T(8,128)(2,1)S(1)} all-gather(bf16[128,256]{0,1:T(8,128)(2,1)S(1)} %add_convert_fusion), channel_id=1, replica_groups=mesh['leaf'=64,'front'=2] {'front'}, dimensions={0}, use_global_device_ids=true | all-gather | bytes 196608 | tf_op jit(solution)/shard_map/all_gather | solution.py:114
  192.2 1.8 all_gather.20
  194.3 1.4 collective-permute-start.9
  195.8 1.7 collective-permute-done.9
  197.5 2.9 %collective-permute-start.10 = (f32[64,256]{1,0:T(8,128)S(1)}, f32[64,256]{1,0:T(8,128)}, u32[]{:S(2)}, u32[]{:S(2)}) collective-permute-start(f32[64,256]{1,0:T(8,128)S(1)} %add.226), channel_id=1, source_target_pairs={{0,4},{4,0},{2,6},{6,2},{8,12},{12,8},{10,14},{14,10},{16,20},{20,... | collective-permute-start | bytes 196616 | tf_op jit(solution)/shard_map/ppermute | solution.py:14
  200.5 0.8 gather_fusion.6
  201.4 0.9 collective-permute-done.10
  202.3 0.8 add_convert_fusion.1
  203.2 4.1 %all_gather.21 = bf16[128,256]{1,0:T(8,128)(2,1)S(1)} all-gather(bf16[64,256]{1,0:T(8,128)(2,1)S(1)} %add_convert_fusion.1), channel_id=1, replica_groups=mesh['leaf'=64,'front'=2] {'front'}, dimensions={0}, use_global_device_ids=true | all-gather | bytes 98304 | tf_op jit(solution)/shard_map/all_gather | solution.py:114
  209.1 1.8 all_gather.22
  211.1 1.3 collective-permute-start.11
  212.4 1.4 fusion.15
  213.9 3.0 %all_gather.23 = bf16[64,256]{1,0:T(8,128)(2,1)S(1)} all-gather(bf16[32,256]{1,0:T(8,128)(2,1)S(1)} %add_convert_fusion.2), channel_id=1, replica_groups=mesh['leaf'=64,'front'=2] {'front'}, dimensions={0}, use_global_device_ids=true | all-gather | bytes 49152 | tf_op jit(solution)/shard_map/all_gather | solution.py:114
  217.5 2.6 %convolution_add_fusion.1 = f32[256,1152]{1,0:T(8,128)} fusion(f32[256,1152]{1,0:T(8,128)} %fusion.15, bf16[64,256]{1,0:T(8,128)(2,1)S(1)} %gather_fusion.4, bf16[1,1,3,64,1152]{4,3,2,1,0:T(8,128)(2,1)S(1)} %copy-done.4), kind=kOutput, calls=%fused_computation.15 | convolution fusion | flops 38043648 | bytes 2539520 | tf_op jit(solution)/shard_map/dot_general | solution.py:121
  220.2 3.8 %convolution_bitcast_fusion = f32[1,1,1152,256]{2,3,1,0:T(8,128)} fusion(bf16[1,1,1152,1152]{3,2,1,0:T(8,128)(2,1)S(1)} %copy-done, f32[256,1152]{1,0:T(8,128)} %copy-done.2, f32[256,1152]{1,0:T(8,128)} %convolution_add_fusion.1, bf16[64,256]{1,0:T(8,128)(2,1)S(1)} %gather_fusion.6, bf16[1,1,3,64,1152]{4,3,2,1,0:T(8,128)(2,1)S(1)} %copy-done.4), kind=kOutput, calls=%fused_computation.17 | convolution fusion | flops 718110720 | bytes 6373376 | tf_op jit(solution)/shard_map/dot_general | solution.py:125
  224.0 2.7 %copy.34 = f32[1,1,1152,256]{3,2,1,0:T(8,128)} copy(f32[1,1,1152,256]{2,3,1,0:T(8,128)} %convolution_bitcast_fusion) | data formatting | bytes 2359296
  (88 shorter events, 13.4 us)
Async XLA Ops:
  7.2 43.4 %copy-start = (bf16[1,1,1152,1152]{3,2,1,0:T(8,128)(2,1)S(1)}, bf16[1,1,1152,1152]{3,2,1,0:T(8,128)(2,1)}, u32[]{:S(2)}) copy-start(bf16[1,1,1152,1152]{3,2,1,0:T(8,128)(2,1)} %param.14) | copy-start | bytes 7962628
  12.5 13.3 %copy-start.13 = (s32[1,1,1152]{2,1,0:T(1,128)S(1)}, s32[1,1,1152]{2,1,0:T(1,128)}, u32[]{:S(2)}) copy-start(s32[1,1,1152]{2,1,0:T(1,128)} %param.12) | copy-start | bytes 13828
  13.5 12.2 %copy-start.18 = (s32[1,1,3,64]{3,1,2,0:T(1,128)S(1)}, s32[1,1,3,64]{3,1,2,0:T(1,128)}, u32[]{:S(2)}) copy-start(s32[1,1,3,64]{3,1,2,0:T(1,128)} %param.16) | copy-start | bytes 2308
  13.5 27.0 %all-to-all-start = ((bf16[64,18,256]{2,1,0:T(8,128)(2,1)}), bf16[64,18,256]{2,1,0:T(8,128)(2,1)S(1)}, u32[]{:S(2)}, u32[]{:S(2)}) async-start(bf16[64,18,256]{2,1,0:T(8,128)(2,1)} %reshape.240), calls=%async_computation | async-start | bytes 1572864 | tf_op jit(solution)/shard_map/all_to_all | solution.py:49
  25.6 41.3 %reduce-scatter.9.cloned.1.call-start = ((), (), s32[]{:S(2)}) async-start(), calls=%async_computation.7 | async-start | bytes 98304 | tf_op jit(solution)/shard_map/reduce_scatter | solution.py:78
  26.3 28.0 %copy-start.14 = (s32[64]{0:T(128)}, s32[64]{0:T(128)S(1)}, u32[]{:S(2)}) copy-start(s32[64]{0:T(128)S(1)} %get-tuple-element.18) | copy-start | bytes 772
  50.5 2.2 copy-start.4
  52.7 1.3 copy-start.2
  58.4 0.6 copy-start.5
  59.1 25.1 %reduce-scatter.11.cloned.1.call-start = ((), (), s32[]{:S(2)}) async-start(), calls=%async_computation.8 | async-start | bytes 49152 | tf_op jit(solution)/shard_map/reduce_scatter | solution.py:83
  66.9 3.0 %collective-permute-start = (f32[32,256]{1,0:T(8,128)}, f32[32,256]{1,0:T(8,128)S(1)}, u32[]{:S(2)}, u32[]{:S(2)}) collective-permute-start(f32[32,256]{1,0:T(8,128)} %reduce-scatter.9.cloned.1.call-done), channel_id=1, source_target_pairs={{0,2},{2,0},{4,6},{6,4},{8,10},{10,8},{12,14},{14,12},{16,18},{18,... | collective-permute-start | bytes 98312 | tf_op jit(solution)/shard_map/ppermute | solution.py:14
  71.4 27.1 %reduce-scatter.13.cloned.1.call-start = ((), (), s32[]{:S(2)}) async-start(), calls=%async_computation.9 | async-start | bytes 196608 | tf_op jit(solution)/shard_map/reduce_scatter | solution.py:78
  86.2 0.6 copy-start.3
  86.9 36.1 %reduce-scatter.15.cloned.1.call-start = ((), (), s32[]{:S(2)}) async-start(), calls=%async_computation.10 | async-start | bytes 49152 | tf_op jit(solution)/shard_map/reduce_scatter | solution.py:83
  98.6 3.9 %collective-permute-start.1 = (f32[64,256]{1,0:T(8,128)}, f32[64,256]{1,0:T(8,128)S(1)}, u32[]{:S(2)}, u32[]{:S(2)}) collective-permute-start(f32[64,256]{1,0:T(8,128)} %reduce-scatter.13.cloned.1.call-done), channel_id=1, source_target_pairs={{0,2},{2,0},{4,6},{6,4},{8,10},{10,8},{12,14},{14,12},{16,18},{18,... | collective-permute-start | bytes 196616 | tf_op jit(solution)/shard_map/ppermute | solution.py:14
  103.3 4.7 %collective-permute-start.2 = (f32[64,256]{1,0:T(8,128)S(1)}, f32[64,256]{1,0:T(8,128)S(1)}, u32[]{:S(2)}, u32[]{:S(2)}) collective-permute-start(f32[64,256]{1,0:T(8,128)S(1)} %add.212), channel_id=1, source_target_pairs={{0,4},{4,0},{2,6},{6,2},{8,12},{12,8},{10,14},{14,10},{16,20},{20,... | collective-permute-start | bytes 196616 | tf_op jit(solution)/shard_map/ppermute | solution.py:14
  109.5 13.4 %copy-start.9 = (bf16[1,1,3,64,16]{3,4,2,1,0:T(8,128)(2,1)S(1)}, bf16[1,1,3,64,16]{3,4,2,1,0:T(8,128)(2,1)}, u32[]{:S(2)}) copy-start(bf16[1,1,3,64,16]{3,4,2,1,0:T(8,128)(2,1)} %param.18) | copy-start | bytes 18436
  109.5 28.0 %reduce-scatter.17.cloned.1.call-start = ((), (), s32[]{:S(2)}) async-start(), calls=%async_computation.11 | async-start | bytes 393216 | tf_op jit(solution)/shard_map/reduce_scatter | solution.py:78
  110.5 13.4 %copy-start.12 = (s32[64]{0:T(128)S(1)}, s32[64]{0:T(128)}, u32[]{:S(2)}) copy-start(s32[64]{0:T(128)} %get-tuple-element.13) | copy-start | bytes 772
  123.8 29.5 %copy-start.7 = (bf16[1,1,32,224]{3,2,1,0:T(8,128)(2,1)S(1)}, bf16[1,1,32,224]{3,2,1,0:T(8,128)(2,1)}, u32[]{:S(2)}) copy-start(bf16[1,1,32,224]{3,2,1,0:T(8,128)(2,1)} %param.17) | copy-start | bytes 43012
  124.9 0.7 copy-start.1
  124.9 47.6 %copy-start.11 = (s32[64]{0:T(128)S(1)}, s32[64]{0:T(128)}, u32[]{:S(2)}) copy-start(s32[64]{0:T(128)} %get-tuple-element.14) | copy-start | bytes 772
  124.9 54.3 %copy-start.10 = (s32[64]{0:T(128)S(1)}, s32[64]{0:T(128)}, u32[]{:S(2)}) copy-start(s32[64]{0:T(128)} %get-tuple-element.15) | copy-start | bytes 772
  125.0 54.3 %copy-start.17 = (s32[64]{0:T(128)S(1)}, s32[64]{0:T(128)}, u32[]{:S(2)}) copy-start(s32[64]{0:T(128)} %get-tuple-element.16) | copy-start | bytes 772
  125.0 58.2 %copy-start.16 = (s32[64]{0:T(128)S(1)}, s32[64]{0:T(128)}, u32[]{:S(2)}) copy-start(s32[64]{0:T(128)} %get-tuple-element.17) | copy-start | bytes 772
  125.0 58.2 %copy-start.15 = (s32[64]{0:T(128)S(1)}, s32[64]{0:T(128)}, u32[]{:S(2)}) copy-start(s32[64]{0:T(128)} %copy-done.14) | copy-start | bytes 772
  125.7 42.8 %reduce-scatter.19.cloned.1.call-start = ((), (), s32[]{:S(2)}) async-start(), calls=%async_computation.12 | async-start | bytes 49152 | tf_op jit(solution)/shard_map/reduce_scatter | solution.py:83
  137.5 5.3 %collective-permute-start.3 = (f32[128,256]{1,0:T(8,128)}, f32[128,256]{1,0:T(8,128)S(1)}, u32[]{:S(2)}, u32[]{:S(2)}) collective-permute-start(f32[128,256]{1,0:T(8,128)} %reduce-scatter.17.cloned.1.call-done), channel_id=1, source_target_pairs={{0,2},{2,0},{4,6},{6,4},{8,10},{10,8},{12,14},{14,12},{16,18},{18,... | collective-permute-start | bytes 393224 | tf_op jit(solution)/shard_map/ppermute | solution.py:14
  143.7 5.8 %collective-permute-start.4 = (f32[128,256]{1,0:T(8,128)S(1)}, f32[128,256]{1,0:T(8,128)S(1)}, u32[]{:S(2)}, u32[]{:S(2)}) collective-permute-start(f32[128,256]{1,0:T(8,128)S(1)} %add.220), channel_id=1, source_target_pairs={{0,4},{4,0},{2,6},{6,2},{8,12},{12,8},{10,14},{14,10},{16,20},{20,... | collective-permute-start | bytes 393224 | tf_op jit(solution)/shard_map/ppermute | solution.py:14
  149.5 3.9 %collective-permute-start.5 = (f32[128,256]{1,0:T(8,128)S(1)}, f32[128,256]{1,0:T(8,128)S(1)}, u32[]{:S(2)}, u32[]{:S(2)}) collective-permute-start(f32[128,256]{1,0:T(8,128)S(1)} %add.221), channel_id=1, source_target_pairs={{0,8},{8,0},{2,10},{10,2},{4,12},{12,4},{6,14},{14,6},{16,24},{24,... | collective-permute-start | bytes 393224 | tf_op jit(solution)/shard_map/ppermute | solution.py:14
  171.0 21.1 %copy-start.8 = (f32[16,256]{1,0:T(8,128)S(1)}, f32[16,256]{1,0:T(8,128)}, u32[]{:S(2)}) copy-start(f32[16,256]{1,0:T(8,128)} %reduce-scatter.15.cloned.1.call-done) | copy-start | bytes 49156
  171.2 5.0 %collective-permute-start.6 = (f32[128,256]{0,1:T(8,128)S(1)}, f32[128,256]{0,1:T(8,128)S(1)}, u32[]{:S(2)}, u32[]{:S(2)}) collective-permute-start(f32[128,256]{0,1:T(8,128)S(1)} %convolution_bitcast_fusion.1), channel_id=1, source_target_pairs={{0,2},{2,0},{4,6},{6,4},{8,10},{10,8},{12,14},{14,12},{16,18},{18,... | collective-permute-start | bytes 393224 | tf_op jit(solution)/shard_map/ppermute | solution.py:14
  176.2 5.6 %collective-permute-start.7 = (f32[128,256]{0,1:T(8,128)S(1)}, f32[128,256]{0,1:T(8,128)S(1)}, u32[]{:S(2)}, u32[]{:S(2)}) collective-permute-start(f32[128,256]{0,1:T(8,128)S(1)} %add.223), channel_id=1, source_target_pairs={{0,4},{4,0},{2,6},{6,2},{8,12},{12,8},{10,14},{14,10},{16,20},{20,... | collective-permute-start | bytes 393224 | tf_op jit(solution)/shard_map/ppermute | solution.py:14
  181.8 3.9 %collective-permute-start.8 = (f32[128,256]{0,1:T(8,128)S(1)}, f32[128,256]{0,1:T(8,128)S(1)}, u32[]{:S(2)}, u32[]{:S(2)}) collective-permute-start(f32[128,256]{0,1:T(8,128)S(1)} %add.224), channel_id=1, source_target_pairs={{0,8},{8,0},{2,10},{10,2},{4,12},{12,4},{6,14},{14,6},{16,24},{24,... | collective-permute-start | bytes 393224 | tf_op jit(solution)/shard_map/ppermute | solution.py:14
  190.6 18.3 %copy-start.6 = (f32[16,256]{1,0:T(8,128)S(1)}, f32[16,256]{1,0:T(8,128)}, u32[]{:S(2)}) copy-start(f32[16,256]{1,0:T(8,128)} %reduce-scatter.11.cloned.1.call-done) | copy-start | bytes 49156
  194.3 3.2 %collective-permute-start.9 = (f32[64,256]{1,0:T(8,128)S(1)}, f32[64,256]{1,0:T(8,128)S(1)}, u32[]{:S(2)}, u32[]{:S(2)}) collective-permute-start(f32[64,256]{1,0:T(8,128)S(1)} %convolution_bitcast_fusion.2), channel_id=1, source_target_pairs={{0,2},{2,0},{4,6},{6,4},{8,10},{10,8},{12,14},{14,12},{16,18},{18,... | collective-permute-start | bytes 196616 | tf_op jit(solution)/shard_map/ppermute | solution.py:14
  197.5 4.8 %collective-permute-start.10 = (f32[64,256]{1,0:T(8,128)S(1)}, f32[64,256]{1,0:T(8,128)}, u32[]{:S(2)}, u32[]{:S(2)}) collective-permute-start(f32[64,256]{1,0:T(8,128)S(1)} %add.226), channel_id=1, source_target_pairs={{0,4},{4,0},{2,6},{6,2},{8,12},{12,8},{10,14},{14,10},{16,20},{20,... | collective-permute-start | bytes 196616 | tf_op jit(solution)/shard_map/ppermute | solution.py:14
  211.1 2.8 %collective-permute-start.11 = (f32[32,256]{1,0:T(8,128)S(1)}, f32[32,256]{1,0:T(8,128)S(1)}, u32[]{:S(2)}, u32[]{:S(2)}) collective-permute-start(f32[32,256]{1,0:T(8,128)S(1)} %convolution_bitcast_fusion.12), channel_id=1, source_target_pairs={{0,2},{2,0},{4,6},{6,4},{8,10},{10,8},{12,14},{14,12},{16,18},{18,... | collective-permute-start | bytes 98312 | tf_op jit(solution)/shard_map/ppermute | solution.py:14
Sparse Core Ops, SparseCore 0:
  59.2 7.6 reduce-scatter.8
  71.5 12.5 reduce-scatter.10
  87.0 11.5 reduce-scatter.12
  109.6 13.2 reduce-scatter.14
  125.8 11.6 reduce-scatter.16
  154.3 14.0 reduce-scatter.18
where the time goes:
time: 235 us; the launch traced here: 234 us
  waiting for transfers between devices  108 us (46%)
  starting transfers between devices  34 us (14%)
  local copies, waits for them, and re-layouts  24.9 us (11%)
  matrix products  19.2 us (8%)
  blocking collectives  17.4 us (7%)
  other arithmetic  16 us (7%)
  between operations  14.5 us (6%)
    reduce_scatter x3, waiting for transfers between devices, on_device(): lax.psum_scatter(partial_value, 'front', scatter_dimension=0, tiled=True)  36.8 us
    reduce_scatter x3, waiting for transfers between devices, on_device(): lax.psum_scatter(pending[height], 'front', scatter_dimension=0, tiled=True)  31.2 us
    ppermute x12, waiting for transfers between devices, from_partner(): return lax.ppermute(block, axis, route)  25.7 us
    ppermute x12, starting transfers between devices, from_partner(): return lax.ppermute(block, axis, route)  21.7 us
    all_to_all x1, waiting for transfers between devices, on_device(): lax.all_to_all(outgoing, 'leaf', split_axis=0, concat_axis=0, tiled=True)  14.3 us
    all_to_all x1, starting transfers between devices, on_device(): lax.all_to_all(outgoing, 'leaf', split_axis=0, concat_axis=0, tiled=True)  12.1 us
    all_gather x3, blocking collectives, on_device(): lax.all_gather(x_block.astype(jnp.bfloat16), 'front', axis=0, tiled=True)  11.9 us
    scatter x1, local copies, waits for them, and re-layouts, on_device(): owned_rows = jnp.zeros((leaf_len, rhs_width), jnp.bfloat16).at[recv_place...  8.97 us
  transfers between devices with their start and end apart: 19, of which 19 were waited for; matrix products, arithmetic and copies ran while one was open for 4% of the time, Pallas kernels for 0%

commit v1 on v0

v1 whole, which is shorter than its diff:
```python
import jax
import jax.numpy as jnp
import numpy as np
from jax import lax
from jax.experimental import pallas as pl
from jax.experimental.pallas import tpu as pltpu
from jax.sharding import Mesh, PartitionSpec as P

BF = jnp.bfloat16
F32 = jnp.float32
SUB = 16
TREE = 8
TEAM = 16
VMEM_CAP = 48 * 1024 * 1024

NN = (((1,), (0,)), ((), ()))
NT = (((1,), (1,)), ((), ()))


def dot(a, b, dims=NN):
    return lax.dot_general(a, b, dims, preferred_element_type=F32)


def lane_ids(rows, cols):
    return lax.broadcasted_iota(jnp.int32, (rows, cols), 1)


def row_ids(rows, cols):
    return lax.broadcasted_iota(jnp.int32, (rows, cols), 0)


def hot(mask):
    return jnp.where(mask, 1.0, 0.0).astype(BF)


def call(kernel, name, outs, scratch=(), flops=0, nbytes=0, smem_first=False, nargs=0):
    vmem = pl.BlockSpec(memory_space=pltpu.VMEM)
    specs = [vmem] * nargs
    if smem_first:
        specs[0] = pl.BlockSpec(memory_space=pltpu.SMEM)
    return pl.pallas_call(
        kernel,
        out_shape=outs,
        in_specs=specs,
        out_specs=jax.tree.map(lambda _: vmem, outs),
        scratch_shapes=list(scratch),
        compiler_params=pltpu.CompilerParams(vmem_limit_bytes=VMEM_CAP),
        cost_estimate=pl.CostEstimate(flops=flops, bytes_accessed=nbytes, transcendentals=0),
        name=name,
    )


def send_kernel(keep, pad, order_ref, rhs_ref, out_ref, picked_ref):
    rows, width = rhs_ref.shape
    rhs = rhs_ref[...]
    step = 384
    lanes = lane_ids(128, rows)
    for base in range(0, rows, step):
        blocks = []
        for at in range(base, base + step, 128):
            ids = jnp.broadcast_to(order_ref[:, at : at + 128], (128, 128)).T
            blocks.append(hot(jnp.concatenate([ids] * (rows // 128), axis=1) == lanes))
        picked_ref[base : base + step, :] = dot(jnp.concatenate(blocks, axis=0), rhs)
    tail = picked_ref.shape[0] - rows
    picked_ref[rows:, :] = jnp.zeros((tail, width), F32)
    for owner in range(rows // keep):
        out_ref[owner * pad : (owner + 1) * pad, :] = picked_ref[
            owner * keep : owner * keep + pad, :
        ].astype(BF)


def factor_kernel(
    place_ref, rows_ref, panels_ref, inv_ref, sinv_ref, span_ref, srow_ref,
    push_ref, back_ref, meta_ref, stage_ref,
):
    leaf = inv_ref.shape[0]
    slots = place_ref.shape[1]
    upd = rows_ref.shape[1]
    product = dot(panels_ref[...], inv_ref[...]).astype(BF)
    spread = hot(row_ids(leaf, slots) == place_ref[...])
    placed = dot(product, spread).astype(BF)
    for level, (base, order) in enumerate(((384, 64), (256, 128), (0, 256))):
        mine = hot(row_ids(order, upd) == rows_ref[level : level + 1, :])
        part = slice(level * upd, (level + 1) * upd)
        push_ref[base : base + order, :] = dot(mine, placed[part, :]).astype(BF)
        stage_ref[base : base + order, :] = dot(mine, product[part, :])
    push_ref[448:, :] = jnp.zeros((64, slots), BF)
    stage_ref[448:, :] = jnp.zeros((64, leaf), F32)
    back_ref[...] = stage_ref[...].T.astype(BF)
    cols = sinv_ref.shape[1]
    lane = lane_ids(cols, 256)
    source = jnp.where(
        lane < 128, lane + 96, jnp.where(lane < 192, lane - 96, jnp.where(lane < 224, lane - 192, -1))
    )
    meta_ref[0:32, :] = dot(sinv_ref[...], hot(row_ids(cols, 256) == source)).astype(BF)
    eye = hot(row_ids(SUB, SUB) == lane_ids(SUB, SUB))
    flipped = dot(eye, span_ref[...], NT)
    tail = jnp.concatenate(
        [srow_ref[...].astype(F32), jnp.zeros((SUB - srow_ref.shape[0], upd), F32)], axis=0
    )
    meta_ref[32:48, :] = jnp.concatenate([flipped, tail], axis=1).astype(BF)


def push_kernel(where_ref, recv_ref, push_ref, srhs_ref, meta_ref, out_ref, sum_ref):
    sum_ref[...] = -dot(push_ref[...], recv_ref[...])
    for level in range(3):
        at = pl.ds(pl.multiple_of(where_ref[level], SUB), SUB)
        sum_ref[at, :] = sum_ref[at, :] + srhs_ref[level].astype(F32)
    turned = sum_ref[...].T.astype(BF)
    meta = meta_ref[...]
    for member in range(TEAM):
        part = turned[member * SUB : (member + 1) * SUB, :]
        out_ref[member, 0:16, :] = part[:, 0:256]
        out_ref[member, 16:32, :] = part[:, 256:512]
        out_ref[member, 32:80, :] = meta


def leaf_kernel(place_ref, recv_ref, inv_ref, out_ref):
    leaf = inv_ref.shape[0]
    slots = place_ref.shape[1]
    spread = hot(row_ids(leaf, slots) == place_ref[...])
    owned = dot(spread, recv_ref[...])
    inv = inv_ref[...]
    y_t = dot(owned.T.astype(BF), inv, NT).astype(BF)
    out_ref[...] = dot(y_t, inv).T


def tree_kernel(got_ref, out_ref, e0_ref, e1_ref, e2_ref, a01_ref, a02_ref, a12_ref):
    lane = lane_ids(32, 128)
    none = jnp.zeros((32, 128), BF)
    for peer in range(TREE):
        rows = slice(peer * 32, (peer + 1) * 32)
        low0 = jnp.zeros((32, 128), F32)
        low1 = jnp.zeros((32, 128), F32)
        for front in range(2):
            src = peer * 2 + front
            e2_ref[rows, front * 128 : (front + 1) * 128] = got_ref[src, 32:64, 0:128]
            rest = got_ref[src, 32:64, 128:256].astype(F32)
            one = jnp.where(lane < 64, rest, 0.0)
            zero = jnp.where((lane >= 64) & (lane < 96), rest, 0.0)
            if front:
                one = pltpu.roll(one, 64, 1)
            to = ((peer // 2) % 2) * 64 + front * 32
            shift = (to - 64) % 128
            if shift:
                zero = pltpu.roll(zero, shift, 1)
            low1 = low1 + one
            low0 = low0 + zero
        for ref, low, tile in ((e1_ref, low1, peer // 4), (e0_ref, low0, peer // 4)):
            ref[rows, tile * 128 : (tile + 1) * 128] = low.astype(BF)
            ref[rows, (1 - tile) * 128 : (2 - tile) * 128] = none
    sub = row_ids(256, 64)
    for src in range(TEAM):
        half = src // 8 * 128
        for pair, ref in enumerate((a01_ref, a02_ref, a12_ref)):
            where = got_ref[src, 64 + pair : 65 + pair, 192:256].astype(F32).astype(jnp.int32)
            if pair == 0:
                where = where + half
            flipped = got_ref[src, 64:80, pair * 64 : (pair + 1) * 64]
            ref[src * SUB : (src + 1) * SUB, :] = dot(flipped, hot(sub == where), NT).astype(BF)
    r2 = jnp.zeros((SUB, 256), F32)
    for src in range(TEAM):
        r2 = r2 + got_ref[src, 0:16, :].astype(F32)
    tiles1, tiles0 = [], []
    lane = lane_ids(SUB, 128)
    for tile in range(2):
        total = jnp.zeros((SUB, 128), F32)
        for src in range(tile * 8, tile * 8 + 8):
            total = total + got_ref[src, 16:32, 0:128].astype(F32)
        tiles1.append(total)
        halves = []
        for group in range(2):
            total = jnp.zeros((SUB, 128), F32)
            for src in range(tile * 8 + group * 4, tile * 8 + group * 4 + 4):
                total = total + got_ref[src, 16:32, 128:256].astype(F32)
            halves.append(total)
        tiles0.append(jnp.where(lane < 64, halves[0], pltpu.roll(halves[1], 64, 1)))
    r1 = jnp.concatenate(tiles1, axis=1)
    r0 = jnp.concatenate(tiles0, axis=1)
    e0, e1, e2 = e0_ref[...], e1_ref[...], e2_ref[...]
    a01, a02, a12 = a01_ref[...], a02_ref[...], a12_ref[...]
    y0 = dot(r0.astype(BF), e0, NT)
    y0b = y0.astype(BF)
    y1 = dot((r1 - dot(y0b, a01)).astype(BF), e1, NT)
    y1b = y1.astype(BF)
    y2 = dot((r2 - dot(y0b, a02) - dot(y1b, a12)).astype(BF), e2, NT)
    x2 = dot(y2.astype(BF), e2).astype(BF)
    x1 = dot((y1 - dot(x2, a12, NT)).astype(BF), e1).astype(BF)
    x0 = dot((y0 - dot(x2, a02, NT) - dot(x1, a01, NT)).astype(BF), e0)
    low = jnp.where(lane < 64, 1.0, 0.0)
    for peer in range(TREE):
        tile = slice(peer // 4 * 128, peer // 4 * 128 + 128)
        own = x0[:, tile]
        if (peer // 2) % 2:
            own = pltpu.roll(own, 64, 1)
        own = (own * low).astype(BF)
        for front in range(2):
            dst = peer * 2 + front
            out_ref[dst, 0:16, :] = x2
            out_ref[dst, 16:32, 0:128] = x1[:, tile]
            out_ref[dst, 16:32, 128:256] = own


def finish_kernel(where_ref, got_ref, back_ref, leaf_ref, out_ref, sep_ref):
    high = got_ref[:, 0:16, :].reshape(256, 256)
    low = got_ref[:, 16:32, :].reshape(256, 256)
    out_ref[...] = (
        leaf_ref[...] - dot(back_ref[:, 0:256], high, NT) - dot(back_ref[:, 256:512], low, NT)
    )
    lane = lane_ids(SUB, 256)
    sub = row_ids(SUB, 256)
    for level, (base, table) in enumerate(((256, low), (256, low), (0, high))):
        pick = hot(lane == sub + (where_ref[level] - base))
        sep_ref[level] = dot(pick, table, NT).astype(BF)


def on_device(
    rhs_parts,
    send_order,
    recv_place,
    sep_rhs,
    leaf_inv,
    leaf_panels,
    leaf_rows,
    sep_inv,
    sep_panels,
    sep_rows,
):
    owners = lax.axis_size("tree") * lax.axis_size("peer")
    rhs = rhs_parts[0, 0]
    leaf, width = rhs.shape
    inv = leaf_inv[0, 0]
    panels = leaf_panels[0, 0].reshape(-1, leaf)
    keep = leaf // owners
    pad = -(-keep // 8) * 8
    slots = owners * pad
    sds = jax.ShapeDtypeStruct

    sent = call(
        lambda *refs: send_kernel(keep, pad, *refs),
        "send_rows",
        sds((slots, width), BF),
        [pltpu.VMEM((-(-(leaf - keep + pad) // 8) * 8 + 8, width), F32)],
        flops=2 * leaf * leaf * width,
        nbytes=2 * leaf * width * 2,
        nargs=2,
    )(send_order[0], rhs)
    recv = lax.all_to_all(
        sent.reshape(owners, pad, width), ("tree", "peer"), split_axis=0, concat_axis=0, tiled=True
    ).reshape(slots, width)

    place = jnp.pad(
        recv_place[0, 0].reshape(owners, keep), ((0, 0), (0, pad - keep)), constant_values=-1
    ).reshape(1, slots)
    push, back, meta = call(
        factor_kernel,
        "factor_products",
        (sds((512, slots), BF), sds((leaf, 512), BF), sds((48, 256), BF)),
        [pltpu.VMEM((512, leaf), F32)],
        flops=2 * 192 * leaf * (leaf + slots) + 2 * 448 * 64 * (leaf + slots),
        nbytes=2 * leaf * leaf + 4 * 512 * slots,
        nargs=7,
    )(
        place,
        leaf_rows[0, 0],
        panels,
        inv,
        sep_inv[0, 0],
        sep_panels[0, 0].reshape(-1, SUB),
        sep_rows[0, 0],
    )

    peer = lax.axis_index("peer")
    front = lax.axis_index("front")
    where = jnp.stack(
        [
            384 + (peer % 2 * 2 + front) * SUB,
            256 + (peer % 4 * 2 + front) * SUB,
            (peer * 2 + front) * SUB,
        ]
    ).astype(jnp.int32)
    team = ("peer", "front")
    chunks = call(
        push_kernel,
        "push_updates",
        sds((TEAM, 80, 256), BF),
        [pltpu.VMEM((512, width), F32)],
        flops=2 * 512 * slots * width,
        nbytes=2 * slots * (512 + width) + TEAM * 80 * 512,
        smem_first=True,
        nargs=5,
    )(where, recv, push, sep_rhs[0, 0], meta)
    got = lax.all_to_all(chunks, team, split_axis=0, concat_axis=0, tiled=True)

    bare = call(
        leaf_kernel,
        "leaf_solve",
        sds((leaf, width), F32),
        flops=2 * leaf * width * (2 * leaf + slots),
        nbytes=2 * leaf * leaf + 6 * slots * width,
        nargs=3,
    )(place, recv, inv)

    square = pltpu.VMEM((256, 256), BF)
    solved = call(
        tree_kernel,
        "separator_tree",
        sds((TEAM, 32, 256), BF),
        [square] * 6,
        flops=2 * 16 * 256 * 256 * 12 + 2 * 48 * 16 * 64 * 256,
        nbytes=TEAM * 112 * 512,
        nargs=1,
    )(got)
    back_got = lax.all_to_all(solved, team, split_axis=0, concat_axis=0, tiled=True)

    leaf_solution, sep_solution = call(
        finish_kernel,
        "finish",
        (sds((leaf, width), F32), sds((3, SUB, width), BF)),
        flops=2 * leaf * 512 * width,
        nbytes=leaf * width * 8 + leaf * 1024 + TEAM * 32 * 512,
        smem_first=True,
        nargs=4,
    )(where, back_got, back, bare)
    return leaf_solution[None, None], sep_solution[None, None]


def solution(mesh):
    leaves, fronts = mesh.shape["leaf"], mesh.shape["front"]
    grid = Mesh(
        np.asarray(mesh.devices).reshape(leaves // TREE, TREE, fronts), ("tree", "peer", "front")
    )
    leaf = ("tree", "peer")
    in_specs = (
        P(leaf, "front", None, None),
        P(leaf, "front", None),
        P(leaf, "front", None),
        P(leaf, "front", None, None, None),
        P(leaf, "front", None, None),
        P(leaf, "front", None, None, None),
        P(leaf, "front", None, None),
        P(leaf, "front", None, None),
        P(leaf, "front", None, None, None),
        P(leaf, "front", None, None),
    )
    out_specs = (P(leaf, "front", None, None), P(leaf, "front", None, None, None))
    return jax.shard_map(
        on_device, mesh=grid, in_specs=in_specs, out_specs=out_specs, check_vma=False
    )
```

time: 235 us -> 67.2 us (0.29)
  waiting for transfers between devices: 108 us -> 7.34 us
  matrix products: 19.2 us -> 0 us
  starting transfers between devices: 34 us -> 15.9 us
  other arithmetic: 16 us -> 0.1 us
  Pallas kernels: 0 us -> 15.3 us
  local copies, waits for them, and re-layouts: 24.9 us -> 10.8 us
  between operations: 14.5 us -> 0.76 us
    reduce_scatter x6 -> x0, waiting for transfers between devices: 68 us -> none  [the longest x3 36.8 us: on_device(): lax.psum_scatter(partial_value, 'front', scatter_dimension=0, tiled=True)]
    ppermute x12 -> x0, waiting for transfers between devices: 25.7 us -> none  [from_partner(): return lax.ppermute(block, axis, route)]
    ppermute x12 -> x0, starting transfers between devices: 21.7 us -> none  [from_partner(): return lax.ppermute(block, axis, route)]
    dot_general x19 -> x0, matrix products: 19.2 us -> none  [the longest x2 4.03 us: on_device(): jnp.dot(leaf_panels[0, 0, height].T, picked, preferred_element_type=jnp.f...]
    all_gather x6 -> x0, blocking collectives: 17.4 us -> none  [the longest x3 11.9 us: on_device(): lax.all_gather(x_block.astype(jnp.bfloat16), 'front', axis=0, tiled=True)]
    all_to_all x0 -> x1, blocking collectives: none -> 16.3 us  [on_device(): got = lax.all_to_all(chunks, team, split_axis=0, concat_axis=0, tiled=True)]
    pallas_call x0 -> x6, Pallas kernels: none -> 15.3 us  [the longest x1 4.56 us: on_device(): call(leaf_kernel, 'leaf_solve', sds((leaf, width), F32), flops=2 * leaf *...]
    gather x7 -> x0, local copies, waits for them, and re-layouts: 8.99 us -> none  [the longest x1 4.41 us: on_device(): rhs_rows[send_order[0, 0]].reshape(leaves, leaf_len // leaves, rhs_width)]
  transfers between devices with their start and end apart: 19 -> 2, of which waited for: 19 -> 2; matrix products, arithmetic and copies ran while one was open for 4% -> 2% of each run, Pallas kernels for 0% -> 11%
where the time goes in v1:
time: 67.2 us; the launch traced here: 66.5 us
  blocking collectives  16.3 us (24%)
  starting transfers between devices  15.9 us (24%)
  Pallas kernels  15.3 us (23%)
  local copies, waits for them, and re-layouts  10.8 us (16%)
  waiting for transfers between devices  7.34 us (11%)
  between operations  0.76 us (1%)
    all_to_all x1, blocking collectives, on_device(): got = lax.all_to_all(chunks, team, split_axis=0, concat_axis=0, tiled=True)  16.3 us
    all_to_all x1, starting transfers between devices, on_device(): lax.all_to_all(sent.reshape(owners, pad, width), ('tree', 'peer'), split_...  12.1 us
    unnamed x30, local copies, waits for them, and re-layouts  10.6 us
    all_to_all x1, waiting for transfers between devices, on_device(): lax.all_to_all(sent.reshape(owners, pad, width), ('tree', 'peer'), split_...  6.4 us
    pallas_call x1, Pallas kernels, on_device(): call(leaf_kernel, 'leaf_solve', sds((leaf, width), F32), flops=2 * leaf *...  4.56 us
    all_to_all x1, starting transfers between devices, on_device(): lax.all_to_all(solved, team, split_axis=0, concat_axis=0, tiled=True)  3.77 us
    pallas_call x1, Pallas kernels, on_device(): call(tree_kernel, 'separator_tree', sds((TEAM, 32, 256), BF), [square] *...  2.91 us
    pallas_call x1, Pallas kernels, on_device(): call(factor_kernel, 'factor_products', (sds((512, slots), BF), sds((leaf,...  2.51 us
  transfers between devices with their start and end apart: 2, of which 2 were waited for; matrix products, arithmetic and copies ran while one was open for 2% of the time, Pallas kernels for 11%

profile of v1, /device:TPU:1, one launch (start us, length us, event | category | flops | bytes accessed | tf_op | source)
XLA Modules:
  0.0 66.5 jit_solution(17567112442642561648)
XLA Ops:
  0.6 0.0 copy-start.6
  0.6 1.1 %copy-done.6 = bf16[1,1,1152,256]{3,2,1,0:T(8,128)(2,1)S(1)} copy-done((bf16[1,1,1152,256]{3,2,1,0:T(8,128)(2,1)S(1)}, bf16[1,1,1152,256]{3,2,1,0:T(8,128)(2,1)}, u32[]{:S(2)}) %copy-start.6) | copy-done | bytes 589848
  1.7 0.0 copy-start.9
  1.7 0.7 %copy-done.9 = s32[1,1,1152]{2,1,0:T(1,128)S(1)} copy-done((s32[1,1,1152]{2,1,0:T(1,128)S(1)}, s32[1,1,1152]{2,1,0:T(1,128)}, u32[]{:S(2)}) %copy-start.9) | copy-done | bytes 4632
  2.4 2.0 %send_rows.1 = bf16[1536,256]{1,0:T(8,128)(2,1)} custom-call(s32[1,1152]{1,0:T(1,128)S(1)} %bitcast.27, bf16[1152,256]{1,0:T(8,128)(2,1)S(1)} %bitcast.24), custom_call_target="tpu_custom_call" | custom-call | flops 679477248 | bytes 1179648 | tf_op jit(solution)/shard_map/send_rows/pallas_call | solution.py:239
  4.3 0.0 copy-start.11
  4.3 0.0 copy-start.10
  4.3 0.0 copy-start.12
  4.3 0.0 copy-start.13
  4.3 12.1 %all-to-all-start = ((bf16[64,24,256]{2,1,0:T(8,128)(2,1)}), bf16[64,24,256]{2,1,0:T(8,128)(2,1)S(1)}, u32[]{:S(2)}, u32[]{:S(2)}) async-start(bf16[64,24,256]{2,1,0:T(8,128)(2,1)} %bitcast.5), calls=%async_computation | async-start | bytes 1572864 | tf_op jit(solution)/shard_map/all_to_all | solution.py:248
  16.5 0.0 copy-done.11
  16.5 0.1 reshape_squeeze.9
  16.7 0.1 reshape.15.place_ref
  16.8 0.0 copy-done.10
  16.8 0.7 %copy.13 = bf16[1,1,3,64,16]{4,3,2,1,0:T(8,128)(2,1)} copy(bf16[1,1,3,64,16]{3,4,2,1,0:T(8,128)(2,1)S(1)} %copy-done.10) | data formatting | bytes 12288 | tf_op args[8]
  17.5 0.1 pad_add_fusion.where_ref
  17.6 0.0 copy-done.12
  17.6 0.0 copy-done.13
  17.6 0.0 copy-start
  17.6 0.8 %copy-done = bf16[1,1,3,64,16]{4,3,2,1,0:T(8,128)(2,1)S(1)} copy-done((bf16[1,1,3,64,16]{4,3,2,1,0:T(8,128)(2,1)S(1)}, bf16[1,1,3,64,16]{4,3,2,1,0:T(8,128)(2,1)}, u32[]{:S(2)}) %copy-start) | copy-done | bytes 6168
  18.4 0.0 copy-start.4
  18.4 1.7 %copy-done.4 = bf16[1,1,1152,1152]{3,2,1,0:T(8,128)(2,1)S(1)} copy-done((bf16[1,1,1152,1152]{3,2,1,0:T(8,128)(2,1)S(1)}, bf16[1,1,1152,1152]{3,2,1,0:T(8,128)(2,1)}, u32[]{:S(2)}) %copy-start.4) | copy-done | bytes 2654232
  20.1 0.0 copy-start.7
  20.1 1.0 %copy-done.7 = bf16[1,1,3,64,1152]{4,3,2,1,0:T(8,128)(2,1)S(1)} copy-done((bf16[1,1,3,64,1152]{4,3,2,1,0:T(8,128)(2,1)S(1)}, bf16[1,1,3,64,1152]{4,3,2,1,0:T(8,128)(2,1)}, u32[]{:S(2)}) %copy-start.7) | copy-done | bytes 442392
  21.1 0.0 copy-start.8
  21.1 0.7 %copy-done.8 = bf16[1,1,32,224]{3,2,1,0:T(8,128)(2,1)S(1)} copy-done((bf16[1,1,32,224]{3,2,1,0:T(8,128)(2,1)S(1)}, bf16[1,1,32,224]{3,2,1,0:T(8,128)(2,1)}, u32[]{:S(2)}) %copy-start.8) | copy-done | bytes 14360
  21.9 2.5 %factor_products.1 = (bf16[512,1536]{1,0:T(8,128)(2,1)S(1)}, bf16[1152,512]{1,0:T(8,128)(2,1)S(1)}, bf16[48,256]{1,0:T(8,128)(2,1)S(1)}) custom-call(s32[1,1536]{1,0:T(1,128)S(1)} %reshape.15.place_ref, s32[3,64]{1,0:T(4,128)S(1)} %get-tuple-element.13.rows_ref, bf16[192,1152]{1,0:T(8,128)(2,1)S(1)} %bitcast.25, bf16[1152,1152]{1,0:T(8,128)(2,1)S(1)} %bitcast.22, ...), custom_call_target="tpu_custom_call" | custom-call | flops 1343225856 | bytes 5799936 | tf_op jit(solution)/shard_map/factor_products/pallas_call | solution.py:255
  24.4 0.0 copy-start.2
  24.4 0.6 copy-done.2
  25.0 6.4 %all-to-all-done = bf16[64,24,256]{2,1,0:T(8,128)(2,1)S(1)} async-done(((bf16[64,24,256]{2,1,0:T(8,128)(2,1)}), bf16[64,24,256]{2,1,0:T(8,128)(2,1)S(1)}, u32[]{:S(2)}, u32[]{:S(2)}) %all-to-all-start) | async-done | bytes 786464 | tf_op jit(solution)/shard_map/all_to_all | solution.py:248
  31.4 0.0 copy-start.1
  31.4 0.7 %copy-done.1 = bf16[1,1,3,16,256]{4,3,2,1,0:T(8,128)(2,1)S(1)} copy-done((bf16[1,1,3,16,256]{4,3,2,1,0:T(8,128)(2,1)S(1)}, bf16[1,1,3,16,256]{4,3,2,1,0:T(8,128)(2,1)}, u32[]{:S(2)}) %copy-start.1) | copy-done | bytes 24600
  32.1 0.0 copy-start.3
  32.1 0.7 %copy-done.3 = bf16[48,256]{1,0:T(8,128)(2,1)S(1)} copy-done((bf16[48,256]{1,0:T(8,128)(2,1)S(1)}, bf16[48,256]{1,0:T(8,128)(2,1)}, u32[]{:S(2)}) %copy-start.3) | copy-done | bytes 24600
  32.9 1.3 %push_updates.1 = bf16[16,80,256]{2,1,0:T(8,128)(2,1)S(1)} custom-call(s32[3]{0:T(128)S(1)} %pad_add_fusion.where_ref, bf16[1536,256]{1,0:T(8,128)(2,1)S(1)} %bitcast.18, bf16[512,1536]{1,0:T(8,128)(2,1)S(1)} %get-tuple-element.7.push_ref, bf16[3,16,256]{2,1,0:T(8,128)(2,1)S(1)} %bitcast.21, bf16[48,256]{1,0:T(8,128)(2,1)S(1)} %copy-done.3), custom_call_target="tpu_custom_call" | custom-call | flops 402653184 | bytes 3014656 | tf_op jit(solution)/shard_map/push_updates/pallas_call | solution.py:283
  34.1 16.3 %all_to_all.15.got_ref = bf16[16,80,256]{2,1,0:T(8,128)(2,1)S(1)} all-to-all(bf16[16,80,256]{2,1,0:T(8,128)(2,1)S(1)} %push_updates.1), channel_id=1, replica_groups=mesh['tree'=8,'peer'=8,'front'=2] {'peer','front'}, dimensions={0} | all-to-all | bytes 1310720 | tf_op jit(solution)/shard_map/all_to_all | solution.py:293
  50.5 2.9 %separator_tree.1 = bf16[16,32,256]{2,1,0:T(8,128)(2,1)} custom-call(bf16[16,80,256]{2,1,0:T(8,128)(2,1)S(1)} %all_to_all.15.got_ref), custom_call_target="tpu_custom_call" | custom-call | flops 50331648 | bytes 917504 | tf_op jit(solution)/shard_map/separator_tree/pallas_call | solution.py:305
  53.4 3.8 %all-to-all-start.2 = ((bf16[16,32,256]{2,1,0:T(8,128)(2,1)}), bf16[16,32,256]{2,1,0:T(8,128)(2,1)S(1)}, u32[]{:S(2)}, u32[]{:S(2)}) async-start(bf16[16,32,256]{2,1,0:T(8,128)(2,1)} %separator_tree.1), calls=%async_computation.2 | async-start | bytes 524288 | tf_op jit(solution)/shard_map/all_to_all | solution.py:314
  57.1 0.0 copy-start.5
  57.2 1.7 %copy-done.5 = bf16[1,1,1152,1152]{3,2,1,0:T(8,128)(2,1)S(1)} copy-done((bf16[1,1,1152,1152]{3,2,1,0:T(8,128)(2,1)S(1)}, bf16[1,1,1152,1152]{3,2,1,0:T(8,128)(2,1)}, u32[]{:S(2)}) %copy-start.5) | copy-done | bytes 2654232
  58.9 4.6 %leaf_solve.1.leaf_ref = f32[1152,256]{1,0:T(8,128)S(1)} custom-call(s32[1,1536]{1,0:T(1,128)S(1)} %reshape.15.place_ref, bf16[1536,256]{1,0:T(8,128)(2,1)S(1)} %bitcast.19, bf16[1152,1152]{1,0:T(8,128)(2,1)S(1)} %bitcast.23), custom_call_target="tpu_custom_call" | custom-call | flops 2264924160 | bytes 5013504 | tf_op jit(solution)/shard_map/leaf_solve/pallas_call | solution.py:295
  63.5 0.9 %all-to-all-done.2.got_ref = bf16[16,32,256]{2,1,0:T(8,128)(2,1)S(1)} async-done(((bf16[16,32,256]{2,1,0:T(8,128)(2,1)}), bf16[16,32,256]{2,1,0:T(8,128)(2,1)S(1)}, u32[]{:S(2)}, u32[]{:S(2)}) %all-to-all-start.2) | async-done | bytes 262176 | tf_op jit(solution)/shard_map/all_to_all | solution.py:314
  64.4 2.1 %finish.1 = (f32[1152,256]{1,0:T(8,128)}, bf16[3,16,256]{2,1,0:T(8,128)(2,1)}) custom-call(s32[3]{0:T(128)S(1)} %pad_add_fusion.where_ref, bf16[16,32,256]{2,1,0:T(8,128)(2,1)S(1)} %all-to-all-done.2.got_ref, bf16[1152,512]{1,0:T(8,128)(2,1)S(1)} %get-tuple-element.9.back_ref, f32[1152,256]{1,0:T(8,128)S(1)} %leaf_solve.1.leaf_ref), custom_call_target="tpu_custom_call" | custom-call | flops 301989888 | bytes 3801088 | tf_op jit(solution)/shard_map/finish/pallas_call | solution.py:316
  (3 shorter events, 0.0 us)
Async XLA Ops:
  0.6 1.1 %copy-start.6 = (bf16[1,1,1152,256]{3,2,1,0:T(8,128)(2,1)S(1)}, bf16[1,1,1152,256]{3,2,1,0:T(8,128)(2,1)}, u32[]{:S(2)}) copy-start(bf16[1,1,1152,256]{3,2,1,0:T(8,128)(2,1)} %param.10) | copy-start | bytes 1769476
  1.7 0.7 %copy-start.9 = (s32[1,1,1152]{2,1,0:T(1,128)S(1)}, s32[1,1,1152]{2,1,0:T(1,128)}, u32[]{:S(2)}) copy-start(s32[1,1,1152]{2,1,0:T(1,128)} %param.11) | copy-start | bytes 13828
  4.3 12.2 %copy-start.11 = (s32[1,1,1152]{2,1,0:T(1,128)S(1)}, s32[1,1,1152]{2,1,0:T(1,128)}, u32[]{:S(2)}) copy-start(s32[1,1,1152]{2,1,0:T(1,128)} %param.12) | copy-start | bytes 13828
  4.3 12.4 %copy-start.10 = (bf16[1,1,3,64,16]{3,4,2,1,0:T(8,128)(2,1)S(1)}, bf16[1,1,3,64,16]{3,4,2,1,0:T(8,128)(2,1)}, u32[]{:S(2)}) copy-start(bf16[1,1,3,64,16]{3,4,2,1,0:T(8,128)(2,1)} %param.18) | copy-start | bytes 18436
  4.3 13.2 %copy-start.12 = (s32[1,1,3,64]{3,1,2,0:T(1,128)S(1)}, s32[1,1,3,64]{3,1,2,0:T(1,128)}, u32[]{:S(2)}) copy-start(s32[1,1,3,64]{3,1,2,0:T(1,128)} %param.19) | copy-start | bytes 2308
  4.3 13.2 %copy-start.13 = (s32[1,1,3,64]{3,1,2,0:T(1,128)S(1)}, s32[1,1,3,64]{3,1,2,0:T(1,128)}, u32[]{:S(2)}) copy-start(s32[1,1,3,64]{3,1,2,0:T(1,128)} %param.16) | copy-start | bytes 2308
  4.3 27.0 %all-to-all-start = ((bf16[64,24,256]{2,1,0:T(8,128)(2,1)}), bf16[64,24,256]{2,1,0:T(8,128)(2,1)S(1)}, u32[]{:S(2)}, u32[]{:S(2)}) async-start(bf16[64,24,256]{2,1,0:T(8,128)(2,1)} %bitcast.5), calls=%async_computation | async-start | bytes 1572864 | tf_op jit(solution)/shard_map/all_to_all | solution.py:248
  17.6 0.8 %copy-start = (bf16[1,1,3,64,16]{4,3,2,1,0:T(8,128)(2,1)S(1)}, bf16[1,1,3,64,16]{4,3,2,1,0:T(8,128)(2,1)}, u32[]{:S(2)}) copy-start(bf16[1,1,3,64,16]{4,3,2,1,0:T(8,128)(2,1)} %copy.13) | copy-start | bytes 18436
  18.4 1.7 %copy-start.4 = (bf16[1,1,1152,1152]{3,2,1,0:T(8,128)(2,1)S(1)}, bf16[1,1,1152,1152]{3,2,1,0:T(8,128)(2,1)}, u32[]{:S(2)}) copy-start(bf16[1,1,1152,1152]{3,2,1,0:T(8,128)(2,1)} %param.14) | copy-start | bytes 7962628
  20.1 1.0 %copy-start.7 = (bf16[1,1,3,64,1152]{4,3,2,1,0:T(8,128)(2,1)S(1)}, bf16[1,1,3,64,1152]{4,3,2,1,0:T(8,128)(2,1)}, u32[]{:S(2)}) copy-start(bf16[1,1,3,64,1152]{4,3,2,1,0:T(8,128)(2,1)} %param.15) | copy-start | bytes 1327108
  21.1 0.7 %copy-start.8 = (bf16[1,1,32,224]{3,2,1,0:T(8,128)(2,1)S(1)}, bf16[1,1,32,224]{3,2,1,0:T(8,128)(2,1)}, u32[]{:S(2)}) copy-start(bf16[1,1,32,224]{3,2,1,0:T(8,128)(2,1)} %param.17) | copy-start | bytes 43012
  24.4 0.6 copy-start.2
  31.4 0.7 %copy-start.1 = (bf16[1,1,3,16,256]{4,3,2,1,0:T(8,128)(2,1)S(1)}, bf16[1,1,3,16,256]{4,3,2,1,0:T(8,128)(2,1)}, u32[]{:S(2)}) copy-start(bf16[1,1,3,16,256]{4,3,2,1,0:T(8,128)(2,1)} %param.13) | copy-start | bytes 73732
  32.1 0.7 %copy-start.3 = (bf16[48,256]{1,0:T(8,128)(2,1)S(1)}, bf16[48,256]{1,0:T(8,128)(2,1)}, u32[]{:S(2)}) copy-start(bf16[48,256]{1,0:T(8,128)(2,1)} %copy-done.2) | copy-start | bytes 73732
  53.4 11.0 %all-to-all-start.2 = ((bf16[16,32,256]{2,1,0:T(8,128)(2,1)}), bf16[16,32,256]{2,1,0:T(8,128)(2,1)S(1)}, u32[]{:S(2)}, u32[]{:S(2)}) async-start(bf16[16,32,256]{2,1,0:T(8,128)(2,1)} %separator_tree.1), calls=%async_computation.2 | async-start | bytes 524288 | tf_op jit(solution)/shard_map/all_to_all | solution.py:314
  57.1 1.7 %copy-start.5 = (bf16[1,1,1152,1152]{3,2,1,0:T(8,128)(2,1)S(1)}, bf16[1,1,1152,1152]{3,2,1,0:T(8,128)(2,1)}, u32[]{:S(2)}) copy-start(bf16[1,1,1152,1152]{3,2,1,0:T(8,128)(2,1)} %param.14) | copy-start | bytes 7962628

commit v2 on v1

--- a/solution.py
+++ b/solution.py
@@ -11,7 +11,8 @@
 SUB = 16
 TREE = 8
 TEAM = 16
-VMEM_CAP = 48 * 1024 * 1024
+VMEM_CAP = 40 * 1024 * 1024
+VMEM_ALL = 62 * 1024 * 1024
 
 NN = (((1,), (0,)), ((), ()))
 NT = (((1,), (1,)), ((), ()))
@@ -33,81 +34,113 @@
     return jnp.where(mask, 1.0, 0.0).astype(BF)
 
 
-def call(kernel, name, outs, scratch=(), flops=0, nbytes=0, smem_first=False, nargs=0):
-    vmem = pl.BlockSpec(memory_space=pltpu.VMEM)
-    specs = [vmem] * nargs
-    if smem_first:
-        specs[0] = pl.BlockSpec(memory_space=pltpu.SMEM)
+VM = pl.BlockSpec(memory_space=pltpu.VMEM)
+SM = pl.BlockSpec(memory_space=pltpu.SMEM)
+HB = pl.BlockSpec(memory_space=pltpu.HBM)
+DMA = pltpu.SemaphoreType.DMA
+
+
+def call(kernel, name, ins, outs, scratch=(), flops=0, nbytes=0, vmem=VMEM_CAP):
     return pl.pallas_call(
         kernel,
-        out_shape=outs,
-        in_specs=specs,
-        out_specs=jax.tree.map(lambda _: vmem, outs),
+        out_shape=[shape for shape, _ in outs],
+        in_specs=list(ins),
+        out_specs=[spec for _, spec in outs],
         scratch_shapes=list(scratch),
-        compiler_params=pltpu.CompilerParams(vmem_limit_bytes=VMEM_CAP),
+        compiler_params=pltpu.CompilerParams(vmem_limit_bytes=vmem),
         cost_estimate=pl.CostEstimate(flops=flops, bytes_accessed=nbytes, transcendentals=0),
         name=name,
     )
 
 
-def send_kernel(keep, pad, order_ref, rhs_ref, out_ref, picked_ref):
+def fetch(source, target, sem):
+    copy = pltpu.make_async_copy(source, target, sem)
+    copy.start()
+    return copy
+
+
+def send_kernel(keep, pad, order_hbm, rhs_hbm, out_hbm, order_ref, rhs_ref, picked_ref, out_ref, sems):
     rows, width = rhs_ref.shape
-    rhs = rhs_ref[...]
+    order_in = fetch(order_hbm, order_ref, sems.at[0])
+    rhs_in = fetch(rhs_hbm, rhs_ref, sems.at[1])
+    tail = picked_ref.shape[0] - rows
+    picked_ref[rows:, :] = jnp.zeros((tail, width), F32)
+    owners = rows // keep
     step = 384
     lanes = lane_ids(128, rows)
-    for base in range(0, rows, step):
-        blocks = []
-        for at in range(base, base + step, 128):
-            ids = jnp.broadcast_to(order_ref[:, at : at + 128], (128, 128)).T
-            blocks.append(hot(jnp.concatenate([ids] * (rows // 128), axis=1) == lanes))
-        picked_ref[base : base + step, :] = dot(jnp.concatenate(blocks, axis=0), rhs)
-    tail = picked_ref.shape[0] - rows
-    picked_ref[rows:, :] = jnp.zeros((tail, width), F32)
-    for owner in range(rows // keep):
-        out_ref[owner * pad : (owner + 1) * pad, :] = picked_ref[
-            owner * keep : owner * keep + pad, :
-        ].astype(BF)
+    order_in.wait()
+    hots = []
+    for at in range(0, rows, 128):
+        ids = jnp.broadcast_to(order_ref[:, at : at + 128], (128, 128)).T
+        hots.append(hot(jnp.concatenate([ids] * (rows // 128), axis=1) == lanes))
+    rhs_in.wait()
+    rhs = rhs_ref[...]
+    done = 0
+    leaving = []
+    for part in range(rows // step):
+        block = jnp.concatenate(hots[part * 3 : part * 3 + 3], axis=0)
+        picked_ref[part * step : (part + 1) * step, :] = dot(block, rhs)
+        have = (part + 1) * step
+        upto = owners if have == rows else ((have - pad) // keep + 1) // 2 * 2
+        for owner in range(done, upto):
+            out_ref[owner * pad : (owner + 1) * pad, :] = picked_ref[
+                owner * keep : owner * keep + pad, :
+            ].astype(BF)
+        span = slice(done * pad, upto * pad)
+        leaving.append(fetch(out_ref.at[span, :], out_hbm.at[span, :], sems.at[2 + part]))
+        done = upto
+    for copy in leaving:
+        copy.wait()
 
 
 def factor_kernel(
-    place_ref, rows_ref, panels_ref, inv_ref, sinv_ref, span_ref, srow_ref,
-    push_ref, back_ref, meta_ref, stage_ref,
+    where_ref, place_ref, rows_ref, srow_ref, panels_hbm, inv_hbm, sinv_hbm, span_hbm, srhs_hbm,
+    push_ref, back_ref, side_ref, stage_ref, panels_ref, inv_ref, sinv_ref, span_ref, srhs_ref, sems,
 ):
+    moves = [
+        fetch(panels_hbm, panels_ref, sems.at[0]),
+        fetch(inv_hbm, inv_ref, sems.at[1]),
+        fetch(sinv_hbm, sinv_ref, sems.at[2]),
+        fetch(span_hbm, span_ref, sems.at[3]),
+        fetch(srhs_hbm, srhs_ref, sems.at[4]),
+    ]
     leaf = inv_ref.shape[0]
     slots = place_ref.shape[1]
     upd = rows_ref.shape[1]
+    spread = hot(row_ids(leaf, slots) == place_ref[...])
+    push_ref[448:, :] = jnp.zeros((64, slots), BF)
+    stage_ref[448:, :] = jnp.zeros((64, leaf), F32)
+    for move in moves:
+        move.wait()
     product = dot(panels_ref[...], inv_ref[...]).astype(BF)
-    spread = hot(row_ids(leaf, slots) == place_ref[...])
     placed = dot(product, spread).astype(BF)
     for level, (base, order) in enumerate(((384, 64), (256, 128), (0, 256))):
         mine = hot(row_ids(order, upd) == rows_ref[level : level + 1, :])
         part = slice(level * upd, (level + 1) * upd)
         push_ref[base : base + order, :] = dot(mine, placed[part, :]).astype(BF)
         stage_ref[base : base + order, :] = dot(mine, product[part, :])
-    push_ref[448:, :] = jnp.zeros((64, slots), BF)
-    stage_ref[448:, :] = jnp.zeros((64, leaf), F32)
     back_ref[...] = stage_ref[...].T.astype(BF)
     cols = sinv_ref.shape[1]
     lane = lane_ids(cols, 256)
     source = jnp.where(
         lane < 128, lane + 96, jnp.where(lane < 192, lane - 96, jnp.where(lane < 224, lane - 192, -1))
     )
-    meta_ref[0:32, :] = dot(sinv_ref[...], hot(row_ids(cols, 256) == source)).astype(BF)
-    eye = hot(row_ids(SUB, SUB) == lane_ids(SUB, SUB))
-    flipped = dot(eye, span_ref[...], NT)
+    side_ref[0:32, :] = dot(sinv_ref[...], hot(row_ids(cols, 256) == source)).astype(BF)
     tail = jnp.concatenate(
         [srow_ref[...].astype(F32), jnp.zeros((SUB - srow_ref.shape[0], upd), F32)], axis=0
     )
-    meta_ref[32:48, :] = jnp.concatenate([flipped, tail], axis=1).astype(BF)
-
-
-def push_kernel(where_ref, recv_ref, push_ref, srhs_ref, meta_ref, out_ref, sum_ref):
-    sum_ref[...] = -dot(push_ref[...], recv_ref[...])
+    flipped = [span_ref[pair].astype(F32) for pair in range(3)]
+    side_ref[32:48, :] = jnp.concatenate(flipped + [tail], axis=1).astype(BF)
+    side_ref[48:, :] = jnp.zeros((512, 256), BF)
     for level in range(3):
-        at = pl.ds(pl.multiple_of(where_ref[level], SUB), SUB)
-        sum_ref[at, :] = sum_ref[at, :] + srhs_ref[level].astype(F32)
-    turned = sum_ref[...].T.astype(BF)
-    meta = meta_ref[...]
+        at = pl.ds(pl.multiple_of(where_ref[level] + 48, SUB), SUB)
+        side_ref[at, :] = srhs_ref[level]
+
+
+def push_kernel(recv_ref, push_ref, side_ref, out_ref):
+    sums = side_ref[48:, :].astype(F32) - dot(push_ref[...], recv_ref[...])
+    turned = sums.T.astype(BF)
+    meta = side_ref[0:48, :]
     for member in range(TEAM):
         part = turned[member * SUB : (member + 1) * SUB, :]
         out_ref[member, 0:16, :] = part[:, 0:256]
@@ -115,17 +148,19 @@
         out_ref[member, 32:80, :] = meta
 
 
-def leaf_kernel(place_ref, recv_ref, inv_ref, out_ref):
+def leaf_kernel(place_ref, recv_ref, inv_hbm, out_ref, inv_ref, sem):
+    inv_in = fetch(inv_hbm, inv_ref, sem)
     leaf = inv_ref.shape[0]
     slots = place_ref.shape[1]
     spread = hot(row_ids(leaf, slots) == place_ref[...])
-    owned = dot(spread, recv_ref[...])
+    owned = dot(spread, recv_ref[...]).T.astype(BF)
+    inv_in.wait()
     inv = inv_ref[...]
-    y_t = dot(owned.T.astype(BF), inv, NT).astype(BF)
+    y_t = dot(owned, inv, NT).astype(BF)
     out_ref[...] = dot(y_t, inv).T
 
 
-def tree_kernel(got_ref, out_ref, e0_ref, e1_ref, e2_ref, a01_ref, a02_ref, a12_ref):
+def tree_kernel(got_ref, bare_hbm, out_ref, e0_ref, e1_ref, e2_ref, a01_ref, a02_ref, a12_ref):
     lane = lane_ids(32, 128)
     none = jnp.zeros((32, 128), BF)
     for peer in range(TREE):
@@ -236,14 +271,21 @@
     slots = owners * pad
     sds = jax.ShapeDtypeStruct
 
-    sent = call(
+    (sent,) = call(
         lambda *refs: send_kernel(keep, pad, *refs),
         "send_rows",
-        sds((slots, width), BF),
-        [pltpu.VMEM((-(-(leaf - keep + pad) // 8) * 8 + 8, width), F32)],
+        [HB, HB],
+        [(sds((slots, width), BF), HB)],
+        [
+            pltpu.VMEM((1, leaf), jnp.int32),
+            pltpu.VMEM((leaf, width), BF),
+            pltpu.VMEM((-(-(leaf - keep + pad) // 8) * 8 + 8, width), F32),
+            pltpu.VMEM((slots, width), BF),
+            DMA((5,)),
+        ],
         flops=2 * leaf * leaf * width,
         nbytes=2 * leaf * width * 2,
-        nargs=2,
+        vmem=VMEM_ALL,
     )(send_order[0], rhs)
     recv = lax.all_to_all(
         sent.reshape(owners, pad, width), ("tree", "peer"), split_axis=0, concat_axis=0, tiled=True
@@ -252,24 +294,6 @@
     place = jnp.pad(
         recv_place[0, 0].reshape(owners, keep), ((0, 0), (0, pad - keep)), constant_values=-1
     ).reshape(1, slots)
-    push, back, meta = call(
-        factor_kernel,
-        "factor_products",
-        (sds((512, slots), BF), sds((leaf, 512), BF), sds((48, 256), BF)),
-        [pltpu.VMEM((512, leaf), F32)],
-        flops=2 * 192 * leaf * (leaf + slots) + 2 * 448 * 64 * (leaf + slots),
-        nbytes=2 * leaf * leaf + 4 * 512 * slots,
-        nargs=7,
-    )(
-        place,
-        leaf_rows[0, 0],
-        panels,
-        inv,
-        sep_inv[0, 0],
-        sep_panels[0, 0].reshape(-1, SUB),
-        sep_rows[0, 0],
-    )
-
     peer = lax.axis_index("peer")
     front = lax.axis_index("front")
     where = jnp.stack(
@@ -279,48 +303,75 @@
             (peer * 2 + front) * SUB,
         ]
     ).astype(jnp.int32)
+    span = jnp.swapaxes(sep_panels[0, 0], 1, 2)
+    push, back, side = call(
+        factor_kernel,
+        "factor_products",
+        [SM, VM, VM, VM, HB, HB, HB, HB, HB],
+        [(sds((512, slots), BF), VM), (sds((leaf, 512), BF), VM), (sds((560, 256), BF), VM)],
+        [
+            pltpu.VMEM((512, leaf), F32),
+            pltpu.VMEM(panels.shape, BF),
+            pltpu.VMEM((leaf, leaf), BF),
+            pltpu.VMEM(sep_inv.shape[2:], BF),
+            pltpu.VMEM(span.shape, BF),
+            pltpu.VMEM(sep_rhs.shape[2:], BF),
+            DMA((5,)),
+        ],
+        flops=2 * 192 * leaf * (leaf + slots) + 2 * 448 * 64 * (leaf + slots),
+        nbytes=2 * leaf * leaf + 4 * 512 * slots,
+    )(
+        where,
+        place,
+        leaf_rows[0, 0],
+        sep_rows[0, 0],
+        panels,
+        inv,
+        sep_inv[0, 0],
+        span,
+        sep_rhs[0, 0],
+    )
+
     team = ("peer", "front")
-    chunks = call(
+    (chunks,) = call(
         push_kernel,
         "push_updates",
-        sds((TEAM, 80, 256), BF),
-        [pltpu.VMEM((512, width), F32)],
+        [VM, VM, VM],
+        [(sds((TEAM, 80, 256), BF), VM)],
         flops=2 * 512 * slots * width,
         nbytes=2 * slots * (512 + width) + TEAM * 80 * 512,
-        smem_first=True,
-        nargs=5,
-    )(where, recv, push, sep_rhs[0, 0], meta)
+    )(recv, push, side)
     got = lax.all_to_all(chunks, team, split_axis=0, concat_axis=0, tiled=True)
 
-    bare = call(
+    (bare,) = call(
         leaf_kernel,
         "leaf_solve",
-        sds((leaf, width), F32),
+        [VM, VM, HB],
+        [(sds((leaf, width), F32), VM)],
+        [pltpu.VMEM((leaf, leaf), BF), DMA],
         flops=2 * leaf * width * (2 * leaf + slots),
         nbytes=2 * leaf * leaf + 6 * slots * width,
-        nargs=3,
     )(place, recv, inv)
 
     square = pltpu.VMEM((256, 256), BF)
-    solved = call(
+    (solved,) = call(
         tree_kernel,
         "separator_tree",
-        sds((TEAM, 32, 256), BF),
+        [VM, pl.BlockSpec(memory_space=pl.ANY)],
+        [(sds((TEAM, 32, 256), BF), VM)],
         [square] * 6,
         flops=2 * 16 * 256 * 256 * 12 + 2 * 48 * 16 * 64 * 256,
         nbytes=TEAM * 112 * 512,
-        nargs=1,
-    )(got)
+    )(got, bare)
     back_got = lax.all_to_all(solved, team, split_axis=0, concat_axis=0, tiled=True)
 
     leaf_solution, sep_solution = call(
         finish_kernel,
         "finish",
-        (sds((leaf, width), F32), sds((3, SUB, width), BF)),
+        [SM, VM, VM, VM],
+        [(sds((leaf, width), F32), VM), (sds((3, SUB, width), BF), VM)],
         flops=2 * leaf * 512 * width,
         nbytes=leaf * width * 8 + leaf * 1024 + TEAM * 32 * 512,
-        smem_first=True,
-        nargs=4,
     )(where, back_got, back, bare)
     return leaf_solution[None, None], sep_solution[None, None]
 

time: 67.2 us -> 64.8 us (0.964)
  local copies, waits for them, and re-layouts: 10.8 us -> 4.78 us
  blocking collectives: 16.3 us -> 10.6 us
  waiting for transfers between devices: 7.34 us -> 12 us
  Pallas kernels: 15.3 us -> 18.5 us
  starting transfers between devices: 15.9 us -> 17.6 us
    unnamed x30 -> x23, local copies, waits for them, and re-layouts: 10.6 us -> 4.55 us
    all_to_all x1, blocking collectives: 16.3 us -> 10.6 us  [on_device(): lax.all_to_all(solved, team, split_axis=0, concat_axis=0, tiled=True)]
    all_to_all x1, waiting for transfers between devices: 0.93 us -> 4.67 us  [on_device(): got = lax.all_to_all(chunks, team, split_axis=0, concat_axis=0, tiled=True)]
    pallas_call x6, Pallas kernels: 15.3 us -> 18.5 us  [the longest x1 5.12 us: on_device(): call(leaf_kernel, 'leaf_solve', [VM, VM, HB], [(sds((leaf, width), F32),...]
    all_to_all x1, starting transfers between devices: 3.77 us -> 5.53 us  [on_device(): got = lax.all_to_all(chunks, team, split_axis=0, concat_axis=0, tiled=True)]
    all_to_all x1, waiting for transfers between devices: 6.4 us -> 7.3 us  [on_device(): lax.all_to_all(sent.reshape(owners, pad, width), ('tree', 'peer'), split_...]
  transfers between devices with their start and end apart: 2 -> 2, of which waited for: 2 -> 2; matrix products, arithmetic and copies ran while one was open for 2% -> 1% of each run, Pallas kernels for 11% -> 15%
where the time goes in v2:
time: 64.8 us; the launch traced here: 64.4 us
  Pallas kernels  18.5 us (29%)
  starting transfers between devices  17.6 us (27%)
  waiting for transfers between devices  12 us (19%)
  blocking collectives  10.6 us (16%)
  local copies, waits for them, and re-layouts  4.78 us (7%)
  between operations  0.84 us (1%)
    all_to_all x1, starting transfers between devices, on_device(): lax.all_to_all(sent.reshape(owners, pad, width), ('tree', 'peer'), split_...  12.1 us
    all_to_all x1, blocking collectives, on_device(): lax.all_to_all(solved, team, split_axis=0, concat_axis=0, tiled=True)  10.6 us
    all_to_all x1, waiting for transfers between devices, on_device(): lax.all_to_all(sent.reshape(owners, pad, width), ('tree', 'peer'), split_...  7.3 us
    all_to_all x1, starting transfers between devices, on_device(): got = lax.all_to_all(chunks, team, split_axis=0, concat_axis=0, tiled=True)  5.53 us
    pallas_call x1, Pallas kernels, on_device(): call(leaf_kernel, 'leaf_solve', [VM, VM, HB], [(sds((leaf, width), F32),...  5.12 us
    all_to_all x1, waiting for transfers between devices, on_device(): got = lax.all_to_all(chunks, team, split_axis=0, concat_axis=0, tiled=True)  4.67 us
    unnamed x23, local copies, waits for them, and re-layouts  4.55 us
    pallas_call x1, Pallas kernels, on_device(): call(factor_kernel, 'factor_products', [SM, VM, VM, VM, HB, HB, HB, HB, H...  4.41 us
  transfers between devices with their start and end apart: 2, of which 2 were waited for; matrix products, arithmetic and copies ran while one was open for 1% of the time, Pallas kernels for 15%

profile of v2, /device:TPU:1, one launch (start us, length us, event | category | flops | bytes accessed | tf_op | source)
XLA Modules:
  0.0 64.4 jit_solution(13671288145625004883)
XLA Ops:
  0.6 3.3 %send_rows.1 = bf16[1536,256]{1,0:T(8,128)(2,1)} custom-call(s32[1,1152]{1,0:T(1,128)} %bitcast.32, bf16[1152,256]{1,0:T(8,128)(2,1)} %bitcast.30), custom_call_target="tpu_custom_call" | custom-call | flops 679477248 | bytes 1179648 | tf_op jit(solution)/shard_map/send_rows/pallas_call | solution.py:274
  3.9 0.0 copy-start.8
  3.9 0.0 copy-start.9
  3.9 0.0 copy-start.10
  3.9 0.0 copy-start.4
  3.9 0.0 copy-start.5
  4.0 0.0 copy-start.6
  4.0 0.0 copy-start.7
  4.0 12.1 %all-to-all-start = ((bf16[64,24,256]{2,1,0:T(8,128)(2,1)}), bf16[64,24,256]{2,1,0:T(8,128)(2,1)S(1)}, u32[]{:S(2)}, u32[]{:S(2)}) async-start(bf16[64,24,256]{2,1,0:T(8,128)(2,1)} %bitcast.28), calls=%async_computation | async-start | bytes 1572864 | tf_op jit(solution)/shard_map/all_to_all | solution.py:290
  16.1 0.0 copy-done.8
  16.2 0.1 reshape_squeeze.6
  16.3 0.1 reshape.15.place_ref
  16.4 0.1 pad_add_fusion.where_ref
  16.5 0.0 copy-done.9
  16.5 0.0 copy-done.10
  16.5 0.0 copy-done.4
  16.5 0.0 copy-done.5
  16.5 0.0 copy-done.6
  16.5 0.0 copy-done.7
  16.5 0.0 copy-start.2
  16.6 1.7 %copy-done.2 = bf16[1,1,1152,1152]{3,2,1,0:T(8,128)(2,1)S(1)} copy-done((bf16[1,1,1152,1152]{3,2,1,0:T(8,128)(2,1)S(1)}, bf16[1,1,1152,1152]{3,2,1,0:T(8,128)(2,1)}, u32[]{:S(2)}) %copy-start.2) | copy-done | bytes 2654232
  18.3 4.4 %factor_products.1 = (bf16[512,1536]{1,0:T(8,128)(2,1)S(1)}, bf16[1152,512]{1,0:T(8,128)(2,1)S(1)}, bf16[560,256]{1,0:T(8,128)(2,1)S(1)}) custom-call(s32[3]{0:T(128)S(1)} %pad_add_fusion.where_ref, s32[1,1536]{1,0:T(1,128)S(1)} %reshape.15.place_ref, s32[3,64]{1,0:T(4,128)S(1)} %get-tuple-element.13.rows_ref, s32[3,64]{1,0:T(4,128)S(1)} %get-tuple-element.12.srow_ref, ...), custom_call_target="tpu_custom_call" | custom-call | flops 1343225856 | bytes 5799936 | tf_op jit(solution)/shard_map/factor_products/pallas_call | solution.py:307
  22.7 0.0 copy-start
  22.7 1.0 %copy-done = bf16[1152,512]{1,0:T(8,128)(2,1)} copy-done((bf16[1152,512]{1,0:T(8,128)(2,1)}, bf16[1152,512]{1,0:T(8,128)(2,1)S(1)}, u32[]{:S(2)}) %copy-start) | copy-done | bytes 1179672
  23.7 7.3 %all-to-all-done = bf16[64,24,256]{2,1,0:T(8,128)(2,1)S(1)} async-done(((bf16[64,24,256]{2,1,0:T(8,128)(2,1)}), bf16[64,24,256]{2,1,0:T(8,128)(2,1)S(1)}, u32[]{:S(2)}, u32[]{:S(2)}) %all-to-all-start) | async-done | bytes 786464 | tf_op jit(solution)/shard_map/all_to_all | solution.py:290
  31.0 1.5 %push_updates.1 = bf16[16,80,256]{2,1,0:T(8,128)(2,1)} custom-call(bf16[1536,256]{1,0:T(8,128)(2,1)S(1)} %bitcast.20, bf16[512,1536]{1,0:T(8,128)(2,1)S(1)} %get-tuple-element.7.push_ref, bf16[560,256]{1,0:T(8,128)(2,1)S(1)} %get-tuple-element.8.side_ref), custom_call_target="tpu_custom_call" | custom-call | flops 402653184 | bytes 3014656 | tf_op jit(solution)/shard_map/push_updates/pallas_call | solution.py:336
  32.5 5.5 %all-to-all-start.1 = ((bf16[16,80,256]{2,1,0:T(8,128)(2,1)}), bf16[16,80,256]{2,1,0:T(8,128)(2,1)S(1)}, u32[]{:S(2)}, u32[]{:S(2)}) async-start(bf16[16,80,256]{2,1,0:T(8,128)(2,1)} %push_updates.1), calls=%async_computation.1 | async-start | bytes 1310720 | tf_op jit(solution)/shard_map/all_to_all | solution.py:344
  38.1 0.0 copy-start.3
  38.1 1.7 %copy-done.3 = bf16[1,1,1152,1152]{3,2,1,0:T(8,128)(2,1)S(1)} copy-done((bf16[1,1,1152,1152]{3,2,1,0:T(8,128)(2,1)S(1)}, bf16[1,1,1152,1152]{3,2,1,0:T(8,128)(2,1)}, u32[]{:S(2)}) %copy-start.3) | copy-done | bytes 2654232
  39.8 5.1 %leaf_solve.1.bare_hbm.leaf_ref = f32[1152,256]{1,0:T(8,128)S(1)} custom-call(s32[1,1536]{1,0:T(1,128)S(1)} %reshape.15.place_ref, bf16[1536,256]{1,0:T(8,128)(2,1)S(1)} %bitcast.21, bf16[1152,1152]{1,0:T(8,128)(2,1)S(1)} %bitcast.23), custom_call_target="tpu_custom_call" | custom-call | flops 2264924160 | bytes 5013504 | tf_op jit(solution)/shard_map/leaf_solve/pallas_call | solution.py:346
  44.9 4.7 %all-to-all-done.1.got_ref = bf16[16,80,256]{2,1,0:T(8,128)(2,1)S(1)} async-done(((bf16[16,80,256]{2,1,0:T(8,128)(2,1)}), bf16[16,80,256]{2,1,0:T(8,128)(2,1)S(1)}, u32[]{:S(2)}, u32[]{:S(2)}) %all-to-all-start.1) | async-done | bytes 655392 | tf_op jit(solution)/shard_map/all_to_all | solution.py:344
  49.6 0.0 copy-start.1
  49.6 2.2 %separator_tree.1 = bf16[16,32,256]{2,1,0:T(8,128)(2,1)S(1)} custom-call(bf16[16,80,256]{2,1,0:T(8,128)(2,1)S(1)} %all-to-all-done.1.got_ref, f32[1152,256]{1,0:T(8,128)S(1)} %leaf_solve.1.bare_hbm.leaf_ref), custom_call_target="tpu_custom_call" | custom-call | flops 50331648 | bytes 917504 | tf_op jit(solution)/shard_map/separator_tree/pallas_call | solution.py:357
  51.8 10.6 %all_to_all.15.got_ref = bf16[16,32,256]{2,1,0:T(8,128)(2,1)S(1)} all-to-all(bf16[16,32,256]{2,1,0:T(8,128)(2,1)S(1)} %separator_tree.1), channel_id=1, replica_groups=mesh['tree'=8,'peer'=8,'front'=2] {'peer','front'}, dimensions={0} | all-to-all | bytes 524288 | tf_op jit(solution)/shard_map/all_to_all | solution.py:366
  62.4 0.0 copy-done.1
  62.4 2.1 %finish.1 = (f32[1152,256]{1,0:T(8,128)}, bf16[3,16,256]{2,1,0:T(8,128)(2,1)}) custom-call(s32[3]{0:T(128)S(1)} %pad_add_fusion.where_ref, bf16[16,32,256]{2,1,0:T(8,128)(2,1)S(1)} %all_to_all.15.got_ref, bf16[1152,512]{1,0:T(8,128)(2,1)S(1)} %copy-done.1, f32[1152,256]{1,0:T(8,128)S(1)} %leaf_solve.1.bare_hbm.leaf_ref), custom_call_target="tpu_custom_call" | custom-call | flops 301989888 | bytes 3801088 | tf_op jit(solution)/shard_map/finish/pallas_call | solution.py:368
  (3 shorter events, 0.0 us)
Async XLA Ops:
  3.9 12.2 %copy-start.8 = (s32[1,1,1152]{2,1,0:T(1,128)S(1)}, s32[1,1,1152]{2,1,0:T(1,128)}, u32[]{:S(2)}) copy-start(s32[1,1,1152]{2,1,0:T(1,128)} %param.12) | copy-start | bytes 13828
  3.9 12.6 %copy-start.9 = (s32[1,1,3,64]{3,1,2,0:T(1,128)S(1)}, s32[1,1,3,64]{3,1,2,0:T(1,128)}, u32[]{:S(2)}) copy-start(s32[1,1,3,64]{3,1,2,0:T(1,128)} %param.19) | copy-start | bytes 2308
  3.9 12.6 %copy-start.10 = (s32[1,1,3,64]{3,1,2,0:T(1,128)S(1)}, s32[1,1,3,64]{3,1,2,0:T(1,128)}, u32[]{:S(2)}) copy-start(s32[1,1,3,64]{3,1,2,0:T(1,128)} %param.16) | copy-start | bytes 2308
  3.9 12.6 %copy-start.4 = (bf16[1,1,3,64,1152]{4,3,2,1,0:T(8,128)(2,1)S(1)}, bf16[1,1,3,64,1152]{4,3,2,1,0:T(8,128)(2,1)}, u32[]{:S(2)}) copy-start(bf16[1,1,3,64,1152]{4,3,2,1,0:T(8,128)(2,1)} %param.15) | copy-start | bytes 1327108
  3.9 12.6 %copy-start.5 = (bf16[1,1,3,16,256]{4,3,2,1,0:T(8,128)(2,1)S(1)}, bf16[1,1,3,16,256]{4,3,2,1,0:T(8,128)(2,1)}, u32[]{:S(2)}) copy-start(bf16[1,1,3,16,256]{4,3,2,1,0:T(8,128)(2,1)} %param.13) | copy-start | bytes 73732
  4.0 12.6 %copy-start.6 = (bf16[1,1,32,224]{3,2,1,0:T(8,128)(2,1)S(1)}, bf16[1,1,32,224]{3,2,1,0:T(8,128)(2,1)}, u32[]{:S(2)}) copy-start(bf16[1,1,32,224]{3,2,1,0:T(8,128)(2,1)} %param.17) | copy-start | bytes 43012
  4.0 12.6 %copy-start.7 = (bf16[1,1,3,64,16]{3,4,2,1,0:T(8,128)(2,1)S(1)}, bf16[1,1,3,64,16]{3,4,2,1,0:T(8,128)(2,1)}, u32[]{:S(2)}) copy-start(bf16[1,1,3,64,16]{3,4,2,1,0:T(8,128)(2,1)} %param.18) | copy-start | bytes 18436
  4.0 27.0 %all-to-all-start = ((bf16[64,24,256]{2,1,0:T(8,128)(2,1)}), bf16[64,24,256]{2,1,0:T(8,128)(2,1)S(1)}, u32[]{:S(2)}, u32[]{:S(2)}) async-start(bf16[64,24,256]{2,1,0:T(8,128)(2,1)} %bitcast.28), calls=%async_computation | async-start | bytes 1572864 | tf_op jit(solution)/shard_map/all_to_all | solution.py:290
  16.5 1.8 %copy-start.2 = (bf16[1,1,1152,1152]{3,2,1,0:T(8,128)(2,1)S(1)}, bf16[1,1,1152,1152]{3,2,1,0:T(8,128)(2,1)}, u32[]{:S(2)}) copy-start(bf16[1,1,1152,1152]{3,2,1,0:T(8,128)(2,1)} %param.14) | copy-start | bytes 7962628
  22.7 1.0 %copy-start = (bf16[1152,512]{1,0:T(8,128)(2,1)}, bf16[1152,512]{1,0:T(8,128)(2,1)S(1)}, u32[]{:S(2)}) copy-start(bf16[1152,512]{1,0:T(8,128)(2,1)S(1)} %get-tuple-element.9.back_ref) | copy-start | bytes 3538948
  32.5 17.1 %all-to-all-start.1 = ((bf16[16,80,256]{2,1,0:T(8,128)(2,1)}), bf16[16,80,256]{2,1,0:T(8,128)(2,1)S(1)}, u32[]{:S(2)}, u32[]{:S(2)}) async-start(bf16[16,80,256]{2,1,0:T(8,128)(2,1)} %push_updates.1), calls=%async_computation.1 | async-start | bytes 1310720 | tf_op jit(solution)/shard_map/all_to_all | solution.py:344
  38.1 1.7 %copy-start.3 = (bf16[1,1,1152,1152]{3,2,1,0:T(8,128)(2,1)S(1)}, bf16[1,1,1152,1152]{3,2,1,0:T(8,128)(2,1)}, u32[]{:S(2)}) copy-start(bf16[1,1,1152,1152]{3,2,1,0:T(8,128)(2,1)} %param.14) | copy-start | bytes 7962628
  49.6 12.8 %copy-start.1 = (bf16[1152,512]{1,0:T(8,128)(2,1)S(1)}, bf16[1152,512]{1,0:T(8,128)(2,1)}, u32[]{:S(2)}) copy-start(bf16[1152,512]{1,0:T(8,128)(2,1)} %copy-done) | copy-start | bytes 3538948

commit v3 on v2

v3 whole, which is shorter than its diff:
```python
import jax
import jax.numpy as jnp
import numpy as np
from jax import lax
from jax.experimental import pallas as pl
from jax.experimental.pallas import tpu as pltpu
from jax.sharding import Mesh, PartitionSpec as P

BF = jnp.bfloat16
F32 = jnp.float32
SUB = 16
TREE = 8
TEAM = 16
VMEM_CAP = 40 * 1024 * 1024
VMEM_ALL = 62 * 1024 * 1024

NN = (((1,), (0,)), ((), ()))
NT = (((1,), (1,)), ((), ()))


def dot(a, b, dims=NN):
    return lax.dot_general(a, b, dims, preferred_element_type=F32)


def lane_ids(rows, cols):
    return lax.broadcasted_iota(jnp.int32, (rows, cols), 1)


def row_ids(rows, cols):
    return lax.broadcasted_iota(jnp.int32, (rows, cols), 0)


def hot(mask):
    return jnp.where(mask, 1.0, 0.0).astype(BF)


VM = pl.BlockSpec(memory_space=pltpu.VMEM)
SM = pl.BlockSpec(memory_space=pltpu.SMEM)
HB = pl.BlockSpec(memory_space=pltpu.HBM)
DMA = pltpu.SemaphoreType.DMA


def call(kernel, name, ins, outs, scratch=(), flops=0, nbytes=0, vmem=VMEM_CAP):
    return pl.pallas_call(
        kernel,
        out_shape=[shape for shape, _ in outs],
        in_specs=list(ins),
        out_specs=[spec for _, spec in outs],
        scratch_shapes=list(scratch),
        compiler_params=pltpu.CompilerParams(vmem_limit_bytes=vmem),
        cost_estimate=pl.CostEstimate(flops=flops, bytes_accessed=nbytes, transcendentals=0),
        name=name,
    )


def fetch(source, target, sem):
    copy = pltpu.make_async_copy(source, target, sem)
    copy.start()
    return copy


def send_kernel(keep, pad, order_hbm, rhs_hbm, out_hbm, order_ref, rhs_ref, picked_ref, out_ref, sems):
    rows, width = rhs_ref.shape
    order_in = fetch(order_hbm, order_ref, sems.at[0])
    rhs_in = fetch(rhs_hbm, rhs_ref, sems.at[1])
    tail = picked_ref.shape[0] - rows
    picked_ref[rows:, :] = jnp.zeros((tail, width), F32)
    owners = rows // keep
    step = 384
    lanes = lane_ids(128, rows)
    order_in.wait()
    hots = []
    for at in range(0, rows, 128):
        ids = jnp.broadcast_to(order_ref[:, at : at + 128], (128, 128)).T
        hots.append(hot(jnp.concatenate([ids] * (rows // 128), axis=1) == lanes))
    rhs_in.wait()
    rhs = rhs_ref[...]
    done = 0
    leaving = []
    for part in range(rows // step):
        block = jnp.concatenate(hots[part * 3 : part * 3 + 3], axis=0)
        picked_ref[part * step : (part + 1) * step, :] = dot(block, rhs)
        have = (part + 1) * step
        upto = owners if have == rows else ((have - pad) // keep + 1) // 2 * 2
        for owner in range(done, upto):
            out_ref[owner * pad : (owner + 1) * pad, :] = picked_ref[
                owner * keep : owner * keep + pad, :
            ].astype(BF)
        span = slice(done * pad, upto * pad)
        leaving.append(fetch(out_ref.at[span, :], out_hbm.at[span, :], sems.at[2 + part]))
        done = upto
    for copy in leaving:
        copy.wait()


def factor_kernel(
    place_ref, rows_ref, srow_ref, panels_hbm, inv_hbm, sinv_hbm, span_hbm, srhs_hbm,
    push_ref, back_ref, side_ref, panels_ref, inv_ref, sinv_ref, span_ref, srhs_ref, sems,
):
    moves = [
        fetch(sinv_hbm, sinv_ref, sems.at[0]),
        fetch(span_hbm, span_ref, sems.at[1]),
        fetch(srhs_hbm, srhs_ref, sems.at[2]),
        fetch(panels_hbm, panels_ref, sems.at[3]),
        fetch(inv_hbm, inv_ref, sems.at[4]),
    ]
    leaf = inv_ref.shape[0]
    slots = place_ref.shape[1]
    upd = rows_ref.shape[2]
    spread = hot(row_ids(leaf, slots) == place_ref[...])
    for move in moves:
        move.wait()
    product = dot(panels_ref[...], inv_ref[...])
    push_ref[...] = dot(product.astype(BF), spread).astype(BF)
    padded = jnp.concatenate([product, jnp.zeros((256 - product.shape[0], leaf), F32)], axis=0)
    back_ref[...] = padded.T.astype(BF)
    cols = sinv_ref.shape[1]
    lane = lane_ids(cols, 256)
    source = jnp.where(
        lane < 128, lane + 96, jnp.where(lane < 192, lane - 96, jnp.where(lane < 224, lane - 192, -1))
    )
    side_ref[0:32, :] = dot(sinv_ref[...], hot(row_ids(cols, 256) == source)).astype(BF)
    lists = [srow_ref[pair].astype(F32) for pair in range(3)]
    lists += [rows_ref[level].astype(F32) for level in range(3)]
    lists = jnp.concatenate(lists + [jnp.zeros((SUB - 6, upd), F32)], axis=0)
    flipped = [span_ref[pair].astype(F32) for pair in range(3)]
    side_ref[32:48, :] = jnp.concatenate(flipped + [lists], axis=1).astype(BF)
    for level in range(3):
        side_ref[48 + level * SUB : 64 + level * SUB, :] = srhs_ref[level]
    side_ref[96:112, :] = jnp.zeros((SUB, 256), BF)


def push_kernel(recv_ref, push_ref, side_ref, out_ref):
    sums = dot(push_ref[...], recv_ref[...])
    rows = jnp.concatenate([sums, side_ref[48:112, :].astype(F32)], axis=0)
    turned = rows.T.astype(BF)
    meta = side_ref[0:48, :]
    for member in range(TEAM):
        out_ref[member, 0:16, :] = turned[member * SUB : (member + 1) * SUB, :]
        out_ref[member, 16:64, :] = meta


def leaf_kernel(place_ref, recv_ref, inv_hbm, out_ref, inv_ref, sem):
    inv_in = fetch(inv_hbm, inv_ref, sem)
    leaf = inv_ref.shape[0]
    slots = place_ref.shape[1]
    spread = hot(row_ids(leaf, slots) == place_ref[...])
    owned = dot(spread, recv_ref[...]).T.astype(BF)
    inv_in.wait()
    inv = inv_ref[...]
    y_t = dot(owned, inv, NT).astype(BF)
    out_ref[...] = dot(y_t, inv).T


def turn(value, shift):
    shift = shift % 128
    return pltpu.roll(value, shift, 1) if shift else value


def tree_kernel(got_ref, bare_hbm, out_ref, e0_ref, e1_ref, e2_ref, a01_ref, a02_ref, a12_ref, spots_ref):
    lane = lane_ids(32, 128)
    none = jnp.zeros((32, 128), BF)
    for peer in range(TREE):
        rows = slice(peer * 32, (peer + 1) * 32)
        low0 = jnp.zeros((32, 128), F32)
        low1 = jnp.zeros((32, 128), F32)
        for front in range(2):
            src = peer * 2 + front
            e2_ref[rows, front * 128 : (front + 1) * 128] = got_ref[src, 16:48, 0:128]
            rest = got_ref[src, 16:48, 128:256].astype(F32)
            one = jnp.where(lane < 64, rest, 0.0)
            zero = jnp.where((lane >= 64) & (lane < 96), rest, 0.0)
            low1 = low1 + turn(one, front * 64)
            low0 = low0 + turn(zero, ((peer // 2) % 2) * 64 + front * 32 - 64)
        tile = peer // 4
        for ref, low in ((e1_ref, low1), (e0_ref, low0)):
            ref[rows, tile * 128 : (tile + 1) * 128] = low.astype(BF)
            ref[rows, (1 - tile) * 128 : (2 - tile) * 128] = none
    sub = row_ids(256, 64)
    for src in range(TEAM):
        for pair, ref in enumerate((a01_ref, a02_ref, a12_ref)):
            where = got_ref[src, 48 + pair : 49 + pair, 192:256].astype(F32).astype(jnp.int32)
            if pair == 0:
                where = where + src // 8 * 128
            flipped = got_ref[src, 48:64, pair * 64 : (pair + 1) * 64]
            ref[src * SUB : (src + 1) * SUB, :] = dot(flipped, hot(sub == where), NT).astype(BF)
    wide = row_ids(256, 256)
    for level in range(3):
        for quad in range(4):
            parts = []
            for src in range(quad * 4, quad * 4 + 4):
                where = got_ref[src, 51 + level : 52 + level, 192:256].astype(F32)
                parts.append(where + (src // 4 * 64, src // 8 * 128, 0)[level])
            where = jnp.concatenate(parts, axis=1).astype(jnp.int32)
            spots_ref[level * 4 + quad] = hot(wide == where)
    lane = lane_ids(SUB, 128)
    first = lane < 64
    sums = []
    for level in range(3):
        tiles = []
        for tile in range(2):
            total = jnp.zeros((SUB, 128), F32)
            for at in range(8):
                piece = got_ref[tile * 8 + at, 0:16, 128:256].astype(F32)
                begin = 64 + level * SUB
                piece = jnp.where((lane >= begin) & (lane < begin + SUB), piece, 0.0)
                total = total + turn(piece, at * SUB - begin)
            tiles.append(total)
        rest = jnp.concatenate(tiles, axis=1)
        tile = slice(level // 2 * 128, level // 2 * 128 + 128)
        for quad in range(4):
            halves = []
            for pair in range(2):
                left = got_ref[quad * 4 + pair * 2, 0:16, tile].astype(F32)
                right = got_ref[quad * 4 + pair * 2 + 1, 0:16, tile].astype(F32)
                if level == 1:
                    halves.append(jnp.where(first, turn(left, 64), right))
                else:
                    halves.append(jnp.where(first, left, turn(right, 64)))
            moved = jnp.concatenate(halves, axis=1).astype(BF)
            rest = rest - dot(moved, spots_ref[level * 4 + quad], NT)
        sums.append(rest)
    r0, r1, r2 = sums
    e0, e1, e2 = e0_ref[...], e1_ref[...], e2_ref[...]
    a01, a02, a12 = a01_ref[...], a02_ref[...], a12_ref[...]
    y0 = dot(r0.astype(BF), e0, NT)
    y0b = y0.astype(BF)
    y1 = dot((r1 - dot(y0b, a01)).astype(BF), e1, NT)
    y1b = y1.astype(BF)
    y2 = dot((r2 - dot(y0b, a02) - dot(y1b, a12)).astype(BF), e2, NT)
    x2 = dot(y2.astype(BF), e2).astype(BF)
    x1 = dot((y1 - dot(x2, a12, NT)).astype(BF), e1).astype(BF)
    x0 = dot((y0 - dot(x2, a02, NT) - dot(x1, a01, NT)).astype(BF), e0).astype(BF)
    solved = (x0, x1, x2)
    for quad in range(4):
        picks = [dot(solved[level], spots_ref[level * 4 + quad]) for level in range(3)]
        for at in range(4):
            dst = quad * 4 + at
            half = slice(at // 2 * 128, at // 2 * 128 + 128)
            p0, p1, p2 = [pick[:, half] for pick in picks]
            if at % 2:
                p0, p2 = turn(p0, 64), turn(p2, 64)
            else:
                p1 = turn(p1, 64)
            out_ref[dst, :, 0:128] = jnp.where(first, p0, p1).astype(BF)
            rest = jnp.where(first, p2, 0.0)
            tile = slice(dst // 8 * 128, dst // 8 * 128 + 128)
            for level in range(3):
                begin = 64 + level * SUB
                piece = turn(solved[level][:, tile].astype(F32), begin - dst % 8 * SUB)
                rest = jnp.where((lane >= begin) & (lane < begin + SUB), piece, rest)
            out_ref[dst, :, 128:256] = rest.astype(BF)


def finish_kernel(got_ref, back_ref, leaf_ref, out_ref, sep_ref):
    table = got_ref[...].reshape(256, 256)
    out_ref[...] = leaf_ref[...] - dot(back_ref[...], table, NT)
    pick = hot(lane_ids(48, 256) == row_ids(48, 256) + 192)
    rows = dot(pick, table, NT).astype(BF)
    for level in range(3):
        sep_ref[level] = rows[level * SUB : (level + 1) * SUB, :]


def on_device(
    rhs_parts,
    send_order,
    recv_place,
    sep_rhs,
    leaf_inv,
    leaf_panels,
    leaf_rows,
    sep_inv,
    sep_panels,
    sep_rows,
):
    owners = lax.axis_size("tree") * lax.axis_size("peer")
    rhs = rhs_parts[0, 0]
    leaf, width = rhs.shape
    inv = leaf_inv[0, 0]
    panels = leaf_panels[0, 0].reshape(-1, leaf)
    keep = leaf // owners
    pad = -(-keep // 8) * 8
    slots = owners * pad
    sds = jax.ShapeDtypeStruct

    (sent,) = call(
        lambda *refs: send_kernel(keep, pad, *refs),
        "send_rows",
        [HB, HB],
        [(sds((slots, width), BF), HB)],
        [
            pltpu.VMEM((1, leaf), jnp.int32),
            pltpu.VMEM((leaf, width), BF),
            pltpu.VMEM((-(-(leaf - keep + pad) // 8) * 8 + 8, width), F32),
            pltpu.VMEM((slots, width), BF),
            DMA((5,)),
        ],
        flops=2 * leaf * leaf * width,
        nbytes=2 * leaf * width * 2,
        vmem=VMEM_ALL,
    )(send_order[0], rhs)
    recv = lax.all_to_all(
        sent.reshape(owners, pad, width), ("tree", "peer"), split_axis=0, concat_axis=0, tiled=True
    ).reshape(slots, width)

    place = jnp.pad(
        recv_place[0, 0].reshape(owners, keep), ((0, 0), (0, pad - keep)), constant_values=-1
    ).reshape(1, slots)
    span = jnp.swapaxes(sep_panels[0, 0], 1, 2)
    push, back, side = call(
        factor_kernel,
        "factor_products",
        [VM, VM, VM, HB, HB, HB, HB, HB],
        [(sds((192, slots), BF), VM), (sds((leaf, 256), BF), VM), (sds((112, 256), BF), VM)],
        [
            pltpu.VMEM(panels.shape, BF),
            pltpu.VMEM((leaf, leaf), BF),
            pltpu.VMEM(sep_inv.shape[2:], BF),
            pltpu.VMEM(span.shape, BF),
            pltpu.VMEM(sep_rhs.shape[2:], BF),
            DMA((5,)),
        ],
        flops=2 * 192 * leaf * (leaf + slots),
        nbytes=2 * leaf * leaf + 2 * 192 * slots + 2 * 256 * leaf,
    )(
        place,
        leaf_rows[0, 0][:, None, :],
        sep_rows[0, 0][:, None, :],
        panels,
        inv,
        sep_inv[0, 0],
        span,
        sep_rhs[0, 0],
    )
    team = ("peer", "front")
    (chunks,) = call(
        push_kernel,
        "push_updates",
        [VM, VM, VM],
        [(sds((TEAM, 64, 256), BF), VM)],
        flops=2 * 192 * slots * width,
        nbytes=2 * slots * (192 + width) + TEAM * 64 * 512,
    )(recv, push, side)
    got = lax.all_to_all(chunks, team, split_axis=0, concat_axis=0, tiled=True)

    (bare,) = call(
        leaf_kernel,
        "leaf_solve",
        [VM, VM, HB],
        [(sds((leaf, width), F32), VM)],
        [pltpu.VMEM((leaf, leaf), BF), DMA],
        flops=2 * leaf * width * (2 * leaf + slots),
        nbytes=2 * leaf * leaf + 6 * slots * width,
    )(place, recv, inv)

    square = pltpu.VMEM((256, 256), BF)
    (solved,) = call(
        tree_kernel,
        "separator_tree",
        [VM, pl.BlockSpec(memory_space=pl.ANY)],
        [(sds((TEAM, SUB, 256), BF), VM)],
        [square] * 6 + [pltpu.VMEM((12, 256, 256), BF)],
        flops=2 * 16 * 256 * 256 * 36 + 2 * 48 * 16 * 64 * 256,
        nbytes=TEAM * 80 * 512,
    )(got, bare)
    back_got = lax.all_to_all(solved, team, split_axis=0, concat_axis=0, tiled=True)

    leaf_solution, sep_solution = call(
        finish_kernel,
        "finish",
        [VM, VM, VM],
        [(sds((leaf, width), F32), VM), (sds((3, SUB, width), BF), VM)],
        flops=2 * leaf * 256 * width,
        nbytes=leaf * width * 8 + leaf * 512 + TEAM * SUB * 512,
    )(back_got, back, bare)
    return leaf_solution[None, None], sep_solution[None, None]


def solution(mesh):
    leaves, fronts = mesh.shape["leaf"], mesh.shape["front"]
    grid = Mesh(
        np.asarray(mesh.devices).reshape(leaves // TREE, TREE, fronts), ("tree", "peer", "front")
    )
    leaf = ("tree", "peer")
    in_specs = (
        P(leaf, "front", None, None),
        P(leaf, "front", None),
        P(leaf, "front", None),
        P(leaf, "front", None, None, None),
        P(leaf, "front", None, None),
        P(leaf, "front", None, None, None),
        P(leaf, "front", None, None),
        P(leaf, "front", None, None),
        P(leaf, "front", None, None, None),
        P(leaf, "front", None, None),
    )
    out_specs = (P(leaf, "front", None, None), P(leaf, "front", None, None, None))
    return jax.shard_map(
        on_device, mesh=grid, in_specs=in_specs, out_specs=out_specs, check_vma=False
    )
```

time: 64.8 us -> 62.1 us (0.958)
  Pallas kernels: 18.5 us -> 16.9 us
  local copies, waits for them, and re-layouts: 4.78 us -> 3.76 us
  blocking collectives: 10.6 us -> 9.61 us
  waiting for transfers between devices: 12 us -> 12.9 us
    all_to_all x1, waiting for transfers between devices: 7.3 us -> 9.84 us  [on_device(): lax.all_to_all(sent.reshape(owners, pad, width), ('tree', 'peer'), split_...]
    pallas_call x3, Pallas kernels: 7.97 us -> 5.57 us  [the longest x1 2.99 us: on_device(): call(factor_kernel, 'factor_products', [VM, VM, VM, HB, HB, HB, HB, HB],...]
    all_to_all x1, waiting for transfers between devices: 4.67 us -> 3.11 us  [on_device(): got = lax.all_to_all(chunks, team, split_axis=0, concat_axis=0, tiled=True)]
    unnamed x23 -> x18, local copies, waits for them, and re-layouts: 4.55 us -> 3.53 us
    all_to_all x1, blocking collectives: 10.6 us -> 9.61 us  [on_device(): lax.all_to_all(solved, team, split_axis=0, concat_axis=0, tiled=True)]
    pallas_call x1, Pallas kernels: 2.19 us -> 3 us  [on_device(): call(tree_kernel, 'separator_tree', [VM, pl.BlockSpec(memory_space=pl.ANY...]
  transfers between devices with their start and end apart: 2 -> 2, of which waited for: 2 -> 2; matrix products, arithmetic and copies ran while one was open for 1% -> 0% of each run, Pallas kernels for 15% -> 13%
where the time goes in v3:
time: 62.1 us; the launch traced here: 61.7 us
  starting transfers between devices  17.6 us (28%)
  Pallas kernels  16.9 us (27%)
  waiting for transfers between devices  12.9 us (21%)
  blocking collectives  9.61 us (15%)
  local copies, waits for them, and re-layouts  3.76 us (6%)
  between operations  0.8 us (1%)
    all_to_all x1, starting transfers between devices, on_device(): lax.all_to_all(sent.reshape(owners, pad, width), ('tree', 'peer'), split_...  12.1 us
    all_to_all x1, waiting for transfers between devices, on_device(): lax.all_to_all(sent.reshape(owners, pad, width), ('tree', 'peer'), split_...  9.84 us
    all_to_all x1, blocking collectives, on_device(): lax.all_to_all(solved, team, split_axis=0, concat_axis=0, tiled=True)  9.61 us
    all_to_all x1, starting transfers between devices, on_device(): got = lax.all_to_all(chunks, team, split_axis=0, concat_axis=0, tiled=True)  5.52 us
    pallas_call x1, Pallas kernels, on_device(): call(leaf_kernel, 'leaf_solve', [VM, VM, HB], [(sds((leaf, width), F32),...  5.12 us
    unnamed x18, local copies, waits for them, and re-layouts  3.53 us
    pallas_call x1, Pallas kernels, on_device(): call(lambda *refs: send_kernel(keep, pad, *refs), 'send_rows', [HB, HB],...  3.23 us
    all_to_all x1, waiting for transfers between devices, on_device(): got = lax.all_to_all(chunks, team, split_axis=0, concat_axis=0, tiled=True)  3.11 us
  transfers between devices with their start and end apart: 2, of which 2 were waited for; matrix products, arithmetic and copies ran while one was open for 0% of the time, Pallas kernels for 13%

profile of v3, /device:TPU:1, one launch (start us, length us, event | category | flops | bytes accessed | tf_op | source)
XLA Modules:
  0.0 61.7 jit_solution(16614534088409242669)
XLA Ops:
  0.6 3.2 %send_rows.1 = bf16[1536,256]{1,0:T(8,128)(2,1)} custom-call(s32[1,1152]{1,0:T(1,128)} %bitcast.29, bf16[1152,256]{1,0:T(8,128)(2,1)} %bitcast.27), custom_call_target="tpu_custom_call" | custom-call | flops 679477248 | bytes 1179648 | tf_op jit(solution)/shard_map/send_rows/pallas_call | solution.py:286
  3.9 0.0 copy-start.8
  3.9 0.0 copy-start.2
  3.9 0.0 copy-start.3
  3.9 0.0 copy-start.4
  3.9 0.0 copy-start.5
  3.9 0.0 copy-start.6
  3.9 0.0 copy-start.7
  4.0 12.1 %all-to-all-start = ((bf16[64,24,256]{2,1,0:T(8,128)(2,1)}), bf16[64,24,256]{2,1,0:T(8,128)(2,1)S(1)}, u32[]{:S(2)}, u32[]{:S(2)}) async-start(bf16[64,24,256]{2,1,0:T(8,128)(2,1)} %bitcast.25), calls=%async_computation | async-start | bytes 1572864 | tf_op jit(solution)/shard_map/all_to_all | solution.py:302
  16.1 0.0 copy-done.8
  16.1 0.1 reshape_squeeze.6
  16.2 0.1 reshape.15.place_ref
  16.3 0.0 copy-done.2
  16.4 0.0 copy-done.3
  16.4 0.0 copy-done.4
  16.4 0.0 copy-done.5
  16.4 0.0 copy-done.6
  16.4 0.0 copy-done.7
  16.4 0.0 copy-start
  16.4 1.7 %copy-done = bf16[1,1,1152,1152]{3,2,1,0:T(8,128)(2,1)S(1)} copy-done((bf16[1,1,1152,1152]{3,2,1,0:T(8,128)(2,1)S(1)}, bf16[1,1,1152,1152]{3,2,1,0:T(8,128)(2,1)}, u32[]{:S(2)}) %copy-start) | copy-done | bytes 2654232
  18.2 3.0 %factor_products.1 = (bf16[192,1536]{1,0:T(8,128)(2,1)S(1)}, bf16[1152,256]{1,0:T(8,128)(2,1)S(1)}, bf16[112,256]{1,0:T(8,128)(2,1)S(1)}) custom-call(s32[1,1536]{1,0:T(1,128)S(1)} %reshape.15.place_ref, s32[3,1,64]{2,1,0:T(1,128)S(1)} %bitcast.23, s32[3,1,64]{2,1,0:T(1,128)S(1)} %bitcast.24, bf16[192,1152]{1,0:T(8,128)(2,1)S(1)} %bitcast.19, ...), custom_call_target="tpu_custom_call" | custom-call | flops 1189085184 | bytes 3833856 | tf_op jit(solution)/shard_map/factor_products/pallas_call | solution.py:310
  21.2 9.8 %all-to-all-done = bf16[64,24,256]{2,1,0:T(8,128)(2,1)S(1)} async-done(((bf16[64,24,256]{2,1,0:T(8,128)(2,1)}), bf16[64,24,256]{2,1,0:T(8,128)(2,1)S(1)}, u32[]{:S(2)}, u32[]{:S(2)}) %all-to-all-start) | async-done | bytes 786464 | tf_op jit(solution)/shard_map/all_to_all | solution.py:302
  31.0 1.2 %push_updates.1 = bf16[16,64,256]{2,1,0:T(8,128)(2,1)} custom-call(bf16[1536,256]{1,0:T(8,128)(2,1)S(1)} %bitcast.15, bf16[192,1536]{1,0:T(8,128)(2,1)S(1)} %get-tuple-element.7.push_ref, bf16[112,256]{1,0:T(8,128)(2,1)S(1)} %get-tuple-element.8.side_ref), custom_call_target="tpu_custom_call" | custom-call | flops 150994944 | bytes 1900544 | tf_op jit(solution)/shard_map/push_updates/pallas_call | solution.py:336
  32.2 5.5 %all-to-all-start.1 = ((bf16[16,64,256]{2,1,0:T(8,128)(2,1)}), bf16[16,64,256]{2,1,0:T(8,128)(2,1)S(1)}, u32[]{:S(2)}, u32[]{:S(2)}) async-start(bf16[16,64,256]{2,1,0:T(8,128)(2,1)} %push_updates.1), calls=%async_computation.1 | async-start | bytes 1048576 | tf_op jit(solution)/shard_map/all_to_all | solution.py:344
  37.7 0.0 copy-start.1
  37.7 1.7 %copy-done.1 = bf16[1,1,1152,1152]{3,2,1,0:T(8,128)(2,1)S(1)} copy-done((bf16[1,1,1152,1152]{3,2,1,0:T(8,128)(2,1)S(1)}, bf16[1,1,1152,1152]{3,2,1,0:T(8,128)(2,1)}, u32[]{:S(2)}) %copy-start.1) | copy-done | bytes 2654232
  39.5 5.1 %leaf_solve.1.bare_hbm.leaf_ref = f32[1152,256]{1,0:T(8,128)S(1)} custom-call(s32[1,1536]{1,0:T(1,128)S(1)} %reshape.15.place_ref, bf16[1536,256]{1,0:T(8,128)(2,1)S(1)} %bitcast.16, bf16[1152,1152]{1,0:T(8,128)(2,1)S(1)} %bitcast.18), custom_call_target="tpu_custom_call" | custom-call | flops 2264924160 | bytes 5013504 | tf_op jit(solution)/shard_map/leaf_solve/pallas_call | solution.py:346
  44.6 3.1 %all-to-all-done.1.got_ref = bf16[16,64,256]{2,1,0:T(8,128)(2,1)S(1)} async-done(((bf16[16,64,256]{2,1,0:T(8,128)(2,1)}), bf16[16,64,256]{2,1,0:T(8,128)(2,1)S(1)}, u32[]{:S(2)}, u32[]{:S(2)}) %all-to-all-start.1) | async-done | bytes 524320 | tf_op jit(solution)/shard_map/all_to_all | solution.py:344
  47.7 3.0 %separator_tree.1 = bf16[16,16,256]{2,1,0:T(8,128)(2,1)S(1)} custom-call(bf16[16,64,256]{2,1,0:T(8,128)(2,1)S(1)} %all-to-all-done.1.got_ref, f32[1152,256]{1,0:T(8,128)S(1)} %leaf_solve.1.bare_hbm.leaf_ref), custom_call_target="tpu_custom_call" | custom-call | flops 100663296 | bytes 655360 | tf_op jit(solution)/shard_map/separator_tree/pallas_call | solution.py:357
  50.7 9.6 %all_to_all.15.got_ref = bf16[16,16,256]{2,1,0:T(8,128)(2,1)S(1)} all-to-all(bf16[16,16,256]{2,1,0:T(8,128)(2,1)S(1)} %separator_tree.1), channel_id=1, replica_groups=mesh['tree'=8,'peer'=8,'front'=2] {'peer','front'}, dimensions={0} | all-to-all | bytes 262144 | tf_op jit(solution)/shard_map/all_to_all | solution.py:366
  60.3 1.4 %finish.1 = (f32[1152,256]{1,0:T(8,128)}, bf16[3,16,256]{2,1,0:T(8,128)(2,1)}) custom-call(bf16[16,16,256]{2,1,0:T(8,128)(2,1)S(1)} %all_to_all.15.got_ref, bf16[1152,256]{1,0:T(8,128)(2,1)S(1)} %get-tuple-element.9.back_ref, f32[1152,256]{1,0:T(8,128)S(1)} %leaf_solve.1.bare_hbm.leaf_ref), custom_call_target="tpu_custom_call" | custom-call | flops 150994944 | bytes 3080192 | tf_op jit(solution)/shard_map/finish/pallas_call | solution.py:368
  (2 shorter events, 0.0 us)
Async XLA Ops:
  3.9 12.2 %copy-start.8 = (s32[1,1,1152]{2,1,0:T(1,128)S(1)}, s32[1,1,1152]{2,1,0:T(1,128)}, u32[]{:S(2)}) copy-start(s32[1,1,1152]{2,1,0:T(1,128)} %param.12) | copy-start | bytes 13828
  3.9 12.5 %copy-start.2 = (bf16[1,1,3,64,1152]{4,3,2,1,0:T(8,128)(2,1)S(1)}, bf16[1,1,3,64,1152]{4,3,2,1,0:T(8,128)(2,1)}, u32[]{:S(2)}) copy-start(bf16[1,1,3,64,1152]{4,3,2,1,0:T(8,128)(2,1)} %param.15) | copy-start | bytes 1327108
  3.9 12.5 %copy-start.3 = (bf16[1,1,3,16,256]{4,3,2,1,0:T(8,128)(2,1)S(1)}, bf16[1,1,3,16,256]{4,3,2,1,0:T(8,128)(2,1)}, u32[]{:S(2)}) copy-start(bf16[1,1,3,16,256]{4,3,2,1,0:T(8,128)(2,1)} %param.13) | copy-start | bytes 73732
  3.9 12.5 %copy-start.4 = (bf16[1,1,32,224]{3,2,1,0:T(8,128)(2,1)S(1)}, bf16[1,1,32,224]{3,2,1,0:T(8,128)(2,1)}, u32[]{:S(2)}) copy-start(bf16[1,1,32,224]{3,2,1,0:T(8,128)(2,1)} %param.17) | copy-start | bytes 43012
  3.9 12.5 %copy-start.5 = (bf16[1,1,3,64,16]{3,4,2,1,0:T(8,128)(2,1)S(1)}, bf16[1,1,3,64,16]{3,4,2,1,0:T(8,128)(2,1)}, u32[]{:S(2)}) copy-start(bf16[1,1,3,64,16]{3,4,2,1,0:T(8,128)(2,1)} %param.18) | copy-start | bytes 18436
  3.9 12.5 %copy-start.6 = (s32[1,1,3,64]{3,1,2,0:T(1,128)S(1)}, s32[1,1,3,64]{3,1,2,0:T(1,128)}, u32[]{:S(2)}) copy-start(s32[1,1,3,64]{3,1,2,0:T(1,128)} %param.16) | copy-start | bytes 2308
  3.9 12.5 %copy-start.7 = (s32[1,1,3,64]{3,1,2,0:T(1,128)S(1)}, s32[1,1,3,64]{3,1,2,0:T(1,128)}, u32[]{:S(2)}) copy-start(s32[1,1,3,64]{3,1,2,0:T(1,128)} %param.19) | copy-start | bytes 2308
  4.0 27.0 %all-to-all-start = ((bf16[64,24,256]{2,1,0:T(8,128)(2,1)}), bf16[64,24,256]{2,1,0:T(8,128)(2,1)S(1)}, u32[]{:S(2)}, u32[]{:S(2)}) async-start(bf16[64,24,256]{2,1,0:T(8,128)(2,1)} %bitcast.25), calls=%async_computation | async-start | bytes 1572864 | tf_op jit(solution)/shard_map/all_to_all | solution.py:302
  16.4 1.8 %copy-start = (bf16[1,1,1152,1152]{3,2,1,0:T(8,128)(2,1)S(1)}, bf16[1,1,1152,1152]{3,2,1,0:T(8,128)(2,1)}, u32[]{:S(2)}) copy-start(bf16[1,1,1152,1152]{3,2,1,0:T(8,128)(2,1)} %param.14) | copy-start | bytes 7962628
  32.2 15.5 %all-to-all-start.1 = ((bf16[16,64,256]{2,1,0:T(8,128)(2,1)}), bf16[16,64,256]{2,1,0:T(8,128)(2,1)S(1)}, u32[]{:S(2)}, u32[]{:S(2)}) async-start(bf16[16,64,256]{2,1,0:T(8,128)(2,1)} %push_updates.1), calls=%async_computation.1 | async-start | bytes 1048576 | tf_op jit(solution)/shard_map/all_to_all | solution.py:344
  37.7 1.7 %copy-start.1 = (bf16[1,1,1152,1152]{3,2,1,0:T(8,128)(2,1)S(1)}, bf16[1,1,1152,1152]{3,2,1,0:T(8,128)(2,1)}, u32[]{:S(2)}) copy-start(bf16[1,1,1152,1152]{3,2,1,0:T(8,128)(2,1)} %param.14) | copy-start | bytes 7962628

commit v4 on v3

--- a/solution.py
+++ b/solution.py
@@ -10,7 +10,7 @@
 F32 = jnp.float32
 SUB = 16
 TREE = 8
-TEAM = 16
+COLS = 32
 VMEM_CAP = 40 * 1024 * 1024
 VMEM_ALL = 62 * 1024 * 1024
 
@@ -110,7 +110,9 @@
     spread = hot(row_ids(leaf, slots) == place_ref[...])
     for move in moves:
         move.wait()
-    product = dot(panels_ref[...], inv_ref[...])
+    cuts = [(low, min(low + 256, leaf)) for low in range(0, leaf, 256)]
+    product = [dot(panels_ref[:, low:], inv_ref[low:, low:high]) for low, high in cuts]
+    product = jnp.concatenate(product, axis=1)
     push_ref[...] = dot(product.astype(BF), spread).astype(BF)
     padded = jnp.concatenate([product, jnp.zeros((256 - product.shape[0], leaf), F32)], axis=0)
     back_ref[...] = padded.T.astype(BF)
@@ -135,9 +137,9 @@
     rows = jnp.concatenate([sums, side_ref[48:112, :].astype(F32)], axis=0)
     turned = rows.T.astype(BF)
     meta = side_ref[0:48, :]
-    for member in range(TEAM):
-        out_ref[member, 0:16, :] = turned[member * SUB : (member + 1) * SUB, :]
-        out_ref[member, 16:64, :] = meta
+    for peer in range(TREE):
+        out_ref[peer, 0:32, :] = turned[peer * COLS : (peer + 1) * COLS, :]
+        out_ref[peer, 32:80, :] = meta
 
 
 def leaf_kernel(place_ref, recv_ref, inv_hbm, out_ref, inv_ref, sem):
@@ -147,9 +149,11 @@
     spread = hot(row_ids(leaf, slots) == place_ref[...])
     owned = dot(spread, recv_ref[...]).T.astype(BF)
     inv_in.wait()
-    inv = inv_ref[...]
-    y_t = dot(owned, inv, NT).astype(BF)
-    out_ref[...] = dot(y_t, inv).T
+    cuts = [(low, min(low + 256, leaf)) for low in range(0, leaf, 256)]
+    y_t = [dot(owned[:, :high], inv_ref[low:high, :high], NT) for low, high in cuts]
+    y_t = jnp.concatenate(y_t, axis=1).astype(BF)
+    bare_t = [dot(y_t[:, low:], inv_ref[low:, low:high]) for low, high in cuts]
+    out_ref[...] = jnp.concatenate(bare_t, axis=1).T
 
 
 def turn(value, shift):
@@ -157,66 +161,85 @@
     return pltpu.roll(value, shift, 1) if shift else value
 
 
-def tree_kernel(got_ref, bare_hbm, out_ref, e0_ref, e1_ref, e2_ref, a01_ref, a02_ref, a12_ref, spots_ref):
+def tree_kernel(
+    front_ref, got_ref, other_ref, bare_hbm, out_ref,
+    e0_ref, e1_ref, e2_ref, a01_ref, a02_ref, a12_ref, spots_ref,
+):
+    front = front_ref[0]
+    first = front == 0
+    sides = (got_ref, other_ref)
     lane = lane_ids(32, 128)
     none = jnp.zeros((32, 128), BF)
     for peer in range(TREE):
         rows = slice(peer * 32, (peer + 1) * 32)
-        low0 = jnp.zeros((32, 128), F32)
-        low1 = jnp.zeros((32, 128), F32)
-        for front in range(2):
-            src = peer * 2 + front
-            e2_ref[rows, front * 128 : (front + 1) * 128] = got_ref[src, 16:48, 0:128]
-            rest = got_ref[src, 16:48, 128:256].astype(F32)
-            one = jnp.where(lane < 64, rest, 0.0)
-            zero = jnp.where((lane >= 64) & (lane < 96), rest, 0.0)
-            low1 = low1 + turn(one, front * 64)
-            low0 = low0 + turn(zero, ((peer // 2) % 2) * 64 + front * 32 - 64)
+        mine = got_ref[peer, 32:64, :].astype(F32)
+        theirs = other_ref[peer, 32:64, :].astype(F32)
+        left = jnp.where(first, mine, theirs)
+        right = jnp.where(first, theirs, mine)
+        e2_ref[rows, 0:128] = left[:, 0:128].astype(BF)
+        e2_ref[rows, 128:256] = right[:, 0:128].astype(BF)
+        left, right = left[:, 128:256], right[:, 128:256]
+        low1 = jnp.where(lane < 64, left, turn(right, 64))
+        inside = (lane >= 64) & (lane < 96)
+        to = ((peer // 2) % 2) * 64
+        low0 = turn(jnp.where(inside, left, 0.0), to - 64)
+        low0 = low0 + turn(jnp.where(inside, right, 0.0), to + 32 - 64)
         tile = peer // 4
         for ref, low in ((e1_ref, low1), (e0_ref, low0)):
             ref[rows, tile * 128 : (tile + 1) * 128] = low.astype(BF)
             ref[rows, (1 - tile) * 128 : (2 - tile) * 128] = none
     sub = row_ids(256, 64)
-    for src in range(TEAM):
-        for pair, ref in enumerate((a01_ref, a02_ref, a12_ref)):
-            where = got_ref[src, 48 + pair : 49 + pair, 192:256].astype(F32).astype(jnp.int32)
-            if pair == 0:
-                where = where + src // 8 * 128
-            flipped = got_ref[src, 48:64, pair * 64 : (pair + 1) * 64]
-            ref[src * SUB : (src + 1) * SUB, :] = dot(flipped, hot(sub == where), NT).astype(BF)
+    for side, table in enumerate(sides):
+        for peer in range(TREE):
+            at = peer * 2 * SUB + (front ^ side) * SUB
+            rows = pl.ds(pl.multiple_of(at, SUB), SUB)
+            for pair, ref in enumerate((a01_ref, a02_ref, a12_ref)):
+                where = table[peer, 64 + pair : 65 + pair, 192:256].astype(F32).astype(jnp.int32)
+                if pair == 0:
+                    where = where + peer // 4 * 128
+                flipped = table[peer, 64:80, pair * 64 : (pair + 1) * 64]
+                ref[rows, :] = dot(flipped, hot(sub == where), NT).astype(BF)
     wide = row_ids(256, 256)
     for level in range(3):
         for quad in range(4):
             parts = []
-            for src in range(quad * 4, quad * 4 + 4):
-                where = got_ref[src, 51 + level : 52 + level, 192:256].astype(F32)
-                parts.append(where + (src // 4 * 64, src // 8 * 128, 0)[level])
+            for peer in range(quad % 2 * 4, quad % 2 * 4 + 4):
+                where = sides[quad // 2][peer, 67 + level : 68 + level, 192:256].astype(F32)
+                parts.append(where + (peer // 2 * 64, peer // 4 * 128, 0)[level])
             where = jnp.concatenate(parts, axis=1).astype(jnp.int32)
             spots_ref[level * 4 + quad] = hot(wide == where)
-    lane = lane_ids(SUB, 128)
-    first = lane < 64
+    lane = lane_ids(COLS, 128)
+    half = lane < 64
     sums = []
     for level in range(3):
+        begin = 64 + level * SUB
+        inside = (lane >= begin) & (lane < begin + SUB)
         tiles = []
         for tile in range(2):
-            total = jnp.zeros((SUB, 128), F32)
-            for at in range(8):
-                piece = got_ref[tile * 8 + at, 0:16, 128:256].astype(F32)
-                begin = 64 + level * SUB
-                piece = jnp.where((lane >= begin) & (lane < begin + SUB), piece, 0.0)
-                total = total + turn(piece, at * SUB - begin)
-            tiles.append(total)
+            totals = []
+            for table in sides:
+                total = jnp.zeros((COLS, 128), F32)
+                for at in range(4):
+                    piece = table[tile * 4 + at, 0:32, 128:256].astype(F32)
+                    total = total + turn(jnp.where(inside, piece, 0.0), at * 32 - begin)
+                totals.append(total)
+            mine, theirs = totals
+            left = jnp.where(first, mine, theirs)
+            right = jnp.where(first, theirs, mine)
+            tiles.append(left + turn(right, SUB))
         rest = jnp.concatenate(tiles, axis=1)
         tile = slice(level // 2 * 128, level // 2 * 128 + 128)
         for quad in range(4):
+            table = sides[quad // 2]
             halves = []
             for pair in range(2):
-                left = got_ref[quad * 4 + pair * 2, 0:16, tile].astype(F32)
-                right = got_ref[quad * 4 + pair * 2 + 1, 0:16, tile].astype(F32)
+                peer = quad % 2 * 4 + pair * 2
+                left = table[peer, 0:32, tile].astype(F32)
+                right = table[peer + 1, 0:32, tile].astype(F32)
                 if level == 1:
-                    halves.append(jnp.where(first, turn(left, 64), right))
+                    halves.append(jnp.where(half, turn(left, 64), right))
                 else:
-                    halves.append(jnp.where(first, left, turn(right, 64)))
+                    halves.append(jnp.where(half, left, turn(right, 64)))
             moved = jnp.concatenate(halves, axis=1).astype(BF)
             rest = rest - dot(moved, spots_ref[level * 4 + quad], NT)
         sums.append(rest)
@@ -232,24 +255,28 @@
     x1 = dot((y1 - dot(x2, a12, NT)).astype(BF), e1).astype(BF)
     x0 = dot((y0 - dot(x2, a02, NT) - dot(x1, a01, NT)).astype(BF), e0).astype(BF)
     solved = (x0, x1, x2)
-    for quad in range(4):
+    own = []
+    for level in range(3):
+        for tile in range(2):
+            piece = solved[level][:, tile * 128 : (tile + 1) * 128].astype(F32)
+            own.append(jnp.where(first, piece, turn(piece, -SUB)))
+    for quad in range(2):
         picks = [dot(solved[level], spots_ref[level * 4 + quad]) for level in range(3)]
         for at in range(4):
-            dst = quad * 4 + at
-            half = slice(at // 2 * 128, at // 2 * 128 + 128)
-            p0, p1, p2 = [pick[:, half] for pick in picks]
+            peer = quad * 4 + at
+            part = slice(at // 2 * 128, at // 2 * 128 + 128)
+            p0, p1, p2 = [pick[:, part] for pick in picks]
             if at % 2:
                 p0, p2 = turn(p0, 64), turn(p2, 64)
             else:
                 p1 = turn(p1, 64)
-            out_ref[dst, :, 0:128] = jnp.where(first, p0, p1).astype(BF)
-            rest = jnp.where(first, p2, 0.0)
-            tile = slice(dst // 8 * 128, dst // 8 * 128 + 128)
+            out_ref[peer, :, 0:128] = jnp.where(half, p0, p1).astype(BF)
+            rest = jnp.where(half, p2, 0.0)
             for level in range(3):
                 begin = 64 + level * SUB
-                piece = turn(solved[level][:, tile].astype(F32), begin - dst % 8 * SUB)
+                piece = turn(own[level * 2 + quad], begin - at * 32)
                 rest = jnp.where((lane >= begin) & (lane < begin + SUB), piece, rest)
-            out_ref[dst, :, 128:256] = rest.astype(BF)
+            out_ref[peer, :, 128:256] = rest.astype(BF)
 
 
 def finish_kernel(got_ref, back_ref, leaf_ref, out_ref, sep_ref):
@@ -332,17 +359,15 @@
         span,
         sep_rhs[0, 0],
     )
-    team = ("peer", "front")
     (chunks,) = call(
         push_kernel,
         "push_updates",
         [VM, VM, VM],
-        [(sds((TEAM, 64, 256), BF), VM)],
+        [(sds((TREE, 80, 256), BF), VM)],
         flops=2 * 192 * slots * width,
-        nbytes=2 * slots * (192 + width) + TEAM * 64 * 512,
+        nbytes=2 * slots * (192 + width) + TREE * 80 * 512,
     )(recv, push, side)
-    got = lax.all_to_all(chunks, team, split_axis=0, concat_axis=0, tiled=True)
-
+    got = lax.all_to_all(chunks, "peer", split_axis=0, concat_axis=0, tiled=True)
     (bare,) = call(
         leaf_kernel,
         "leaf_solve",
@@ -353,17 +378,20 @@
         nbytes=2 * leaf * leaf + 6 * slots * width,
     )(place, recv, inv)
 
+    got, bare = lax.optimization_barrier((got, bare))
+    other = lax.ppermute(got, "front", [(0, 1), (1, 0)])
+    front = lax.axis_index("front").astype(jnp.int32).reshape(1)
     square = pltpu.VMEM((256, 256), BF)
     (solved,) = call(
         tree_kernel,
         "separator_tree",
-        [VM, pl.BlockSpec(memory_space=pl.ANY)],
-        [(sds((TEAM, SUB, 256), BF), VM)],
+        [SM, VM, VM, pl.BlockSpec(memory_space=pl.ANY)],
+        [(sds((TREE, COLS, 256), BF), VM)],
         [square] * 6 + [pltpu.VMEM((12, 256, 256), BF)],
-        flops=2 * 16 * 256 * 256 * 36 + 2 * 48 * 16 * 64 * 256,
-        nbytes=TEAM * 80 * 512,
-    )(got, bare)
-    back_got = lax.all_to_all(solved, team, split_axis=0, concat_axis=0, tiled=True)
+        flops=2 * 32 * 256 * 256 * 30 + 2 * 48 * 16 * 64 * 256,
+        nbytes=TREE * 192 * 512,
+    )(front, got, other, bare)
+    back_got = lax.all_to_all(solved, "peer", split_axis=0, concat_axis=0, tiled=True)
 
     leaf_solution, sep_solution = call(
         finish_kernel,
@@ -371,7 +399,7 @@
         [VM, VM, VM],
         [(sds((leaf, width), F32), VM), (sds((3, SUB, width), BF), VM)],
         flops=2 * leaf * 256 * width,
-        nbytes=leaf * width * 8 + leaf * 512 + TEAM * SUB * 512,
+        nbytes=leaf * width * 8 + leaf * 512 + TREE * COLS * 512,
     )(back_got, back, bare)
     return leaf_solution[None, None], sep_solution[None, None]
 

time: 62.1 us -> 60.9 us (0.981)
  waiting for transfers between devices: 12.9 us -> 11.7 us
  Pallas kernels: 16.9 us -> 15.7 us
  starting transfers between devices: 17.6 us -> 18.8 us
    ppermute x0 -> x1, starting transfers between devices: none -> 3.26 us  [on_device(): other = lax.ppermute(got, 'front', [(0, 1), (1, 0)])]
    all_to_all x1, waiting for transfers between devices: 3.11 us -> 0.37 us  [on_device(): lax.all_to_all(chunks, 'peer', split_axis=0, concat_axis=0, tiled=True)]
    all_to_all x1, starting transfers between devices: 5.52 us -> 3.43 us  [on_device(): lax.all_to_all(chunks, 'peer', split_axis=0, concat_axis=0, tiled=True)]
    ppermute x0 -> x1, waiting for transfers between devices: none -> 1.26 us  [on_device(): other = lax.ppermute(got, 'front', [(0, 1), (1, 0)])]
    pallas_call x1, Pallas kernels: 5.12 us -> 4.34 us  [on_device(): call(leaf_kernel, 'leaf_solve', [VM, VM, HB], [(sds((leaf, width), F32),...]
  transfers between devices with their start and end apart: 2 -> 3, of which waited for: 2 -> 3; matrix products, arithmetic and copies ran while one was open for 0% -> 0% of each run, Pallas kernels for 13% -> 12%
where the time goes in v4:
time: 60.9 us; the launch traced here: 60.1 us
  starting transfers between devices  18.8 us (31%)
  Pallas kernels  15.7 us (26%)
  waiting for transfers between devices  11.7 us (19%)
  blocking collectives  9.2 us (15%)
  local copies, waits for them, and re-layouts  3.76 us (6%)
  between operations  0.82 us (1%)
    all_to_all x1, starting transfers between devices, on_device(): lax.all_to_all(sent.reshape(owners, pad, width), ('tree', 'peer'), split_...  12.1 us
    all_to_all x1, waiting for transfers between devices, on_device(): lax.all_to_all(sent.reshape(owners, pad, width), ('tree', 'peer'), split_...  10.1 us
    all_to_all x1, blocking collectives, on_device(): lax.all_to_all(solved, 'peer', split_axis=0, concat_axis=0, tiled=True)  9.2 us
    pallas_call x1, Pallas kernels, on_device(): call(leaf_kernel, 'leaf_solve', [VM, VM, HB], [(sds((leaf, width), F32),...  4.34 us
    unnamed x18, local copies, waits for them, and re-layouts  3.53 us
    all_to_all x1, starting transfers between devices, on_device(): lax.all_to_all(chunks, 'peer', split_axis=0, concat_axis=0, tiled=True)  3.43 us
    ppermute x1, starting transfers between devices, on_device(): other = lax.ppermute(got, 'front', [(0, 1), (1, 0)])  3.26 us
    pallas_call x1, Pallas kernels, on_device(): call(lambda *refs: send_kernel(keep, pad, *refs), 'send_rows', [HB, HB],...  3.23 us
  transfers between devices with their start and end apart: 3, of which 3 were waited for; matrix products, arithmetic and copies ran while one was open for 0% of the time, Pallas kernels for 12%

profile of v4, /device:TPU:1, one launch (start us, length us, event | category | flops | bytes accessed | tf_op | source)
XLA Modules:
  0.0 60.1 jit_solution(7237726189438345320)
XLA Ops:
  0.6 3.2 %send_rows.1 = bf16[1536,256]{1,0:T(8,128)(2,1)} custom-call(s32[1,1152]{1,0:T(1,128)} %bitcast.30, bf16[1152,256]{1,0:T(8,128)(2,1)} %bitcast.28), custom_call_target="tpu_custom_call" | custom-call | flops 679477248 | bytes 1179648 | tf_op jit(solution)/shard_map/send_rows/pallas_call | solution.py:313
  3.9 0.0 copy-start.8
  3.9 0.0 copy-start.2
  3.9 0.0 copy-start.3
  3.9 0.0 copy-start.4
  3.9 0.0 copy-start.5
  3.9 0.0 copy-start.6
  3.9 0.0 copy-start.7
  4.0 12.1 %all-to-all-start = ((bf16[64,24,256]{2,1,0:T(8,128)(2,1)}), bf16[64,24,256]{2,1,0:T(8,128)(2,1)S(1)}, u32[]{:S(2)}, u32[]{:S(2)}) async-start(bf16[64,24,256]{2,1,0:T(8,128)(2,1)} %bitcast.26), calls=%async_computation | async-start | bytes 1572864 | tf_op jit(solution)/shard_map/all_to_all | solution.py:329
  16.1 0.0 copy-done.8
  16.1 0.1 reshape_squeeze.6
  16.2 0.1 reshape.19.place_ref
  16.3 0.0 copy-done.2
  16.4 0.0 copy-done.3
  16.4 0.0 copy-done.4
  16.4 0.0 copy-done.5
  16.4 0.0 copy-done.6
  16.4 0.0 copy-done.7
  16.4 0.0 copy-start
  16.4 1.7 %copy-done = bf16[1,1,1152,1152]{3,2,1,0:T(8,128)(2,1)S(1)} copy-done((bf16[1,1,1152,1152]{3,2,1,0:T(8,128)(2,1)S(1)}, bf16[1,1,1152,1152]{3,2,1,0:T(8,128)(2,1)}, u32[]{:S(2)}) %copy-start) | copy-done | bytes 2654232
  18.2 2.7 %factor_products.1 = (bf16[192,1536]{1,0:T(8,128)(2,1)S(1)}, bf16[1152,256]{1,0:T(8,128)(2,1)S(1)}, bf16[112,256]{1,0:T(8,128)(2,1)S(1)}) custom-call(s32[1,1536]{1,0:T(1,128)S(1)} %reshape.19.place_ref, s32[3,1,64]{2,1,0:T(1,128)S(1)} %bitcast.24, s32[3,1,64]{2,1,0:T(1,128)S(1)} %bitcast.25, bf16[192,1152]{1,0:T(8,128)(2,1)S(1)} %bitcast.20, ...), custom_call_target="tpu_custom_call" | custom-call | flops 1189085184 | bytes 3833856 | tf_op jit(solution)/shard_map/factor_products/pallas_call | solution.py:337
  20.9 10.1 %all-to-all-done = bf16[64,24,256]{2,1,0:T(8,128)(2,1)S(1)} async-done(((bf16[64,24,256]{2,1,0:T(8,128)(2,1)}), bf16[64,24,256]{2,1,0:T(8,128)(2,1)S(1)}, u32[]{:S(2)}, u32[]{:S(2)}) %all-to-all-start) | async-done | bytes 786464 | tf_op jit(solution)/shard_map/all_to_all | solution.py:329
  31.0 1.1 %push_updates.1 = bf16[8,80,256]{2,1,0:T(8,128)(2,1)} custom-call(bf16[1536,256]{1,0:T(8,128)(2,1)S(1)} %bitcast.16, bf16[192,1536]{1,0:T(8,128)(2,1)S(1)} %get-tuple-element.9.push_ref, bf16[112,256]{1,0:T(8,128)(2,1)S(1)} %get-tuple-element.10.side_ref), custom_call_target="tpu_custom_call" | custom-call | flops 150994944 | bytes 1703936 | tf_op jit(solution)/shard_map/push_updates/pallas_call | solution.py:362
  32.1 3.4 %all-to-all-start.1 = ((bf16[8,80,256]{2,1,0:T(8,128)(2,1)}), bf16[8,80,256]{2,1,0:T(8,128)(2,1)S(1)}, u32[]{:S(2)}, u32[]{:S(2)}) async-start(bf16[8,80,256]{2,1,0:T(8,128)(2,1)} %push_updates.1), calls=%async_computation.1 | async-start | bytes 655360 | tf_op jit(solution)/shard_map/all_to_all | solution.py:370
  35.6 0.0 copy-start.1
  35.6 1.7 %copy-done.1 = bf16[1,1,1152,1152]{3,2,1,0:T(8,128)(2,1)S(1)} copy-done((bf16[1,1,1152,1152]{3,2,1,0:T(8,128)(2,1)S(1)}, bf16[1,1,1152,1152]{3,2,1,0:T(8,128)(2,1)}, u32[]{:S(2)}) %copy-start.1) | copy-done | bytes 2654232
  37.3 4.3 %leaf_solve.1.bare_hbm.leaf_ref = f32[1152,256]{1,0:T(8,128)S(1)} custom-call(s32[1,1536]{1,0:T(1,128)S(1)} %reshape.19.place_ref, bf16[1536,256]{1,0:T(8,128)(2,1)S(1)} %bitcast.17, bf16[1152,1152]{1,0:T(8,128)(2,1)S(1)} %bitcast.19), custom_call_target="tpu_custom_call" | custom-call | flops 2264924160 | bytes 5013504 | tf_op jit(solution)/shard_map/leaf_solve/pallas_call | solution.py:371
  41.7 0.4 all-to-all-done.1.got_ref
  42.0 3.3 %collective-permute-start = (bf16[8,80,256]{2,1,0:T(8,128)(2,1)S(1)}, bf16[8,80,256]{2,1,0:T(8,128)(2,1)S(1)}, u32[]{:S(2)}, u32[]{:S(2)}) collective-permute-start(bf16[8,80,256]{2,1,0:T(8,128)(2,1)S(1)} %all-to-all-done.1.got_ref), channel_id=1, source_target_pairs={{0,1},{1,0},{2,3},{3,2},{4,5},{5,4},{6,7},{7,6},{8,9},{9,8},{10,11... | collective-permute-start | bytes 983048 | tf_op jit(solution)/shard_map/ppermute | solution.py:382
  45.3 1.3 %collective-permute-done.other_ref = bf16[8,80,256]{2,1,0:T(8,128)(2,1)S(1)} collective-permute-done((bf16[8,80,256]{2,1,0:T(8,128)(2,1)S(1)}, bf16[8,80,256]{2,1,0:T(8,128)(2,1)S(1)}, u32[]{:S(2)}, u32[]{:S(2)}) %collective-permute-start) | collective-permute-done | bytes 327712 | tf_op jit(solution)/shard_map/ppermute | solution.py:382
  46.6 2.9 %separator_tree.1 = bf16[8,32,256]{2,1,0:T(8,128)(2,1)S(1)} custom-call(s32[1]{0:T(128)} %bitcast.front_ref, bf16[8,80,256]{2,1,0:T(8,128)(2,1)S(1)} %all-to-all-done.1.got_ref, bf16[8,80,256]{2,1,0:T(8,128)(2,1)S(1)} %collective-permute-done.other_ref, f32[1152,256]{1,0:T(8,128)S(1)} %leaf_solve.1.bare_hbm.leaf_ref), custom_call_target="tpu_custom_call" | custom-call | flops 150994944 | bytes 786432 | tf_op jit(solution)/shard_map/separator_tree/pallas_call | solution.py:385
  49.5 9.2 %all_to_all.15.got_ref = bf16[8,32,256]{2,1,0:T(8,128)(2,1)S(1)} all-to-all(bf16[8,32,256]{2,1,0:T(8,128)(2,1)S(1)} %separator_tree.1), channel_id=1, replica_groups=mesh['tree'=8,'peer'=8,'front'=2] {'peer'}, dimensions={0} | all-to-all | bytes 262144 | tf_op jit(solution)/shard_map/all_to_all | solution.py:394
  58.7 1.4 %finish.1 = (f32[1152,256]{1,0:T(8,128)}, bf16[3,16,256]{2,1,0:T(8,128)(2,1)}) custom-call(bf16[8,32,256]{2,1,0:T(8,128)(2,1)S(1)} %all_to_all.15.got_ref, bf16[1152,256]{1,0:T(8,128)(2,1)S(1)} %get-tuple-element.13.back_ref, f32[1152,256]{1,0:T(8,128)S(1)} %leaf_solve.1.bare_hbm.leaf_ref), custom_call_target="tpu_custom_call" | custom-call | flops 150994944 | bytes 3080192 | tf_op jit(solution)/shard_map/finish/pallas_call | solution.py:396
  (2 shorter events, 0.0 us)
Async XLA Ops:
  3.9 12.2 %copy-start.8 = (s32[1,1,1152]{2,1,0:T(1,128)S(1)}, s32[1,1,1152]{2,1,0:T(1,128)}, u32[]{:S(2)}) copy-start(s32[1,1,1152]{2,1,0:T(1,128)} %param.12) | copy-start | bytes 13828
  3.9 12.5 %copy-start.2 = (bf16[1,1,3,64,1152]{4,3,2,1,0:T(8,128)(2,1)S(1)}, bf16[1,1,3,64,1152]{4,3,2,1,0:T(8,128)(2,1)}, u32[]{:S(2)}) copy-start(bf16[1,1,3,64,1152]{4,3,2,1,0:T(8,128)(2,1)} %param.15) | copy-start | bytes 1327108
  3.9 12.5 %copy-start.3 = (bf16[1,1,3,16,256]{4,3,2,1,0:T(8,128)(2,1)S(1)}, bf16[1,1,3,16,256]{4,3,2,1,0:T(8,128)(2,1)}, u32[]{:S(2)}) copy-start(bf16[1,1,3,16,256]{4,3,2,1,0:T(8,128)(2,1)} %param.13) | copy-start | bytes 73732
  3.9 12.5 %copy-start.4 = (bf16[1,1,32,224]{3,2,1,0:T(8,128)(2,1)S(1)}, bf16[1,1,32,224]{3,2,1,0:T(8,128)(2,1)}, u32[]{:S(2)}) copy-start(bf16[1,1,32,224]{3,2,1,0:T(8,128)(2,1)} %param.17) | copy-start | bytes 43012
  3.9 12.5 %copy-start.5 = (bf16[1,1,3,64,16]{3,4,2,1,0:T(8,128)(2,1)S(1)}, bf16[1,1,3,64,16]{3,4,2,1,0:T(8,128)(2,1)}, u32[]{:S(2)}) copy-start(bf16[1,1,3,64,16]{3,4,2,1,0:T(8,128)(2,1)} %param.18) | copy-start | bytes 18436
  3.9 12.5 %copy-start.6 = (s32[1,1,3,64]{3,1,2,0:T(1,128)S(1)}, s32[1,1,3,64]{3,1,2,0:T(1,128)}, u32[]{:S(2)}) copy-start(s32[1,1,3,64]{3,1,2,0:T(1,128)} %param.16) | copy-start | bytes 2308
  3.9 12.5 %copy-start.7 = (s32[1,1,3,64]{3,1,2,0:T(1,128)S(1)}, s32[1,1,3,64]{3,1,2,0:T(1,128)}, u32[]{:S(2)}) copy-start(s32[1,1,3,64]{3,1,2,0:T(1,128)} %param.19) | copy-start | bytes 2308
  4.0 27.0 %all-to-all-start = ((bf16[64,24,256]{2,1,0:T(8,128)(2,1)}), bf16[64,24,256]{2,1,0:T(8,128)(2,1)S(1)}, u32[]{:S(2)}, u32[]{:S(2)}) async-start(bf16[64,24,256]{2,1,0:T(8,128)(2,1)} %bitcast.26), calls=%async_computation | async-start | bytes 1572864 | tf_op jit(solution)/shard_map/all_to_all | solution.py:329
  16.4 1.8 %copy-start = (bf16[1,1,1152,1152]{3,2,1,0:T(8,128)(2,1)S(1)}, bf16[1,1,1152,1152]{3,2,1,0:T(8,128)(2,1)}, u32[]{:S(2)}) copy-start(bf16[1,1,1152,1152]{3,2,1,0:T(8,128)(2,1)} %param.14) | copy-start | bytes 7962628
  32.1 9.9 %all-to-all-start.1 = ((bf16[8,80,256]{2,1,0:T(8,128)(2,1)}), bf16[8,80,256]{2,1,0:T(8,128)(2,1)S(1)}, u32[]{:S(2)}, u32[]{:S(2)}) async-start(bf16[8,80,256]{2,1,0:T(8,128)(2,1)} %push_updates.1), calls=%async_computation.1 | async-start | bytes 655360 | tf_op jit(solution)/shard_map/all_to_all | solution.py:370
  35.6 1.8 %copy-start.1 = (bf16[1,1,1152,1152]{3,2,1,0:T(8,128)(2,1)S(1)}, bf16[1,1,1152,1152]{3,2,1,0:T(8,128)(2,1)}, u32[]{:S(2)}) copy-start(bf16[1,1,1152,1152]{3,2,1,0:T(8,128)(2,1)} %param.14) | copy-start | bytes 7962628
  42.0 4.5 %collective-permute-start = (bf16[8,80,256]{2,1,0:T(8,128)(2,1)S(1)}, bf16[8,80,256]{2,1,0:T(8,128)(2,1)S(1)}, u32[]{:S(2)}, u32[]{:S(2)}) collective-permute-start(bf16[8,80,256]{2,1,0:T(8,128)(2,1)S(1)} %all-to-all-done.1.got_ref), channel_id=1, source_target_pairs={{0,1},{1,0},{2,3},{3,2},{4,5},{5,4},{6,7},{7,6},{8,9},{9,8},{10,11... | collective-permute-start | bytes 983048 | tf_op jit(solution)/shard_map/ppermute | solution.py:382

commit v5 on v4

--- a/solution.py
+++ b/solution.py
@@ -93,25 +93,40 @@
         copy.wait()
 
 
+def column_cuts(leaf):
+    cuts, base = [], 0
+    for low in range(0, leaf, 256):
+        cuts.append((low, min(low + 256, leaf), base))
+        base += leaf - low
+    return cuts
+
+
 def factor_kernel(
-    place_ref, rows_ref, srow_ref, panels_hbm, inv_hbm, sinv_hbm, span_hbm, srhs_hbm,
-    push_ref, back_ref, side_ref, panels_ref, inv_ref, sinv_ref, span_ref, srhs_ref, sems,
+    place_ref, rows_ref, srow_ref, inv_ref, panels_hbm, sinv_hbm, span_hbm, srhs_hbm,
+    push_ref, back_ref, side_ref, packed_hbm, panels_ref, sinv_ref, span_ref, srhs_ref, sems,
 ):
     moves = [
         fetch(sinv_hbm, sinv_ref, sems.at[0]),
         fetch(span_hbm, span_ref, sems.at[1]),
         fetch(srhs_hbm, srhs_ref, sems.at[2]),
         fetch(panels_hbm, panels_ref, sems.at[3]),
-        fetch(inv_hbm, inv_ref, sems.at[4]),
     ]
     leaf = inv_ref.shape[0]
     slots = place_ref.shape[1]
     upd = rows_ref.shape[2]
+    cuts = column_cuts(leaf)
+    leaving = [
+        fetch(
+            inv_ref.at[low:leaf, low:high],
+            packed_hbm.at[base : base + leaf - low, 0 : high - low],
+            sems.at[4 + at],
+        )
+        for at, (low, high, base) in enumerate(cuts)
+    ]
     spread = hot(row_ids(leaf, slots) == place_ref[...])
     for move in moves:
         move.wait()
-    cuts = [(low, min(low + 256, leaf)) for low in range(0, leaf, 256)]
-    product = [dot(panels_ref[:, low:], inv_ref[low:, low:high]) for low, high in cuts]
+    product = [dot(panels_ref[:, low:], inv_ref[low:, low:high]) for low, high, _ in cuts]
     product = jnp.concatenate(product, axis=1)
     push_ref[...] = dot(product.astype(BF), spread).astype(BF)
     padded = jnp.concatenate([product, jnp.zeros((256 - product.shape[0], leaf), F32)], axis=0)
@@ -130,6 +145,8 @@
     for level in range(3):
         side_ref[48 + level * SUB : 64 + level * SUB, :] = srhs_ref[level]
     side_ref[96:112, :] = jnp.zeros((SUB, 256), BF)
+    for copy in leaving:
+        copy.wait()
 
 
 def push_kernel(recv_ref, push_ref, side_ref, out_ref):
@@ -142,17 +159,31 @@
         out_ref[peer, 32:80, :] = meta
 
 
-def leaf_kernel(place_ref, recv_ref, inv_hbm, out_ref, inv_ref, sem):
-    inv_in = fetch(inv_hbm, inv_ref, sem)
-    leaf = inv_ref.shape[0]
+def forward_kernel(leaf, place_ref, recv_ref, packed_ref, y_ref):
     slots = place_ref.shape[1]
     spread = hot(row_ids(leaf, slots) == place_ref[...])
     owned = dot(spread, recv_ref[...]).T.astype(BF)
-    inv_in.wait()
-    cuts = [(low, min(low + 256, leaf)) for low in range(0, leaf, 256)]
-    y_t = [dot(owned[:, :high], inv_ref[low:high, :high], NT) for low, high in cuts]
-    y_t = jnp.concatenate(y_t, axis=1).astype(BF)
-    bare_t = [dot(y_t[:, low:], inv_ref[low:, low:high]) for low, high in cuts]
+    cuts = column_cuts(leaf)
+    y_t = []
+    for low, high, _ in cuts:
+        total = None
+        for left, right, base in cuts:
+            if left <= low:
+                rows = slice(base + low - left, base + high - left)
+                term = dot(owned[:, left:right], packed_ref[rows, 0 : right - left], NT)
+                total = term if total is None else total + term
+        y_t.append(total)
+    y_ref[...] = jnp.concatenate(y_t, axis=1).astype(BF)
+
+
+def backward_kernel(y_ref, packed_ref, out_ref):
+    leaf = out_ref.shape[0]
+    cuts = column_cuts(leaf)
+    y_t = y_ref[...]
+    bare_t = [
+        dot(y_t[:, low:], packed_ref[base : base + leaf - low, 0 : high - low])
+        for low, high, base in cuts
+    ]
     out_ref[...] = jnp.concatenate(bare_t, axis=1).T
 
 
@@ -334,18 +365,23 @@
         recv_place[0, 0].reshape(owners, keep), ((0, 0), (0, pad - keep)), constant_values=-1
     ).reshape(1, slots)
     span = jnp.swapaxes(sep_panels[0, 0], 1, 2)
-    push, back, side = call(
+    packed_rows = sum(leaf - low for low, _, _ in column_cuts(leaf))
+    push, back, side, packed = call(
         factor_kernel,
         "factor_products",
-        [VM, VM, VM, HB, HB, HB, HB, HB],
-        [(sds((192, slots), BF), VM), (sds((leaf, 256), BF), VM), (sds((112, 256), BF), VM)],
+        [VM, VM, VM, VM, HB, HB, HB, HB],
+        [
+            (sds((192, slots), BF), VM),
+            (sds((leaf, 256), BF), VM),
+            (sds((112, 256), BF), VM),
+            (sds((packed_rows, 256), BF), HB),
+        ],
         [
             pltpu.VMEM(panels.shape, BF),
-            pltpu.VMEM((leaf, leaf), BF),
             pltpu.VMEM(sep_inv.shape[2:], BF),
             pltpu.VMEM(span.shape, BF),
             pltpu.VMEM(sep_rhs.shape[2:], BF),
-            DMA((5,)),
+            DMA((4 + len(column_cuts(leaf)),)),
         ],
         flops=2 * 192 * leaf * (leaf + slots),
         nbytes=2 * leaf * leaf + 2 * 192 * slots + 2 * 256 * leaf,
@@ -353,8 +389,8 @@
         place,
         leaf_rows[0, 0][:, None, :],
         sep_rows[0, 0][:, None, :],
+        inv,
         panels,
-        inv,
         sep_inv[0, 0],
         span,
         sep_rhs[0, 0],
@@ -368,19 +404,25 @@
         nbytes=2 * slots * (192 + width) + TREE * 80 * 512,
     )(recv, push, side)
     got = lax.all_to_all(chunks, "peer", split_axis=0, concat_axis=0, tiled=True)
-    (bare,) = call(
-        leaf_kernel,
-        "leaf_solve",
-        [VM, VM, HB],
-        [(sds((leaf, width), F32), VM)],
-        [pltpu.VMEM((leaf, leaf), BF), DMA],
-        flops=2 * leaf * width * (2 * leaf + slots),
-        nbytes=2 * leaf * leaf + 6 * slots * width,
-    )(place, recv, inv)
-
-    got, bare = lax.optimization_barrier((got, bare))
+    (leaf_y,) = call(
+        lambda *refs: forward_kernel(leaf, *refs),
+        "leaf_forward",
+        [VM, VM, VM],
+        [(sds((width, leaf), BF), VM)],
+        flops=2 * leaf * width * (leaf + slots),
+        nbytes=2 * leaf * leaf + 4 * slots * width,
+    )(place, recv, packed)
+    got, leaf_y = lax.optimization_barrier((got, leaf_y))
     other = lax.ppermute(got, "front", [(0, 1), (1, 0)])
     front = lax.axis_index("front").astype(jnp.int32).reshape(1)
+    (bare,) = call(
+        backward_kernel,
+        "leaf_backward",
+        [VM, VM],
+        [(sds((leaf, width), F32), VM)],
+        flops=2 * leaf * width * leaf,
+        nbytes=2 * leaf * leaf + 6 * leaf * width,
+    )(leaf_y, packed)
     square = pltpu.VMEM((256, 256), BF)
     (solved,) = call(
         tree_kernel,

time: 60.9 us -> 59.2 us (0.972)
  blocking collectives: 9.2 us -> 7.83 us
  Pallas kernels: 15.7 us -> 14.7 us
  waiting for transfers between devices: 11.7 us -> 12.7 us
    all_to_all x1, waiting for transfers between devices: 0.37 us -> 3.96 us  [on_device(): lax.all_to_all(chunks, 'peer', split_axis=0, concat_axis=0, tiled=True)]
    all_to_all x1, waiting for transfers between devices: 10.1 us -> 8.32 us  [on_device(): lax.all_to_all(sent.reshape(owners, pad, width), ('tree', 'peer'), split_...]
    all_to_all x1, blocking collectives: 9.2 us -> 7.83 us  [on_device(): lax.all_to_all(solved, 'peer', split_axis=0, concat_axis=0, tiled=True)]
    pallas_call x2 -> x3, Pallas kernels: 7.07 us -> 5.97 us  [the longest x1 2.68 us: on_device(): call(factor_kernel, 'factor_products', [VM, VM, VM, VM, HB, HB, HB, HB],...]
    ppermute x1, waiting for transfers between devices: 1.26 us -> 0.46 us  [on_device(): other = lax.ppermute(got, 'front', [(0, 1), (1, 0)])]
    unnamed x18 -> x20, local copies, waits for them, and re-layouts: 3.53 us -> 3.6 us
  transfers between devices with their start and end apart: 3 -> 3, of which waited for: 3 -> 3; matrix products, arithmetic and copies ran while one was open for 0% -> 0% of each run, Pallas kernels for 12% -> 10%
where the time goes in v5:
time: 59.2 us; the launch traced here: 58.6 us
  starting transfers between devices  18.7 us (32%)
  Pallas kernels  14.7 us (25%)
  waiting for transfers between devices  12.7 us (21%)
  blocking collectives  7.83 us (13%)
  local copies, waits for them, and re-layouts  3.83 us (6%)
  between operations  0.83 us (1%)
    all_to_all x1, starting transfers between devices, on_device(): lax.all_to_all(sent.reshape(owners, pad, width), ('tree', 'peer'), split_...  12 us
    all_to_all x1, waiting for transfers between devices, on_device(): lax.all_to_all(sent.reshape(owners, pad, width), ('tree', 'peer'), split_...  8.32 us
    all_to_all x1, blocking collectives, on_device(): lax.all_to_all(solved, 'peer', split_axis=0, concat_axis=0, tiled=True)  7.83 us
    all_to_all x1, waiting for transfers between devices, on_device(): lax.all_to_all(chunks, 'peer', split_axis=0, concat_axis=0, tiled=True)  3.96 us
    unnamed x20, local copies, waits for them, and re-layouts  3.6 us
    all_to_all x1, starting transfers between devices, on_device(): lax.all_to_all(chunks, 'peer', split_axis=0, concat_axis=0, tiled=True)  3.43 us
    pallas_call x1, Pallas kernels, on_device(): call(lambda *refs: send_kernel(keep, pad, *refs), 'send_rows', [HB, HB],...  3.26 us
    ppermute x1, starting transfers between devices, on_device(): other = lax.ppermute(got, 'front', [(0, 1), (1, 0)])  3.26 us
  transfers between devices with their start and end apart: 3, of which 3 were waited for; matrix products, arithmetic and copies ran while one was open for 0% of the time, Pallas kernels for 10%

profile of v5, /device:TPU:1, one launch (start us, length us, event | category | flops | bytes accessed | tf_op | source)
XLA Modules:
  0.0 58.6 jit_solution(14810042630432221415)
XLA Ops:
  0.6 0.0 copy-start.9
  0.6 0.0 copy-start.4
  0.7 0.0 copy-start.5
  0.7 0.0 copy-start.6
  0.7 0.0 copy-start.7
  0.7 0.0 copy-start.8
  0.7 3.3 %send_rows.1 = bf16[1536,256]{1,0:T(8,128)(2,1)} custom-call(s32[1,1152]{1,0:T(1,128)} %bitcast.29, bf16[1152,256]{1,0:T(8,128)(2,1)} %bitcast.27), custom_call_target="tpu_custom_call" | custom-call | flops 679477248 | bytes 1179648 | tf_op jit(solution)/shard_map/send_rows/pallas_call | solution.py:344
  4.0 12.0 %all-to-all-start = ((bf16[64,24,256]{2,1,0:T(8,128)(2,1)}), bf16[64,24,256]{2,1,0:T(8,128)(2,1)S(1)}, u32[]{:S(2)}, u32[]{:S(2)}) async-start(bf16[64,24,256]{2,1,0:T(8,128)(2,1)} %bitcast.25), calls=%async_computation | async-start | bytes 1572864 | tf_op jit(solution)/shard_map/all_to_all | solution.py:360
  15.9 0.0 copy-done.9
  16.0 0.1 reshape_squeeze.6
  16.1 0.1 reshape.19.place_ref.refs_0_
  16.2 0.0 copy-done.4
  16.2 0.0 copy-done.5
  16.2 0.0 copy-done.6
  16.3 0.0 copy-done.7
  16.3 0.0 copy-done.8
  16.3 0.0 copy-start.2
  16.3 1.7 %copy-done.2 = bf16[1,1,1152,1152]{3,2,1,0:T(8,128)(2,1)S(1)} copy-done((bf16[1,1,1152,1152]{3,2,1,0:T(8,128)(2,1)S(1)}, bf16[1,1,1152,1152]{3,2,1,0:T(8,128)(2,1)}, u32[]{:S(2)}) %copy-start.2) | copy-done | bytes 2654232
  18.0 0.0 copy-start.3
  18.0 1.0 %copy-done.3 = bf16[1,1,3,64,1152]{4,3,2,1,0:T(8,128)(2,1)S(1)} copy-done((bf16[1,1,3,64,1152]{4,3,2,1,0:T(8,128)(2,1)S(1)}, bf16[1,1,3,64,1152]{4,3,2,1,0:T(8,128)(2,1)}, u32[]{:S(2)}) %copy-start.3) | copy-done | bytes 442392
  19.0 2.7 %factor_products.1 = (bf16[192,1536]{1,0:T(8,128)(2,1)S(1)}, bf16[1152,256]{1,0:T(8,128)(2,1)S(1)}, bf16[112,256]{1,0:T(8,128)(2,1)S(1)}, bf16[3200,256]{1,0:T(8,128)(2,1)S(1)}) custom-call(s32[1,1536]{1,0:T(1,128)S(1)} %reshape.19.place_ref.refs_0_, s32[3,1,64]{2,1,0:T(1,128)S(1)} %bitcast.23, s32[3,1,64]{2,1,0:T(1,128)S(1)} %bitcast.24, ...), custom_call_target="tpu_custom_call" | custom-call | flops 1189085184 | bytes 3833856 | tf_op jit(solution)/shard_map/factor_products/pallas_call | solution.py:369
  21.7 0.0 copy-start
  21.7 0.8 %copy-done = bf16[1152,256]{1,0:T(8,128)(2,1)} copy-done((bf16[1152,256]{1,0:T(8,128)(2,1)}, bf16[1152,256]{1,0:T(8,128)(2,1)S(1)}, u32[]{:S(2)}) %copy-start) | copy-done | bytes 589848
  22.6 8.3 %all-to-all-done = bf16[64,24,256]{2,1,0:T(8,128)(2,1)S(1)} async-done(((bf16[64,24,256]{2,1,0:T(8,128)(2,1)}), bf16[64,24,256]{2,1,0:T(8,128)(2,1)S(1)}, u32[]{:S(2)}, u32[]{:S(2)}) %all-to-all-start) | async-done | bytes 786464 | tf_op jit(solution)/shard_map/all_to_all | solution.py:360
  30.9 1.1 %push_updates.1 = bf16[8,80,256]{2,1,0:T(8,128)(2,1)} custom-call(bf16[1536,256]{1,0:T(8,128)(2,1)S(1)} %bitcast.16, bf16[192,1536]{1,0:T(8,128)(2,1)S(1)} %get-tuple-element.10.push_ref, bf16[112,256]{1,0:T(8,128)(2,1)S(1)} %get-tuple-element.11.side_ref), custom_call_target="tpu_custom_call" | custom-call | flops 150994944 | bytes 1703936 | tf_op jit(solution)/shard_map/push_updates/pallas_call | solution.py:398
  32.0 3.4 %all-to-all-start.1 = ((bf16[8,80,256]{2,1,0:T(8,128)(2,1)}), bf16[8,80,256]{2,1,0:T(8,128)(2,1)S(1)}, u32[]{:S(2)}, u32[]{:S(2)}) async-start(bf16[8,80,256]{2,1,0:T(8,128)(2,1)} %push_updates.1), calls=%async_computation.1 | async-start | bytes 655360 | tf_op jit(solution)/shard_map/all_to_all | solution.py:406
  35.4 2.5 %leaf_forward.1.y_ref = bf16[256,1152]{1,0:T(8,128)(2,1)S(1)} custom-call(s32[1,1536]{1,0:T(1,128)S(1)} %reshape.19.place_ref.refs_0_, bf16[1536,256]{1,0:T(8,128)(2,1)S(1)} %bitcast.17, bf16[3200,256]{1,0:T(8,128)(2,1)S(1)} %get-tuple-element.12.refs_2_.packed_ref), custom_call_target="tpu_custom_call" | custom-call | flops 1585446912 | bytes 4227072 | tf_op jit(solution)/shard_map/leaf_forward/pallas_call | solution.py:407
  38.0 4.0 %all-to-all-done.1.got_ref = bf16[8,80,256]{2,1,0:T(8,128)(2,1)S(1)} async-done(((bf16[8,80,256]{2,1,0:T(8,128)(2,1)}), bf16[8,80,256]{2,1,0:T(8,128)(2,1)S(1)}, u32[]{:S(2)}, u32[]{:S(2)}) %all-to-all-start.1) | async-done | bytes 327712 | tf_op jit(solution)/shard_map/all_to_all | solution.py:406
  41.9 3.3 %collective-permute-start = (bf16[8,80,256]{2,1,0:T(8,128)(2,1)S(1)}, bf16[8,80,256]{2,1,0:T(8,128)(2,1)S(1)}, u32[]{:S(2)}, u32[]{:S(2)}) collective-permute-start(bf16[8,80,256]{2,1,0:T(8,128)(2,1)S(1)} %all-to-all-done.1.got_ref), channel_id=1, source_target_pairs={{0,1},{1,0},{2,3},{3,2},{4,5},{5,4},{6,7},{7,6},{8,9},{9,8},{10,11... | collective-permute-start | bytes 983048 | tf_op jit(solution)/shard_map/ppermute | solution.py:416
  45.2 0.8 %leaf_backward.1.bare_hbm.leaf_ref = f32[1152,256]{1,0:T(8,128)S(1)} custom-call(bf16[256,1152]{1,0:T(8,128)(2,1)S(1)} %leaf_forward.1.y_ref, bf16[3200,256]{1,0:T(8,128)(2,1)S(1)} %get-tuple-element.12.refs_2_.packed_ref), custom_call_target="tpu_custom_call" | custom-call | flops 679477248 | bytes 4423680 | tf_op jit(solution)/shard_map/leaf_backward/pallas_call | solution.py:418
  46.0 0.0 copy-start.1
  46.0 0.5 collective-permute-done.other_ref
  46.4 2.9 %separator_tree.1 = bf16[8,32,256]{2,1,0:T(8,128)(2,1)S(1)} custom-call(s32[1]{0:T(128)} %bitcast.front_ref, bf16[8,80,256]{2,1,0:T(8,128)(2,1)S(1)} %all-to-all-done.1.got_ref, bf16[8,80,256]{2,1,0:T(8,128)(2,1)S(1)} %collective-permute-done.other_ref, f32[1152,256]{1,0:T(8,128)S(1)} %leaf_backward.1.bare_hbm.leaf_ref), custom_call_target="tpu_custom_call" | custom-call | flops 150994944 | bytes 786432 | tf_op jit(solution)/shard_map/separator_tree/pallas_call | solution.py:427
  49.4 7.8 %all_to_all.15.got_ref = bf16[8,32,256]{2,1,0:T(8,128)(2,1)S(1)} all-to-all(bf16[8,32,256]{2,1,0:T(8,128)(2,1)S(1)} %separator_tree.1), channel_id=1, replica_groups=mesh['tree'=8,'peer'=8,'front'=2] {'peer'}, dimensions={0} | all-to-all | bytes 262144 | tf_op jit(solution)/shard_map/all_to_all | solution.py:436
  57.2 0.0 copy-done.1
  57.2 1.4 %finish.1 = (f32[1152,256]{1,0:T(8,128)}, bf16[3,16,256]{2,1,0:T(8,128)(2,1)}) custom-call(bf16[8,32,256]{2,1,0:T(8,128)(2,1)S(1)} %all_to_all.15.got_ref, bf16[1152,256]{1,0:T(8,128)(2,1)S(1)} %copy-done.1, f32[1152,256]{1,0:T(8,128)S(1)} %leaf_backward.1.bare_hbm.leaf_ref), custom_call_target="tpu_custom_call" | custom-call | flops 150994944 | bytes 3080192 | tf_op jit(solution)/shard_map/finish/pallas_call | solution.py:438
  (2 shorter events, 0.0 us)
Async XLA Ops:
  0.6 15.3 %copy-start.9 = (s32[1,1,1152]{2,1,0:T(1,128)S(1)}, s32[1,1,1152]{2,1,0:T(1,128)}, u32[]{:S(2)}) copy-start(s32[1,1,1152]{2,1,0:T(1,128)} %param.12) | copy-start | bytes 13828
  0.6 15.6 %copy-start.4 = (bf16[1,1,3,16,256]{4,3,2,1,0:T(8,128)(2,1)S(1)}, bf16[1,1,3,16,256]{4,3,2,1,0:T(8,128)(2,1)}, u32[]{:S(2)}) copy-start(bf16[1,1,3,16,256]{4,3,2,1,0:T(8,128)(2,1)} %param.13) | copy-start | bytes 73732
  0.7 15.6 %copy-start.5 = (bf16[1,1,32,224]{3,2,1,0:T(8,128)(2,1)S(1)}, bf16[1,1,32,224]{3,2,1,0:T(8,128)(2,1)}, u32[]{:S(2)}) copy-start(bf16[1,1,32,224]{3,2,1,0:T(8,128)(2,1)} %param.17) | copy-start | bytes 43012
  0.7 15.6 %copy-start.6 = (bf16[1,1,3,64,16]{3,4,2,1,0:T(8,128)(2,1)S(1)}, bf16[1,1,3,64,16]{3,4,2,1,0:T(8,128)(2,1)}, u32[]{:S(2)}) copy-start(bf16[1,1,3,64,16]{3,4,2,1,0:T(8,128)(2,1)} %param.18) | copy-start | bytes 18436
  0.7 15.6 %copy-start.7 = (s32[1,1,3,64]{3,1,2,0:T(1,128)S(1)}, s32[1,1,3,64]{3,1,2,0:T(1,128)}, u32[]{:S(2)}) copy-start(s32[1,1,3,64]{3,1,2,0:T(1,128)} %param.16) | copy-start | bytes 2308
  0.7 15.6 %copy-start.8 = (s32[1,1,3,64]{3,1,2,0:T(1,128)S(1)}, s32[1,1,3,64]{3,1,2,0:T(1,128)}, u32[]{:S(2)}) copy-start(s32[1,1,3,64]{3,1,2,0:T(1,128)} %param.19) | copy-start | bytes 2308
  4.0 26.9 %all-to-all-start = ((bf16[64,24,256]{2,1,0:T(8,128)(2,1)}), bf16[64,24,256]{2,1,0:T(8,128)(2,1)S(1)}, u32[]{:S(2)}, u32[]{:S(2)}) async-start(bf16[64,24,256]{2,1,0:T(8,128)(2,1)} %bitcast.25), calls=%async_computation | async-start | bytes 1572864 | tf_op jit(solution)/shard_map/all_to_all | solution.py:360
  16.3 1.8 %copy-start.2 = (bf16[1,1,1152,1152]{3,2,1,0:T(8,128)(2,1)S(1)}, bf16[1,1,1152,1152]{3,2,1,0:T(8,128)(2,1)}, u32[]{:S(2)}) copy-start(bf16[1,1,1152,1152]{3,2,1,0:T(8,128)(2,1)} %param.14) | copy-start | bytes 7962628
  18.0 1.0 %copy-start.3 = (bf16[1,1,3,64,1152]{4,3,2,1,0:T(8,128)(2,1)S(1)}, bf16[1,1,3,64,1152]{4,3,2,1,0:T(8,128)(2,1)}, u32[]{:S(2)}) copy-start(bf16[1,1,3,64,1152]{4,3,2,1,0:T(8,128)(2,1)} %param.15) | copy-start | bytes 1327108
  21.7 0.8 %copy-start = (bf16[1152,256]{1,0:T(8,128)(2,1)}, bf16[1152,256]{1,0:T(8,128)(2,1)S(1)}, u32[]{:S(2)}) copy-start(bf16[1152,256]{1,0:T(8,128)(2,1)S(1)} %get-tuple-element.15.back_ref) | copy-start | bytes 1769476
  32.0 9.9 %all-to-all-start.1 = ((bf16[8,80,256]{2,1,0:T(8,128)(2,1)}), bf16[8,80,256]{2,1,0:T(8,128)(2,1)S(1)}, u32[]{:S(2)}, u32[]{:S(2)}) async-start(bf16[8,80,256]{2,1,0:T(8,128)(2,1)} %push_updates.1), calls=%async_computation.1 | async-start | bytes 655360 | tf_op jit(solution)/shard_map/all_to_all | solution.py:406
  41.9 4.5 %collective-permute-start = (bf16[8,80,256]{2,1,0:T(8,128)(2,1)S(1)}, bf16[8,80,256]{2,1,0:T(8,128)(2,1)S(1)}, u32[]{:S(2)}, u32[]{:S(2)}) collective-permute-start(bf16[8,80,256]{2,1,0:T(8,128)(2,1)S(1)} %all-to-all-done.1.got_ref), channel_id=1, source_target_pairs={{0,1},{1,0},{2,3},{3,2},{4,5},{5,4},{6,7},{7,6},{8,9},{9,8},{10,11... | collective-permute-start | bytes 983048 | tf_op jit(solution)/shard_map/ppermute | solution.py:416
  46.0 11.2 %copy-start.1 = (bf16[1152,256]{1,0:T(8,128)(2,1)S(1)}, bf16[1152,256]{1,0:T(8,128)(2,1)}, u32[]{:S(2)}) copy-start(bf16[1152,256]{1,0:T(8,128)(2,1)} %copy-done) | copy-start | bytes 1769476

commit v6 on v5

--- a/solution.py
+++ b/solution.py
@@ -16,6 +16,7 @@
 
 NN = (((1,), (0,)), ((), ()))
 NT = (((1,), (1,)), ((), ()))
+TN = (((0,), (0,)), ((), ()))
 
 
 def dot(a, b, dims=NN):
@@ -65,32 +66,21 @@
     rhs_in = fetch(rhs_hbm, rhs_ref, sems.at[1])
     tail = picked_ref.shape[0] - rows
     picked_ref[rows:, :] = jnp.zeros((tail, width), F32)
-    owners = rows // keep
-    step = 384
-    lanes = lane_ids(128, rows)
+    lanes = lane_ids(128, 128).astype(F32).astype(BF)
+    one, zero = jnp.ones((128, 128), BF), jnp.zeros((128, 128), BF)
     order_in.wait()
     hots = []
     for at in range(0, rows, 128):
-        ids = jnp.broadcast_to(order_ref[:, at : at + 128], (128, 128)).T
-        hots.append(hot(jnp.concatenate([ids] * (rows // 128), axis=1) == lanes))
+        ids = jnp.broadcast_to(order_ref[:, at : at + 128], (128, 128)).T.astype(F32)
+        tiles = [jnp.where(lanes == (ids - base).astype(BF), one, zero) for base in range(0, rows, 128)]
+        hots.append(jnp.concatenate(tiles, axis=1))
     rhs_in.wait()
-    rhs = rhs_ref[...]
-    done = 0
-    leaving = []
-    for part in range(rows // step):
-        block = jnp.concatenate(hots[part * 3 : part * 3 + 3], axis=0)
-        picked_ref[part * step : (part + 1) * step, :] = dot(block, rhs)
-        have = (part + 1) * step
-        upto = owners if have == rows else ((have - pad) // keep + 1) // 2 * 2
-        for owner in range(done, upto):
-            out_ref[owner * pad : (owner + 1) * pad, :] = picked_ref[
-                owner * keep : owner * keep + pad, :
-            ].astype(BF)
-        span = slice(done * pad, upto * pad)
-        leaving.append(fetch(out_ref.at[span, :], out_hbm.at[span, :], sems.at[2 + part]))
-        done = upto
-    for copy in leaving:
-        copy.wait()
+    picked_ref[0:rows, :] = dot(jnp.concatenate(hots, axis=0), rhs_ref[...])
+    for owner in range(rows // keep):
+        out_ref[owner * pad : (owner + 1) * pad, :] = picked_ref[
+            owner * keep : owner * keep + pad, :
+        ].astype(BF)
+    fetch(out_ref, out_hbm, sems.at[2]).wait()
 
 
 def column_cuts(leaf):
@@ -187,6 +177,14 @@
     out_ref[...] = jnp.concatenate(bare_t, axis=1).T
 
 
+def hot_at(where, rows):
+    cols = where.shape[1]
+    here = row_ids(rows, cols).astype(F32).astype(BF)
+    there = jnp.broadcast_to(where, (SUB, cols)).astype(BF)
+    there = jnp.concatenate([there] * (rows // SUB), axis=0)
+    return jnp.where(here == there, jnp.ones((rows, cols), BF), jnp.zeros((rows, cols), BF))
+
+
 def turn(value, shift):
     shift = shift % 128
     return pltpu.roll(value, shift, 1) if shift else value
@@ -219,26 +217,23 @@
         for ref, low in ((e1_ref, low1), (e0_ref, low0)):
             ref[rows, tile * 128 : (tile + 1) * 128] = low.astype(BF)
             ref[rows, (1 - tile) * 128 : (2 - tile) * 128] = none
-    sub = row_ids(256, 64)
     for side, table in enumerate(sides):
         for peer in range(TREE):
             at = peer * 2 * SUB + (front ^ side) * SUB
             rows = pl.ds(pl.multiple_of(at, SUB), SUB)
             for pair, ref in enumerate((a01_ref, a02_ref, a12_ref)):
-                where = table[peer, 64 + pair : 65 + pair, 192:256].astype(F32).astype(jnp.int32)
+                where = table[peer, 64 + pair : 65 + pair, 192:256].astype(F32)
                 if pair == 0:
-                    where = where + peer // 4 * 128
+                    where = where + float(peer // 4 * 128)
                 flipped = table[peer, 64:80, pair * 64 : (pair + 1) * 64]
-                ref[rows, :] = dot(flipped, hot(sub == where), NT).astype(BF)
-    wide = row_ids(256, 256)
+                ref[rows, :] = dot(flipped, hot_at(where, 256), NT).astype(BF)
     for level in range(3):
         for quad in range(4):
             parts = []
             for peer in range(quad % 2 * 4, quad % 2 * 4 + 4):
                 where = sides[quad // 2][peer, 67 + level : 68 + level, 192:256].astype(F32)
-                parts.append(where + (peer // 2 * 64, peer // 4 * 128, 0)[level])
-            where = jnp.concatenate(parts, axis=1).astype(jnp.int32)
-            spots_ref[level * 4 + quad] = hot(wide == where)
+                parts.append(where + (peer // 2 * 64.0, peer // 4 * 128.0, 0.0)[level])
+            spots_ref[level * 4 + quad] = hot_at(jnp.concatenate(parts, axis=1), 256)
     lane = lane_ids(COLS, 128)
     half = lane < 64
     sums = []
@@ -277,14 +272,18 @@
     r0, r1, r2 = sums
     e0, e1, e2 = e0_ref[...], e1_ref[...], e2_ref[...]
     a01, a02, a12 = a01_ref[...], a02_ref[...], a12_ref[...]
-    y0 = dot(r0.astype(BF), e0, NT)
-    y0b = y0.astype(BF)
-    y1 = dot((r1 - dot(y0b, a01)).astype(BF), e1, NT)
-    y1b = y1.astype(BF)
-    y2 = dot((r2 - dot(y0b, a02) - dot(y1b, a12)).astype(BF), e2, NT)
-    x2 = dot(y2.astype(BF), e2).astype(BF)
-    x1 = dot((y1 - dot(x2, a12, NT)).astype(BF), e1).astype(BF)
-    x0 = dot((y0 - dot(x2, a02, NT) - dot(x1, a01, NT)).astype(BF), e0).astype(BF)
+    c01 = dot(e0, a01, TN).astype(BF)
+    c02 = dot(e0, a02, TN).astype(BF)
+    c12 = dot(e1, a12, TN).astype(BF)
+    g0 = dot(e0, e0, TN).astype(BF)
+    g1 = dot(e1, e1, TN).astype(BF)
+    g2 = dot(e2, e2, TN).astype(BF)
+    r0 = r0.astype(BF)
+    r1 = (r1 - dot(r0, c01)).astype(BF)
+    r2 = (r2 - dot(r0, c02) - dot(r1, c12)).astype(BF)
+    x2 = dot(r2, g2).astype(BF)
+    x1 = (dot(r1, g1) - dot(x2, c12, NT)).astype(BF)
+    x0 = (dot(r0, g0) - dot(x2, c02, NT) - dot(x1, c01, NT)).astype(BF)
     solved = (x0, x1, x2)
     own = []
     for level in range(3):
@@ -351,7 +350,7 @@
             pltpu.VMEM((leaf, width), BF),
             pltpu.VMEM((-(-(leaf - keep + pad) // 8) * 8 + 8, width), F32),
             pltpu.VMEM((slots, width), BF),
-            DMA((5,)),
+            DMA((3,)),
         ],
         flops=2 * leaf * leaf * width,
         nbytes=2 * leaf * width * 2,

time: 59.2 us -> 58.7 us (level)
  Pallas kernels: 14.7 us -> 14.1 us
where the time goes in v6:
time: 58.7 us; the launch traced here: 58 us
  starting transfers between devices  18.7 us (32%)
  Pallas kernels  14.1 us (24%)
  waiting for transfers between devices  12.7 us (22%)
  blocking collectives  7.83 us (13%)
  local copies, waits for them, and re-layouts  3.83 us (7%)
  between operations  0.83 us (1%)
    all_to_all x1, starting transfers between devices, on_device(): lax.all_to_all(sent.reshape(owners, pad, width), ('tree', 'peer'), split_...  12 us
    all_to_all x1, waiting for transfers between devices, on_device(): lax.all_to_all(sent.reshape(owners, pad, width), ('tree', 'peer'), split_...  8.32 us
    all_to_all x1, blocking collectives, on_device(): lax.all_to_all(solved, 'peer', split_axis=0, concat_axis=0, tiled=True)  7.83 us
    all_to_all x1, waiting for transfers between devices, on_device(): lax.all_to_all(chunks, 'peer', split_axis=0, concat_axis=0, tiled=True)  3.96 us
    unnamed x20, local copies, waits for them, and re-layouts  3.6 us
    all_to_all x1, starting transfers between devices, on_device(): lax.all_to_all(chunks, 'peer', split_axis=0, concat_axis=0, tiled=True)  3.43 us
    ppermute x1, starting transfers between devices, on_device(): other = lax.ppermute(got, 'front', [(0, 1), (1, 0)])  3.26 us
    pallas_call x1, Pallas kernels, on_device(): call(lambda *refs: send_kernel(keep, pad, *refs), 'send_rows', [HB, HB],...  3.18 us
  transfers between devices with their start and end apart: 3, of which 3 were waited for; matrix products, arithmetic and copies ran while one was open for 0% of the time, Pallas kernels for 10%

profile of v6, /device:TPU:1, one launch (start us, length us, event | category | flops | bytes accessed | tf_op | source)
XLA Modules:
  0.0 58.0 jit_solution(16312198517511205424)
XLA Ops:
  0.6 0.0 copy-start.9
  0.6 0.0 copy-start.4
  0.7 0.0 copy-start.5
  0.7 0.0 copy-start.6
  0.7 0.0 copy-start.7
  0.7 0.0 copy-start.8
  0.7 3.2 %send_rows.1 = bf16[1536,256]{1,0:T(8,128)(2,1)} custom-call(s32[1,1152]{1,0:T(1,128)} %bitcast.29, bf16[1152,256]{1,0:T(8,128)(2,1)} %bitcast.27), custom_call_target="tpu_custom_call" | custom-call | flops 679477248 | bytes 1179648 | tf_op jit(solution)/shard_map/send_rows/pallas_call | solution.py:343
  3.9 12.0 %all-to-all-start = ((bf16[64,24,256]{2,1,0:T(8,128)(2,1)}), bf16[64,24,256]{2,1,0:T(8,128)(2,1)S(1)}, u32[]{:S(2)}, u32[]{:S(2)}) async-start(bf16[64,24,256]{2,1,0:T(8,128)(2,1)} %bitcast.25), calls=%async_computation | async-start | bytes 1572864 | tf_op jit(solution)/shard_map/all_to_all | solution.py:359
  15.9 0.0 copy-done.9
  15.9 0.1 reshape_squeeze.6
  16.0 0.1 reshape.19.place_ref.refs_0_
  16.1 0.0 copy-done.4
  16.2 0.0 copy-done.5
  16.2 0.0 copy-done.6
  16.2 0.0 copy-done.7
  16.2 0.0 copy-done.8
  16.2 0.0 copy-start.2
  16.2 1.7 %copy-done.2 = bf16[1,1,1152,1152]{3,2,1,0:T(8,128)(2,1)S(1)} copy-done((bf16[1,1,1152,1152]{3,2,1,0:T(8,128)(2,1)S(1)}, bf16[1,1,1152,1152]{3,2,1,0:T(8,128)(2,1)}, u32[]{:S(2)}) %copy-start.2) | copy-done | bytes 2654232
  17.9 0.0 copy-start.3
  17.9 1.0 %copy-done.3 = bf16[1,1,3,64,1152]{4,3,2,1,0:T(8,128)(2,1)S(1)} copy-done((bf16[1,1,3,64,1152]{4,3,2,1,0:T(8,128)(2,1)S(1)}, bf16[1,1,3,64,1152]{4,3,2,1,0:T(8,128)(2,1)}, u32[]{:S(2)}) %copy-start.3) | copy-done | bytes 442392
  19.0 2.7 %factor_products.1 = (bf16[192,1536]{1,0:T(8,128)(2,1)S(1)}, bf16[1152,256]{1,0:T(8,128)(2,1)S(1)}, bf16[112,256]{1,0:T(8,128)(2,1)S(1)}, bf16[3200,256]{1,0:T(8,128)(2,1)S(1)}) custom-call(s32[1,1536]{1,0:T(1,128)S(1)} %reshape.19.place_ref.refs_0_, s32[3,1,64]{2,1,0:T(1,128)S(1)} %bitcast.23, s32[3,1,64]{2,1,0:T(1,128)S(1)} %bitcast.24, ...), custom_call_target="tpu_custom_call" | custom-call | flops 1189085184 | bytes 3833856 | tf_op jit(solution)/shard_map/factor_products/pallas_call | solution.py:368
  21.6 0.0 copy-start
  21.7 0.8 %copy-done = bf16[1152,256]{1,0:T(8,128)(2,1)} copy-done((bf16[1152,256]{1,0:T(8,128)(2,1)}, bf16[1152,256]{1,0:T(8,128)(2,1)S(1)}, u32[]{:S(2)}) %copy-start) | copy-done | bytes 589848
  22.5 8.3 %all-to-all-done = bf16[64,24,256]{2,1,0:T(8,128)(2,1)S(1)} async-done(((bf16[64,24,256]{2,1,0:T(8,128)(2,1)}), bf16[64,24,256]{2,1,0:T(8,128)(2,1)S(1)}, u32[]{:S(2)}, u32[]{:S(2)}) %all-to-all-start) | async-done | bytes 786464 | tf_op jit(solution)/shard_map/all_to_all | solution.py:359
  30.8 1.1 %push_updates.1 = bf16[8,80,256]{2,1,0:T(8,128)(2,1)} custom-call(bf16[1536,256]{1,0:T(8,128)(2,1)S(1)} %bitcast.16, bf16[192,1536]{1,0:T(8,128)(2,1)S(1)} %get-tuple-element.10.push_ref, bf16[112,256]{1,0:T(8,128)(2,1)S(1)} %get-tuple-element.11.side_ref), custom_call_target="tpu_custom_call" | custom-call | flops 150994944 | bytes 1703936 | tf_op jit(solution)/shard_map/push_updates/pallas_call | solution.py:397
  31.9 3.4 %all-to-all-start.1 = ((bf16[8,80,256]{2,1,0:T(8,128)(2,1)}), bf16[8,80,256]{2,1,0:T(8,128)(2,1)S(1)}, u32[]{:S(2)}, u32[]{:S(2)}) async-start(bf16[8,80,256]{2,1,0:T(8,128)(2,1)} %push_updates.1), calls=%async_computation.1 | async-start | bytes 655360 | tf_op jit(solution)/shard_map/all_to_all | solution.py:405
  35.4 2.5 %leaf_forward.1.y_ref = bf16[256,1152]{1,0:T(8,128)(2,1)S(1)} custom-call(s32[1,1536]{1,0:T(1,128)S(1)} %reshape.19.place_ref.refs_0_, bf16[1536,256]{1,0:T(8,128)(2,1)S(1)} %bitcast.17, bf16[3200,256]{1,0:T(8,128)(2,1)S(1)} %get-tuple-element.12.refs_2_.packed_ref), custom_call_target="tpu_custom_call" | custom-call | flops 1585446912 | bytes 4227072 | tf_op jit(solution)/shard_map/leaf_forward/pallas_call | solution.py:406
  37.9 4.0 %all-to-all-done.1.got_ref = bf16[8,80,256]{2,1,0:T(8,128)(2,1)S(1)} async-done(((bf16[8,80,256]{2,1,0:T(8,128)(2,1)}), bf16[8,80,256]{2,1,0:T(8,128)(2,1)S(1)}, u32[]{:S(2)}, u32[]{:S(2)}) %all-to-all-start.1) | async-done | bytes 327712 | tf_op jit(solution)/shard_map/all_to_all | solution.py:405
  41.8 3.3 %collective-permute-start = (bf16[8,80,256]{2,1,0:T(8,128)(2,1)S(1)}, bf16[8,80,256]{2,1,0:T(8,128)(2,1)S(1)}, u32[]{:S(2)}, u32[]{:S(2)}) collective-permute-start(bf16[8,80,256]{2,1,0:T(8,128)(2,1)S(1)} %all-to-all-done.1.got_ref), channel_id=1, source_target_pairs={{0,1},{1,0},{2,3},{3,2},{4,5},{5,4},{6,7},{7,6},{8,9},{9,8},{10,11... | collective-permute-start | bytes 983048 | tf_op jit(solution)/shard_map/ppermute | solution.py:415
  45.1 0.8 %leaf_backward.1.bare_hbm.leaf_ref = f32[1152,256]{1,0:T(8,128)S(1)} custom-call(bf16[256,1152]{1,0:T(8,128)(2,1)S(1)} %leaf_forward.1.y_ref, bf16[3200,256]{1,0:T(8,128)(2,1)S(1)} %get-tuple-element.12.refs_2_.packed_ref), custom_call_target="tpu_custom_call" | custom-call | flops 679477248 | bytes 4423680 | tf_op jit(solution)/shard_map/leaf_backward/pallas_call | solution.py:417
  45.9 0.0 copy-start.1
  45.9 0.5 collective-permute-done.other_ref
  46.4 2.4 %separator_tree.1 = bf16[8,32,256]{2,1,0:T(8,128)(2,1)S(1)} custom-call(s32[1]{0:T(128)} %bitcast.front_ref, bf16[8,80,256]{2,1,0:T(8,128)(2,1)S(1)} %all-to-all-done.1.got_ref, bf16[8,80,256]{2,1,0:T(8,128)(2,1)S(1)} %collective-permute-done.other_ref, f32[1152,256]{1,0:T(8,128)S(1)} %leaf_backward.1.bare_hbm.leaf_ref), custom_call_target="tpu_custom_call" | custom-call | flops 150994944 | bytes 786432 | tf_op jit(solution)/shard_map/separator_tree/pallas_call | solution.py:426
  48.8 7.8 %all_to_all.15.got_ref = bf16[8,32,256]{2,1,0:T(8,128)(2,1)S(1)} all-to-all(bf16[8,32,256]{2,1,0:T(8,128)(2,1)S(1)} %separator_tree.1), channel_id=1, replica_groups=mesh['tree'=8,'peer'=8,'front'=2] {'peer'}, dimensions={0} | all-to-all | bytes 262144 | tf_op jit(solution)/shard_map/all_to_all | solution.py:435
  56.6 0.0 copy-done.1
  56.6 1.4 %finish.1 = (f32[1152,256]{1,0:T(8,128)}, bf16[3,16,256]{2,1,0:T(8,128)(2,1)}) custom-call(bf16[8,32,256]{2,1,0:T(8,128)(2,1)S(1)} %all_to_all.15.got_ref, bf16[1152,256]{1,0:T(8,128)(2,1)S(1)} %copy-done.1, f32[1152,256]{1,0:T(8,128)S(1)} %leaf_backward.1.bare_hbm.leaf_ref), custom_call_target="tpu_custom_call" | custom-call | flops 150994944 | bytes 3080192 | tf_op jit(solution)/shard_map/finish/pallas_call | solution.py:437
  (2 shorter events, 0.0 us)
Async XLA Ops:
  0.6 15.2 %copy-start.9 = (s32[1,1,1152]{2,1,0:T(1,128)S(1)}, s32[1,1,1152]{2,1,0:T(1,128)}, u32[]{:S(2)}) copy-start(s32[1,1,1152]{2,1,0:T(1,128)} %param.12) | copy-start | bytes 13828
  0.6 15.5 %copy-start.4 = (bf16[1,1,3,16,256]{4,3,2,1,0:T(8,128)(2,1)S(1)}, bf16[1,1,3,16,256]{4,3,2,1,0:T(8,128)(2,1)}, u32[]{:S(2)}) copy-start(bf16[1,1,3,16,256]{4,3,2,1,0:T(8,128)(2,1)} %param.13) | copy-start | bytes 73732
  0.7 15.5 %copy-start.5 = (bf16[1,1,32,224]{3,2,1,0:T(8,128)(2,1)S(1)}, bf16[1,1,32,224]{3,2,1,0:T(8,128)(2,1)}, u32[]{:S(2)}) copy-start(bf16[1,1,32,224]{3,2,1,0:T(8,128)(2,1)} %param.17) | copy-start | bytes 43012
  0.7 15.5 %copy-start.6 = (bf16[1,1,3,64,16]{3,4,2,1,0:T(8,128)(2,1)S(1)}, bf16[1,1,3,64,16]{3,4,2,1,0:T(8,128)(2,1)}, u32[]{:S(2)}) copy-start(bf16[1,1,3,64,16]{3,4,2,1,0:T(8,128)(2,1)} %param.18) | copy-start | bytes 18436
  0.7 15.5 %copy-start.7 = (s32[1,1,3,64]{3,1,2,0:T(1,128)S(1)}, s32[1,1,3,64]{3,1,2,0:T(1,128)}, u32[]{:S(2)}) copy-start(s32[1,1,3,64]{3,1,2,0:T(1,128)} %param.16) | copy-start | bytes 2308
  0.7 15.5 %copy-start.8 = (s32[1,1,3,64]{3,1,2,0:T(1,128)S(1)}, s32[1,1,3,64]{3,1,2,0:T(1,128)}, u32[]{:S(2)}) copy-start(s32[1,1,3,64]{3,1,2,0:T(1,128)} %param.19) | copy-start | bytes 2308
  3.9 26.9 %all-to-all-start = ((bf16[64,24,256]{2,1,0:T(8,128)(2,1)}), bf16[64,24,256]{2,1,0:T(8,128)(2,1)S(1)}, u32[]{:S(2)}, u32[]{:S(2)}) async-start(bf16[64,24,256]{2,1,0:T(8,128)(2,1)} %bitcast.25), calls=%async_computation | async-start | bytes 1572864 | tf_op jit(solution)/shard_map/all_to_all | solution.py:359
  16.2 1.8 %copy-start.2 = (bf16[1,1,1152,1152]{3,2,1,0:T(8,128)(2,1)S(1)}, bf16[1,1,1152,1152]{3,2,1,0:T(8,128)(2,1)}, u32[]{:S(2)}) copy-start(bf16[1,1,1152,1152]{3,2,1,0:T(8,128)(2,1)} %param.14) | copy-start | bytes 7962628
  17.9 1.0 %copy-start.3 = (bf16[1,1,3,64,1152]{4,3,2,1,0:T(8,128)(2,1)S(1)}, bf16[1,1,3,64,1152]{4,3,2,1,0:T(8,128)(2,1)}, u32[]{:S(2)}) copy-start(bf16[1,1,3,64,1152]{4,3,2,1,0:T(8,128)(2,1)} %param.15) | copy-start | bytes 1327108
  21.6 0.8 %copy-start = (bf16[1152,256]{1,0:T(8,128)(2,1)}, bf16[1152,256]{1,0:T(8,128)(2,1)S(1)}, u32[]{:S(2)}) copy-start(bf16[1152,256]{1,0:T(8,128)(2,1)S(1)} %get-tuple-element.15.back_ref) | copy-start | bytes 1769476
  31.9 9.9 %all-to-all-start.1 = ((bf16[8,80,256]{2,1,0:T(8,128)(2,1)}), bf16[8,80,256]{2,1,0:T(8,128)(2,1)S(1)}, u32[]{:S(2)}, u32[]{:S(2)}) async-start(bf16[8,80,256]{2,1,0:T(8,128)(2,1)} %push_updates.1), calls=%async_computation.1 | async-start | bytes 655360 | tf_op jit(solution)/shard_map/all_to_all | solution.py:405
  41.8 4.5 %collective-permute-start = (bf16[8,80,256]{2,1,0:T(8,128)(2,1)S(1)}, bf16[8,80,256]{2,1,0:T(8,128)(2,1)S(1)}, u32[]{:S(2)}, u32[]{:S(2)}) collective-permute-start(bf16[8,80,256]{2,1,0:T(8,128)(2,1)S(1)} %all-to-all-done.1.got_ref), channel_id=1, source_target_pairs={{0,1},{1,0},{2,3},{3,2},{4,5},{5,4},{6,7},{7,6},{8,9},{9,8},{10,11... | collective-permute-start | bytes 983048 | tf_op jit(solution)/shard_map/ppermute | solution.py:415
  45.9 10.8 %copy-start.1 = (bf16[1152,256]{1,0:T(8,128)(2,1)S(1)}, bf16[1152,256]{1,0:T(8,128)(2,1)}, u32[]{:S(2)}) copy-start(bf16[1152,256]{1,0:T(8,128)(2,1)} %copy-done) | copy-start | bytes 1769476

commit v7 on v6

--- a/solution.py
+++ b/solution.py
@@ -60,8 +60,11 @@
     return copy
 
 
-def send_kernel(keep, pad, order_hbm, rhs_hbm, out_hbm, order_ref, rhs_ref, picked_ref, out_ref, sems):
+def send_kernel(
+    keep, tall, order_hbm, rhs_hbm, out_hbm, order_ref, rhs_ref, picked_ref, stage_ref, out_ref, sems
+):
     rows, width = rhs_ref.shape
+    half = width // 2
     order_in = fetch(order_hbm, order_ref, sems.at[0])
     rhs_in = fetch(rhs_hbm, rhs_ref, sems.at[1])
     tail = picked_ref.shape[0] - rows
@@ -76,11 +79,27 @@
         hots.append(jnp.concatenate(tiles, axis=1))
     rhs_in.wait()
     picked_ref[0:rows, :] = dot(jnp.concatenate(hots, axis=0), rhs_ref[...])
+    span = -(-keep // 8) * 8
     for owner in range(rows // keep):
-        out_ref[owner * pad : (owner + 1) * pad, :] = picked_ref[
-            owner * keep : owner * keep + pad, :
-        ].astype(BF)
+        source = slice(owner * keep, owner * keep + span)
+        base = owner * tall
+        stage_ref[base : base + span, :] = picked_ref[source, 0:half]
+        stage_ref[base + keep : base + keep + span, :] = picked_ref[source, half:width]
+    out_ref[...] = stage_ref[0 : out_ref.shape[0], :].astype(BF)
     fetch(out_ref, out_hbm, sems.at[2]).wait()
+
+
+def side_by_side(keep, tall, recv_ref, wide_ref):
+    sent = recv_ref.shape[0]
+    span = wide_ref.shape[0] - sent
+    wide_ref[0:sent, :] = recv_ref[...].astype(F32)
+    wide_ref[sent:, :] = jnp.zeros((span, wide_ref.shape[1]), F32)
+    rows = []
+    for base in range(0, sent, tall):
+        left = wide_ref[base : base + span, :]
+        right = wide_ref[base + keep : base + keep + span, :]
+        rows.append(jnp.concatenate([left, right], axis=1))
+    return jnp.concatenate(rows, axis=0).astype(BF)
 
 
 def column_cuts(leaf):
@@ -118,7 +137,7 @@
         move.wait()
     product = [dot(panels_ref[:, low:], inv_ref[low:, low:high]) for low, high, _ in cuts]
     product = jnp.concatenate(product, axis=1)
-    push_ref[...] = dot(product.astype(BF), spread).astype(BF)
+    push_ref[0:192, :] = dot(product.astype(BF), spread).astype(BF)
     padded = jnp.concatenate([product, jnp.zeros((256 - product.shape[0], leaf), F32)], axis=0)
     back_ref[...] = padded.T.astype(BF)
     cols = sinv_ref.shape[1]
@@ -139,8 +158,8 @@
         copy.wait()
 
 
-def push_kernel(recv_ref, push_ref, side_ref, out_ref):
-    sums = dot(push_ref[...], recv_ref[...])
+def push_kernel(keep, tall, recv_ref, push_ref, side_ref, out_ref, wide_ref):
+    sums = dot(push_ref[0:192, :], side_by_side(keep, tall, recv_ref, wide_ref))
     rows = jnp.concatenate([sums, side_ref[48:112, :].astype(F32)], axis=0)
     turned = rows.T.astype(BF)
     meta = side_ref[0:48, :]
@@ -149,10 +168,10 @@
         out_ref[peer, 32:80, :] = meta
 
 
-def forward_kernel(leaf, place_ref, recv_ref, packed_ref, y_ref):
+def forward_kernel(leaf, keep, tall, place_ref, recv_ref, packed_ref, y_ref, wide_ref):
     slots = place_ref.shape[1]
     spread = hot(row_ids(leaf, slots) == place_ref[...])
-    owned = dot(spread, recv_ref[...]).T.astype(BF)
+    owned = dot(spread, side_by_side(keep, tall, recv_ref, wide_ref)).T.astype(BF)
     cuts = column_cuts(leaf)
     y_t = []
     for low, high, _ in cuts:
@@ -336,20 +355,24 @@
     inv = leaf_inv[0, 0]
     panels = leaf_panels[0, 0].reshape(-1, leaf)
     keep = leaf // owners
-    pad = -(-keep // 8) * 8
-    slots = owners * pad
+    half = width // 2
+    tall = -(-2 * keep // 8) * 8
+    span = -(-keep // 8) * 8
+    slots = owners * span
+    wide = pltpu.VMEM((owners * tall + span, half), F32)
     sds = jax.ShapeDtypeStruct
 
     (sent,) = call(
-        lambda *refs: send_kernel(keep, pad, *refs),
+        lambda *refs: send_kernel(keep, tall, *refs),
         "send_rows",
         [HB, HB],
-        [(sds((slots, width), BF), HB)],
+        [(sds((owners * tall, half), BF), HB)],
         [
             pltpu.VMEM((1, leaf), jnp.int32),
             pltpu.VMEM((leaf, width), BF),
-            pltpu.VMEM((-(-(leaf - keep + pad) // 8) * 8 + 8, width), F32),
-            pltpu.VMEM((slots, width), BF),
+            pltpu.VMEM((leaf + 8, width), F32),
+            pltpu.VMEM((owners * tall + 8, half), F32),
+            pltpu.VMEM((owners * tall, half), BF),
             DMA((3,)),
         ],
         flops=2 * leaf * leaf * width,
@@ -357,11 +380,11 @@
         vmem=VMEM_ALL,
     )(send_order[0], rhs)
     recv = lax.all_to_all(
-        sent.reshape(owners, pad, width), ("tree", "peer"), split_axis=0, concat_axis=0, tiled=True
-    ).reshape(slots, width)
+        sent.reshape(owners, tall, half), ("tree", "peer"), split_axis=0, concat_axis=0, tiled=True
+    ).reshape(owners * tall, half)
 
     place = jnp.pad(
-        recv_place[0, 0].reshape(owners, keep), ((0, 0), (0, pad - keep)), constant_values=-1
+        recv_place[0, 0].reshape(owners, keep), ((0, 0), (0, span - keep)), constant_values=-1
     ).reshape(1, slots)
     span = jnp.swapaxes(sep_panels[0, 0], 1, 2)
     packed_rows = sum(leaf - low for low, _, _ in column_cuts(leaf))
@@ -370,7 +393,7 @@
         "factor_products",
         [VM, VM, VM, VM, HB, HB, HB, HB],
         [
-            (sds((192, slots), BF), VM),
+            (sds((320, slots), BF), VM),
             (sds((leaf, 256), BF), VM),
             (sds((112, 256), BF), VM),
             (sds((packed_rows, 256), BF), HB),
@@ -395,19 +418,21 @@
         sep_rhs[0, 0],
     )
     (chunks,) = call(
-        push_kernel,
+        lambda *refs: push_kernel(keep, tall, *refs),
         "push_updates",
         [VM, VM, VM],
         [(sds((TREE, 80, 256), BF), VM)],
+        [wide],
         flops=2 * 192 * slots * width,
         nbytes=2 * slots * (192 + width) + TREE * 80 * 512,
     )(recv, push, side)
     got = lax.all_to_all(chunks, "peer", split_axis=0, concat_axis=0, tiled=True)
     (leaf_y,) = call(
-        lambda *refs: forward_kernel(leaf, *refs),
+        lambda *refs: forward_kernel(leaf, keep, tall, *refs),
         "leaf_forward",
         [VM, VM, VM],
         [(sds((width, leaf), BF), VM)],
+        [wide],
         flops=2 * leaf * width * (leaf + slots),
         nbytes=2 * leaf * leaf + 4 * slots * width,
     )(place, recv, packed)

time: 58.7 us -> 57.3 us (0.976)
  waiting for transfers between devices: 12.7 us -> 11.3 us
    all_to_all x1, waiting for transfers between devices: 8.32 us -> 6.93 us  [on_device(): lax.all_to_all(sent.reshape(owners, tall, half), ('tree', 'peer'), split_...]
  transfers between devices with their start and end apart: 3 -> 3, of which waited for: 3 -> 3; matrix products, arithmetic and copies ran while one was open for 0% -> 0% of each run, Pallas kernels for 10% -> 11%
where the time goes in v7:
time: 57.3 us; the launch traced here: 56.7 us
  starting transfers between devices  18.7 us (33%)
  Pallas kernels  14.2 us (25%)
  waiting for transfers between devices  11.3 us (20%)
  blocking collectives  7.83 us (14%)
  local copies, waits for them, and re-layouts  3.83 us (7%)
  between operations  0.83 us (1%)
    all_to_all x1, starting transfers between devices, on_device(): lax.all_to_all(sent.reshape(owners, tall, half), ('tree', 'peer'), split_...  12 us
    all_to_all x1, blocking collectives, on_device(): lax.all_to_all(solved, 'peer', split_axis=0, concat_axis=0, tiled=True)  7.83 us
    all_to_all x1, waiting for transfers between devices, on_device(): lax.all_to_all(sent.reshape(owners, tall, half), ('tree', 'peer'), split_...  6.93 us
    all_to_all x1, waiting for transfers between devices, on_device(): lax.all_to_all(chunks, 'peer', split_axis=0, concat_axis=0, tiled=True)  3.92 us
    unnamed x20, local copies, waits for them, and re-layouts  3.6 us
    all_to_all x1, starting transfers between devices, on_device(): lax.all_to_all(chunks, 'peer', split_axis=0, concat_axis=0, tiled=True)  3.43 us
    ppermute x1, starting transfers between devices, on_device(): other = lax.ppermute(got, 'front', [(0, 1), (1, 0)])  3.26 us
    pallas_call x1, Pallas kernels, on_device(): call(lambda *refs: send_kernel(keep, tall, *refs), 'send_rows', [HB, HB],...  3.17 us
  transfers between devices with their start and end apart: 3, of which 3 were waited for; matrix products, arithmetic and copies ran while one was open for 0% of the time, Pallas kernels for 11%

profile of v7, /device:TPU:1, one launch (start us, length us, event | category | flops | bytes accessed | tf_op | source)
XLA Modules:
  0.0 56.7 jit_solution(12386591374148813890)
XLA Ops:
  0.6 0.0 copy-start.9
  0.6 0.0 copy-start.4
  0.7 0.0 copy-start.5
  0.7 0.0 copy-start.6
  0.7 0.0 copy-start.7
  0.7 0.0 copy-start.8
  0.7 3.2 %send_rows.1 = bf16[2560,128]{1,0:T(8,128)(2,1)} custom-call(s32[1,1152]{1,0:T(1,128)} %bitcast.29, bf16[1152,256]{1,0:T(8,128)(2,1)} %bitcast.27), custom_call_target="tpu_custom_call" | custom-call | flops 679477248 | bytes 1179648 | tf_op jit(solution)/shard_map/send_rows/pallas_call | solution.py:365
  3.9 12.0 %all-to-all-start = ((bf16[64,40,128]{2,1,0:T(8,128)(2,1)}), bf16[64,40,128]{2,1,0:T(8,128)(2,1)S(1)}, u32[]{:S(2)}, u32[]{:S(2)}) async-start(bf16[64,40,128]{2,1,0:T(8,128)(2,1)} %bitcast.25), calls=%async_computation | async-start | bytes 1310720 | tf_op jit(solution)/shard_map/all_to_all | solution.py:382
  15.9 0.0 copy-done.9
  15.9 0.1 reshape_squeeze.6
  16.0 0.1 reshape.19.place_ref.refs_0_
  16.1 0.0 copy-done.4
  16.1 0.0 copy-done.5
  16.2 0.0 copy-done.6
  16.2 0.0 copy-done.7
  16.2 0.0 copy-done.8
  16.2 0.0 copy-start.2
  16.2 1.7 %copy-done.2 = bf16[1,1,1152,1152]{3,2,1,0:T(8,128)(2,1)S(1)} copy-done((bf16[1,1,1152,1152]{3,2,1,0:T(8,128)(2,1)S(1)}, bf16[1,1,1152,1152]{3,2,1,0:T(8,128)(2,1)}, u32[]{:S(2)}) %copy-start.2) | copy-done | bytes 2654232
  17.9 0.0 copy-start.3
  17.9 1.0 %copy-done.3 = bf16[1,1,3,64,1152]{4,3,2,1,0:T(8,128)(2,1)S(1)} copy-done((bf16[1,1,3,64,1152]{4,3,2,1,0:T(8,128)(2,1)S(1)}, bf16[1,1,3,64,1152]{4,3,2,1,0:T(8,128)(2,1)}, u32[]{:S(2)}) %copy-start.3) | copy-done | bytes 442392
  18.9 2.7 %factor_products.1 = (bf16[320,1536]{1,0:T(8,128)(2,1)S(1)}, bf16[1152,256]{1,0:T(8,128)(2,1)S(1)}, bf16[112,256]{1,0:T(8,128)(2,1)S(1)}, bf16[3200,256]{1,0:T(8,128)(2,1)S(1)}) custom-call(s32[1,1536]{1,0:T(1,128)S(1)} %reshape.19.place_ref.refs_0_, s32[3,1,64]{2,1,0:T(1,128)S(1)} %bitcast.23, s32[3,1,64]{2,1,0:T(1,128)S(1)} %bitcast.24, ...), custom_call_target="tpu_custom_call" | custom-call | flops 1189085184 | bytes 3833856 | tf_op jit(solution)/shard_map/factor_products/pallas_call | solution.py:391
  21.6 0.0 copy-start
  21.6 0.8 %copy-done = bf16[1152,256]{1,0:T(8,128)(2,1)} copy-done((bf16[1152,256]{1,0:T(8,128)(2,1)}, bf16[1152,256]{1,0:T(8,128)(2,1)S(1)}, u32[]{:S(2)}) %copy-start) | copy-done | bytes 589848
  22.5 6.9 %all-to-all-done = bf16[64,40,128]{2,1,0:T(8,128)(2,1)S(1)} async-done(((bf16[64,40,128]{2,1,0:T(8,128)(2,1)}), bf16[64,40,128]{2,1,0:T(8,128)(2,1)S(1)}, u32[]{:S(2)}, u32[]{:S(2)}) %all-to-all-start) | async-done | bytes 655392 | tf_op jit(solution)/shard_map/all_to_all | solution.py:382
  29.4 1.2 %push_updates.1 = bf16[8,80,256]{2,1,0:T(8,128)(2,1)} custom-call(bf16[2560,128]{1,0:T(8,128)(2,1)S(1)} %bitcast.16, bf16[320,1536]{1,0:T(8,128)(2,1)S(1)} %get-tuple-element.10.refs_1_, bf16[112,256]{1,0:T(8,128)(2,1)S(1)} %get-tuple-element.11.refs_2_), custom_call_target="tpu_custom_call" | custom-call | flops 150994944 | bytes 1703936 | tf_op jit(solution)/shard_map/push_updates/pallas_call | solution.py:420
  30.6 3.4 %all-to-all-start.1 = ((bf16[8,80,256]{2,1,0:T(8,128)(2,1)}), bf16[8,80,256]{2,1,0:T(8,128)(2,1)S(1)}, u32[]{:S(2)}, u32[]{:S(2)}) async-start(bf16[8,80,256]{2,1,0:T(8,128)(2,1)} %push_updates.1), calls=%async_computation.1 | async-start | bytes 655360 | tf_op jit(solution)/shard_map/all_to_all | solution.py:429
  34.0 2.5 %leaf_forward.1.y_ref = bf16[256,1152]{1,0:T(8,128)(2,1)S(1)} custom-call(s32[1,1536]{1,0:T(1,128)S(1)} %reshape.19.place_ref.refs_0_, bf16[2560,128]{1,0:T(8,128)(2,1)S(1)} %bitcast.17, bf16[3200,256]{1,0:T(8,128)(2,1)S(1)} %get-tuple-element.12.refs_2_.packed_ref), custom_call_target="tpu_custom_call" | custom-call | flops 1585446912 | bytes 4227072 | tf_op jit(solution)/shard_map/leaf_forward/pallas_call | solution.py:430
  36.6 3.9 %all-to-all-done.1.got_ref = bf16[8,80,256]{2,1,0:T(8,128)(2,1)S(1)} async-done(((bf16[8,80,256]{2,1,0:T(8,128)(2,1)}), bf16[8,80,256]{2,1,0:T(8,128)(2,1)S(1)}, u32[]{:S(2)}, u32[]{:S(2)}) %all-to-all-start.1) | async-done | bytes 327712 | tf_op jit(solution)/shard_map/all_to_all | solution.py:429
  40.5 3.3 %collective-permute-start = (bf16[8,80,256]{2,1,0:T(8,128)(2,1)S(1)}, bf16[8,80,256]{2,1,0:T(8,128)(2,1)S(1)}, u32[]{:S(2)}, u32[]{:S(2)}) collective-permute-start(bf16[8,80,256]{2,1,0:T(8,128)(2,1)S(1)} %all-to-all-done.1.got_ref), channel_id=1, source_target_pairs={{0,1},{1,0},{2,3},{3,2},{4,5},{5,4},{6,7},{7,6},{8,9},{9,8},{10,11... | collective-permute-start | bytes 983048 | tf_op jit(solution)/shard_map/ppermute | solution.py:440
  43.7 0.8 %leaf_backward.1.bare_hbm.leaf_ref = f32[1152,256]{1,0:T(8,128)S(1)} custom-call(bf16[256,1152]{1,0:T(8,128)(2,1)S(1)} %leaf_forward.1.y_ref, bf16[3200,256]{1,0:T(8,128)(2,1)S(1)} %get-tuple-element.12.refs_2_.packed_ref), custom_call_target="tpu_custom_call" | custom-call | flops 679477248 | bytes 4423680 | tf_op jit(solution)/shard_map/leaf_backward/pallas_call | solution.py:442
  44.5 0.0 copy-start.1
  44.5 0.5 collective-permute-done.other_ref
  45.0 2.4 %separator_tree.1 = bf16[8,32,256]{2,1,0:T(8,128)(2,1)S(1)} custom-call(s32[1]{0:T(128)} %bitcast.front_ref, bf16[8,80,256]{2,1,0:T(8,128)(2,1)S(1)} %all-to-all-done.1.got_ref, bf16[8,80,256]{2,1,0:T(8,128)(2,1)S(1)} %collective-permute-done.other_ref, f32[1152,256]{1,0:T(8,128)S(1)} %leaf_backward.1.bare_hbm.leaf_ref), custom_call_target="tpu_custom_call" | custom-call | flops 150994944 | bytes 786432 | tf_op jit(solution)/shard_map/separator_tree/pallas_call | solution.py:451
  47.5 7.8 %all_to_all.15.got_ref = bf16[8,32,256]{2,1,0:T(8,128)(2,1)S(1)} all-to-all(bf16[8,32,256]{2,1,0:T(8,128)(2,1)S(1)} %separator_tree.1), channel_id=1, replica_groups=mesh['tree'=8,'peer'=8,'front'=2] {'peer'}, dimensions={0} | all-to-all | bytes 262144 | tf_op jit(solution)/shard_map/all_to_all | solution.py:460
  55.3 0.0 copy-done.1
  55.3 1.4 %finish.1 = (f32[1152,256]{1,0:T(8,128)}, bf16[3,16,256]{2,1,0:T(8,128)(2,1)}) custom-call(bf16[8,32,256]{2,1,0:T(8,128)(2,1)S(1)} %all_to_all.15.got_ref, bf16[1152,256]{1,0:T(8,128)(2,1)S(1)} %copy-done.1, f32[1152,256]{1,0:T(8,128)S(1)} %leaf_backward.1.bare_hbm.leaf_ref), custom_call_target="tpu_custom_call" | custom-call | flops 150994944 | bytes 3080192 | tf_op jit(solution)/shard_map/finish/pallas_call | solution.py:462
  (2 shorter events, 0.0 us)
Async XLA Ops:
  0.6 15.2 %copy-start.9 = (s32[1,1,1152]{2,1,0:T(1,128)S(1)}, s32[1,1,1152]{2,1,0:T(1,128)}, u32[]{:S(2)}) copy-start(s32[1,1,1152]{2,1,0:T(1,128)} %param.12) | copy-start | bytes 13828
  0.6 15.5 %copy-start.4 = (bf16[1,1,3,16,256]{4,3,2,1,0:T(8,128)(2,1)S(1)}, bf16[1,1,3,16,256]{4,3,2,1,0:T(8,128)(2,1)}, u32[]{:S(2)}) copy-start(bf16[1,1,3,16,256]{4,3,2,1,0:T(8,128)(2,1)} %param.13) | copy-start | bytes 73732
  0.7 15.5 %copy-start.5 = (bf16[1,1,32,224]{3,2,1,0:T(8,128)(2,1)S(1)}, bf16[1,1,32,224]{3,2,1,0:T(8,128)(2,1)}, u32[]{:S(2)}) copy-start(bf16[1,1,32,224]{3,2,1,0:T(8,128)(2,1)} %param.17) | copy-start | bytes 43012
  0.7 15.5 %copy-start.6 = (bf16[1,1,3,64,16]{3,4,2,1,0:T(8,128)(2,1)S(1)}, bf16[1,1,3,64,16]{3,4,2,1,0:T(8,128)(2,1)}, u32[]{:S(2)}) copy-start(bf16[1,1,3,64,16]{3,4,2,1,0:T(8,128)(2,1)} %param.18) | copy-start | bytes 18436
  0.7 15.5 %copy-start.7 = (s32[1,1,3,64]{3,1,2,0:T(1,128)S(1)}, s32[1,1,3,64]{3,1,2,0:T(1,128)}, u32[]{:S(2)}) copy-start(s32[1,1,3,64]{3,1,2,0:T(1,128)} %param.16) | copy-start | bytes 2308
  0.7 15.5 %copy-start.8 = (s32[1,1,3,64]{3,1,2,0:T(1,128)S(1)}, s32[1,1,3,64]{3,1,2,0:T(1,128)}, u32[]{:S(2)}) copy-start(s32[1,1,3,64]{3,1,2,0:T(1,128)} %param.19) | copy-start | bytes 2308
  3.9 25.5 %all-to-all-start = ((bf16[64,40,128]{2,1,0:T(8,128)(2,1)}), bf16[64,40,128]{2,1,0:T(8,128)(2,1)S(1)}, u32[]{:S(2)}, u32[]{:S(2)}) async-start(bf16[64,40,128]{2,1,0:T(8,128)(2,1)} %bitcast.25), calls=%async_computation | async-start | bytes 1310720 | tf_op jit(solution)/shard_map/all_to_all | solution.py:382
  16.2 1.8 %copy-start.2 = (bf16[1,1,1152,1152]{3,2,1,0:T(8,128)(2,1)S(1)}, bf16[1,1,1152,1152]{3,2,1,0:T(8,128)(2,1)}, u32[]{:S(2)}) copy-start(bf16[1,1,1152,1152]{3,2,1,0:T(8,128)(2,1)} %param.14) | copy-start | bytes 7962628
  17.9 1.0 %copy-start.3 = (bf16[1,1,3,64,1152]{4,3,2,1,0:T(8,128)(2,1)S(1)}, bf16[1,1,3,64,1152]{4,3,2,1,0:T(8,128)(2,1)}, u32[]{:S(2)}) copy-start(bf16[1,1,3,64,1152]{4,3,2,1,0:T(8,128)(2,1)} %param.15) | copy-start | bytes 1327108
  21.6 0.8 %copy-start = (bf16[1152,256]{1,0:T(8,128)(2,1)}, bf16[1152,256]{1,0:T(8,128)(2,1)S(1)}, u32[]{:S(2)}) copy-start(bf16[1152,256]{1,0:T(8,128)(2,1)S(1)} %get-tuple-element.15.back_ref) | copy-start | bytes 1769476
  30.6 9.9 %all-to-all-start.1 = ((bf16[8,80,256]{2,1,0:T(8,128)(2,1)}), bf16[8,80,256]{2,1,0:T(8,128)(2,1)S(1)}, u32[]{:S(2)}, u32[]{:S(2)}) async-start(bf16[8,80,256]{2,1,0:T(8,128)(2,1)} %push_updates.1), calls=%async_computation.1 | async-start | bytes 655360 | tf_op jit(solution)/shard_map/all_to_all | solution.py:429
  40.5 4.5 %collective-permute-start = (bf16[8,80,256]{2,1,0:T(8,128)(2,1)S(1)}, bf16[8,80,256]{2,1,0:T(8,128)(2,1)S(1)}, u32[]{:S(2)}, u32[]{:S(2)}) collective-permute-start(bf16[8,80,256]{2,1,0:T(8,128)(2,1)S(1)} %all-to-all-done.1.got_ref), channel_id=1, source_target_pairs={{0,1},{1,0},{2,3},{3,2},{4,5},{5,4},{6,7},{7,6},{8,9},{9,8},{10,11... | collective-permute-start | bytes 983048 | tf_op jit(solution)/shard_map/ppermute | solution.py:440
  44.5 10.8 %copy-start.1 = (bf16[1152,256]{1,0:T(8,128)(2,1)S(1)}, bf16[1152,256]{1,0:T(8,128)(2,1)}, u32[]{:S(2)}) copy-start(bf16[1152,256]{1,0:T(8,128)(2,1)} %copy-done) | copy-start | bytes 1769476

commit v8 on v7

--- a/solution.py
+++ b/solution.py
@@ -356,7 +356,7 @@
     panels = leaf_panels[0, 0].reshape(-1, leaf)
     keep = leaf // owners
     half = width // 2
-    tall = -(-2 * keep // 8) * 8
+    tall = 2 * keep
     span = -(-keep // 8) * 8
     slots = owners * span
     wide = pltpu.VMEM((owners * tall + span, half), F32)
@@ -380,7 +380,7 @@
         vmem=VMEM_ALL,
     )(send_order[0], rhs)
     recv = lax.all_to_all(
-        sent.reshape(owners, tall, half), ("tree", "peer"), split_axis=0, concat_axis=0, tiled=True
+        sent.reshape(owners, tall // 4, 4, half), ("tree", "peer"), split_axis=0, concat_axis=0, tiled=True
     ).reshape(owners * tall, half)
 
     place = jnp.pad(

time: 57.3 us -> 56.6 us (0.988)
  waiting for transfers between devices: 11.3 us -> 10.6 us
    all_to_all x1, waiting for transfers between devices: 6.93 us -> 6.23 us  [on_device(): lax.all_to_all(sent.reshape(owners, tall // 4, 4, half), ('tree', 'peer')...]
where the time goes in v8:
time: 56.6 us; the launch traced here: 55.9 us
  starting transfers between devices  18.7 us (33%)
  Pallas kernels  14.2 us (25%)
  waiting for transfers between devices  10.6 us (19%)
  blocking collectives  7.83 us (14%)
  local copies, waits for them, and re-layouts  3.83 us (7%)
  between operations  0.83 us (1%)
    all_to_all x1, starting transfers between devices, on_device(): lax.all_to_all(sent.reshape(owners, tall // 4, 4, half), ('tree', 'peer')...  12 us
    all_to_all x1, blocking collectives, on_device(): lax.all_to_all(solved, 'peer', split_axis=0, concat_axis=0, tiled=True)  7.83 us
    all_to_all x1, waiting for transfers between devices, on_device(): lax.all_to_all(sent.reshape(owners, tall // 4, 4, half), ('tree', 'peer')...  6.23 us
    all_to_all x1, waiting for transfers between devices, on_device(): lax.all_to_all(chunks, 'peer', split_axis=0, concat_axis=0, tiled=True)  3.92 us
    unnamed x20, local copies, waits for them, and re-layouts  3.6 us
    all_to_all x1, starting transfers between devices, on_device(): lax.all_to_all(chunks, 'peer', split_axis=0, concat_axis=0, tiled=True)  3.43 us
    ppermute x1, starting transfers between devices, on_device(): other = lax.ppermute(got, 'front', [(0, 1), (1, 0)])  3.26 us
    pallas_call x1, Pallas kernels, on_device(): call(lambda *refs: send_kernel(keep, tall, *refs), 'send_rows', [HB, HB],...  3.14 us
  transfers between devices with their start and end apart: 3, of which 3 were waited for; matrix products, arithmetic and copies ran while one was open for 0% of the time, Pallas kernels for 11%

profile of v8, /device:TPU:1, one launch (start us, length us, event | category | flops | bytes accessed | tf_op | source)
XLA Modules:
  0.0 55.9 jit_solution(8362593343099605652)
XLA Ops:
  0.6 0.0 copy-start.9
  0.6 0.0 copy-start.4
  0.7 0.0 copy-start.5
  0.7 0.0 copy-start.6
  0.7 0.0 copy-start.7
  0.7 0.0 copy-start.8
  0.7 3.1 %send_rows.1 = bf16[2304,128]{1,0:T(8,128)(2,1)} custom-call(s32[1,1152]{1,0:T(1,128)} %bitcast.29, bf16[1152,256]{1,0:T(8,128)(2,1)} %bitcast.27), custom_call_target="tpu_custom_call" | custom-call | flops 679477248 | bytes 1179648 | tf_op jit(solution)/shard_map/send_rows/pallas_call | solution.py:365
  3.8 12.0 %all-to-all-start = ((bf16[64,9,4,128]{3,2,1,0:T(4,128)(2,1)}), bf16[64,9,4,128]{3,2,1,0:T(4,128)(2,1)S(1)}, u32[]{:S(2)}, u32[]{:S(2)}) async-start(bf16[64,9,4,128]{3,2,1,0:T(4,128)(2,1)} %bitcast.25), calls=%async_computation | async-start | bytes 1179648 | tf_op jit(solution)/shard_map/all_to_all | solution.py:382
  15.8 0.0 copy-done.9
  15.9 0.1 reshape_squeeze.6
  16.0 0.1 reshape.19.place_ref.refs_0_
  16.1 0.0 copy-done.4
  16.1 0.0 copy-done.5
  16.1 0.0 copy-done.6
  16.1 0.0 copy-done.7
  16.1 0.0 copy-done.8
  16.2 0.0 copy-start.2
  16.2 1.7 %copy-done.2 = bf16[1,1,1152,1152]{3,2,1,0:T(8,128)(2,1)S(1)} copy-done((bf16[1,1,1152,1152]{3,2,1,0:T(8,128)(2,1)S(1)}, bf16[1,1,1152,1152]{3,2,1,0:T(8,128)(2,1)}, u32[]{:S(2)}) %copy-start.2) | copy-done | bytes 2654232
  17.9 0.0 copy-start.3
  17.9 1.0 %copy-done.3 = bf16[1,1,3,64,1152]{4,3,2,1,0:T(8,128)(2,1)S(1)} copy-done((bf16[1,1,3,64,1152]{4,3,2,1,0:T(8,128)(2,1)S(1)}, bf16[1,1,3,64,1152]{4,3,2,1,0:T(8,128)(2,1)}, u32[]{:S(2)}) %copy-start.3) | copy-done | bytes 442392
  18.9 2.7 %factor_products.1 = (bf16[320,1536]{1,0:T(8,128)(2,1)S(1)}, bf16[1152,256]{1,0:T(8,128)(2,1)S(1)}, bf16[112,256]{1,0:T(8,128)(2,1)S(1)}, bf16[3200,256]{1,0:T(8,128)(2,1)S(1)}) custom-call(s32[1,1536]{1,0:T(1,128)S(1)} %reshape.19.place_ref.refs_0_, s32[3,1,64]{2,1,0:T(1,128)S(1)} %bitcast.23, s32[3,1,64]{2,1,0:T(1,128)S(1)} %bitcast.24, ...), custom_call_target="tpu_custom_call" | custom-call | flops 1189085184 | bytes 3833856 | tf_op jit(solution)/shard_map/factor_products/pallas_call | solution.py:391
  21.6 0.0 copy-start
  21.6 0.8 %copy-done = bf16[1152,256]{1,0:T(8,128)(2,1)} copy-done((bf16[1152,256]{1,0:T(8,128)(2,1)}, bf16[1152,256]{1,0:T(8,128)(2,1)S(1)}, u32[]{:S(2)}) %copy-start) | copy-done | bytes 589848
  22.4 6.2 %all-to-all-done = bf16[64,9,4,128]{3,2,1,0:T(4,128)(2,1)S(1)} async-done(((bf16[64,9,4,128]{3,2,1,0:T(4,128)(2,1)}), bf16[64,9,4,128]{3,2,1,0:T(4,128)(2,1)S(1)}, u32[]{:S(2)}, u32[]{:S(2)}) %all-to-all-start) | async-done | bytes 589856 | tf_op jit(solution)/shard_map/all_to_all | solution.py:382
  28.7 1.2 %push_updates.1 = bf16[8,80,256]{2,1,0:T(8,128)(2,1)} custom-call(bf16[2304,128]{1,0:T(8,128)(2,1)S(1)} %bitcast.16, bf16[320,1536]{1,0:T(8,128)(2,1)S(1)} %get-tuple-element.10.refs_1_, bf16[112,256]{1,0:T(8,128)(2,1)S(1)} %get-tuple-element.11.refs_2_), custom_call_target="tpu_custom_call" | custom-call | flops 150994944 | bytes 1703936 | tf_op jit(solution)/shard_map/push_updates/pallas_call | solution.py:420
  29.8 3.4 %all-to-all-start.1 = ((bf16[8,80,256]{2,1,0:T(8,128)(2,1)}), bf16[8,80,256]{2,1,0:T(8,128)(2,1)S(1)}, u32[]{:S(2)}, u32[]{:S(2)}) async-start(bf16[8,80,256]{2,1,0:T(8,128)(2,1)} %push_updates.1), calls=%async_computation.1 | async-start | bytes 655360 | tf_op jit(solution)/shard_map/all_to_all | solution.py:429
  33.3 2.6 %leaf_forward.1.y_ref = bf16[256,1152]{1,0:T(8,128)(2,1)S(1)} custom-call(s32[1,1536]{1,0:T(1,128)S(1)} %reshape.19.place_ref.refs_0_, bf16[2304,128]{1,0:T(8,128)(2,1)S(1)} %bitcast.17, bf16[3200,256]{1,0:T(8,128)(2,1)S(1)} %get-tuple-element.12.refs_2_.packed_ref), custom_call_target="tpu_custom_call" | custom-call | flops 1585446912 | bytes 4227072 | tf_op jit(solution)/shard_map/leaf_forward/pallas_call | solution.py:430
  35.8 3.9 %all-to-all-done.1.got_ref = bf16[8,80,256]{2,1,0:T(8,128)(2,1)S(1)} async-done(((bf16[8,80,256]{2,1,0:T(8,128)(2,1)}), bf16[8,80,256]{2,1,0:T(8,128)(2,1)S(1)}, u32[]{:S(2)}, u32[]{:S(2)}) %all-to-all-start.1) | async-done | bytes 327712 | tf_op jit(solution)/shard_map/all_to_all | solution.py:429
  39.8 3.3 %collective-permute-start = (bf16[8,80,256]{2,1,0:T(8,128)(2,1)S(1)}, bf16[8,80,256]{2,1,0:T(8,128)(2,1)S(1)}, u32[]{:S(2)}, u32[]{:S(2)}) collective-permute-start(bf16[8,80,256]{2,1,0:T(8,128)(2,1)S(1)} %all-to-all-done.1.got_ref), channel_id=1, source_target_pairs={{0,1},{1,0},{2,3},{3,2},{4,5},{5,4},{6,7},{7,6},{8,9},{9,8},{10,11... | collective-permute-start | bytes 983048 | tf_op jit(solution)/shard_map/ppermute | solution.py:440
  43.0 0.8 %leaf_backward.1.bare_hbm.leaf_ref = f32[1152,256]{1,0:T(8,128)S(1)} custom-call(bf16[256,1152]{1,0:T(8,128)(2,1)S(1)} %leaf_forward.1.y_ref, bf16[3200,256]{1,0:T(8,128)(2,1)S(1)} %get-tuple-element.12.refs_2_.packed_ref), custom_call_target="tpu_custom_call" | custom-call | flops 679477248 | bytes 4423680 | tf_op jit(solution)/shard_map/leaf_backward/pallas_call | solution.py:442
  43.8 0.0 copy-start.1
  43.8 0.5 collective-permute-done.other_ref
  44.3 2.4 %separator_tree.1 = bf16[8,32,256]{2,1,0:T(8,128)(2,1)S(1)} custom-call(s32[1]{0:T(128)} %bitcast.front_ref, bf16[8,80,256]{2,1,0:T(8,128)(2,1)S(1)} %all-to-all-done.1.got_ref, bf16[8,80,256]{2,1,0:T(8,128)(2,1)S(1)} %collective-permute-done.other_ref, f32[1152,256]{1,0:T(8,128)S(1)} %leaf_backward.1.bare_hbm.leaf_ref), custom_call_target="tpu_custom_call" | custom-call | flops 150994944 | bytes 786432 | tf_op jit(solution)/shard_map/separator_tree/pallas_call | solution.py:451
  46.7 7.8 %all_to_all.15.got_ref = bf16[8,32,256]{2,1,0:T(8,128)(2,1)S(1)} all-to-all(bf16[8,32,256]{2,1,0:T(8,128)(2,1)S(1)} %separator_tree.1), channel_id=1, replica_groups=mesh['tree'=8,'peer'=8,'front'=2] {'peer'}, dimensions={0} | all-to-all | bytes 262144 | tf_op jit(solution)/shard_map/all_to_all | solution.py:460
  54.6 0.0 copy-done.1
  54.6 1.4 %finish.1 = (f32[1152,256]{1,0:T(8,128)}, bf16[3,16,256]{2,1,0:T(8,128)(2,1)}) custom-call(bf16[8,32,256]{2,1,0:T(8,128)(2,1)S(1)} %all_to_all.15.got_ref, bf16[1152,256]{1,0:T(8,128)(2,1)S(1)} %copy-done.1, f32[1152,256]{1,0:T(8,128)S(1)} %leaf_backward.1.bare_hbm.leaf_ref), custom_call_target="tpu_custom_call" | custom-call | flops 150994944 | bytes 3080192 | tf_op jit(solution)/shard_map/finish/pallas_call | solution.py:462
  (2 shorter events, 0.0 us)
Async XLA Ops:
  0.6 15.2 %copy-start.9 = (s32[1,1,1152]{2,1,0:T(1,128)S(1)}, s32[1,1,1152]{2,1,0:T(1,128)}, u32[]{:S(2)}) copy-start(s32[1,1,1152]{2,1,0:T(1,128)} %param.12) | copy-start | bytes 13828
  0.6 15.5 %copy-start.4 = (bf16[1,1,3,16,256]{4,3,2,1,0:T(8,128)(2,1)S(1)}, bf16[1,1,3,16,256]{4,3,2,1,0:T(8,128)(2,1)}, u32[]{:S(2)}) copy-start(bf16[1,1,3,16,256]{4,3,2,1,0:T(8,128)(2,1)} %param.13) | copy-start | bytes 73732
  0.7 15.5 %copy-start.5 = (bf16[1,1,32,224]{3,2,1,0:T(8,128)(2,1)S(1)}, bf16[1,1,32,224]{3,2,1,0:T(8,128)(2,1)}, u32[]{:S(2)}) copy-start(bf16[1,1,32,224]{3,2,1,0:T(8,128)(2,1)} %param.17) | copy-start | bytes 43012
  0.7 15.5 %copy-start.6 = (bf16[1,1,3,64,16]{3,4,2,1,0:T(8,128)(2,1)S(1)}, bf16[1,1,3,64,16]{3,4,2,1,0:T(8,128)(2,1)}, u32[]{:S(2)}) copy-start(bf16[1,1,3,64,16]{3,4,2,1,0:T(8,128)(2,1)} %param.18) | copy-start | bytes 18436
  0.7 15.5 %copy-start.7 = (s32[1,1,3,64]{3,1,2,0:T(1,128)S(1)}, s32[1,1,3,64]{3,1,2,0:T(1,128)}, u32[]{:S(2)}) copy-start(s32[1,1,3,64]{3,1,2,0:T(1,128)} %param.16) | copy-start | bytes 2308
  0.7 15.5 %copy-start.8 = (s32[1,1,3,64]{3,1,2,0:T(1,128)S(1)}, s32[1,1,3,64]{3,1,2,0:T(1,128)}, u32[]{:S(2)}) copy-start(s32[1,1,3,64]{3,1,2,0:T(1,128)} %param.19) | copy-start | bytes 2308
  3.8 24.8 %all-to-all-start = ((bf16[64,9,4,128]{3,2,1,0:T(4,128)(2,1)}), bf16[64,9,4,128]{3,2,1,0:T(4,128)(2,1)S(1)}, u32[]{:S(2)}, u32[]{:S(2)}) async-start(bf16[64,9,4,128]{3,2,1,0:T(4,128)(2,1)} %bitcast.25), calls=%async_computation | async-start | bytes 1179648 | tf_op jit(solution)/shard_map/all_to_all | solution.py:382
  16.2 1.8 %copy-start.2 = (bf16[1,1,1152,1152]{3,2,1,0:T(8,128)(2,1)S(1)}, bf16[1,1,1152,1152]{3,2,1,0:T(8,128)(2,1)}, u32[]{:S(2)}) copy-start(bf16[1,1,1152,1152]{3,2,1,0:T(8,128)(2,1)} %param.14) | copy-start | bytes 7962628
  17.9 1.0 %copy-start.3 = (bf16[1,1,3,64,1152]{4,3,2,1,0:T(8,128)(2,1)S(1)}, bf16[1,1,3,64,1152]{4,3,2,1,0:T(8,128)(2,1)}, u32[]{:S(2)}) copy-start(bf16[1,1,3,64,1152]{4,3,2,1,0:T(8,128)(2,1)} %param.15) | copy-start | bytes 1327108
  21.6 0.8 %copy-start = (bf16[1152,256]{1,0:T(8,128)(2,1)}, bf16[1152,256]{1,0:T(8,128)(2,1)S(1)}, u32[]{:S(2)}) copy-start(bf16[1152,256]{1,0:T(8,128)(2,1)S(1)} %get-tuple-element.15.back_ref) | copy-start | bytes 1769476
  29.8 9.9 %all-to-all-start.1 = ((bf16[8,80,256]{2,1,0:T(8,128)(2,1)}), bf16[8,80,256]{2,1,0:T(8,128)(2,1)S(1)}, u32[]{:S(2)}, u32[]{:S(2)}) async-start(bf16[8,80,256]{2,1,0:T(8,128)(2,1)} %push_updates.1), calls=%async_computation.1 | async-start | bytes 655360 | tf_op jit(solution)/shard_map/all_to_all | solution.py:429
  39.8 4.5 %collective-permute-start = (bf16[8,80,256]{2,1,0:T(8,128)(2,1)S(1)}, bf16[8,80,256]{2,1,0:T(8,128)(2,1)S(1)}, u32[]{:S(2)}, u32[]{:S(2)}) collective-permute-start(bf16[8,80,256]{2,1,0:T(8,128)(2,1)S(1)} %all-to-all-done.1.got_ref), channel_id=1, source_target_pairs={{0,1},{1,0},{2,3},{3,2},{4,5},{5,4},{6,7},{7,6},{8,9},{9,8},{10,11... | collective-permute-start | bytes 983048 | tf_op jit(solution)/shard_map/ppermute | solution.py:440
  43.8 10.8 %copy-start.1 = (bf16[1152,256]{1,0:T(8,128)(2,1)S(1)}, bf16[1152,256]{1,0:T(8,128)(2,1)}, u32[]{:S(2)}) copy-start(bf16[1152,256]{1,0:T(8,128)(2,1)} %copy-done) | copy-start | bytes 1769476

commit v9 on v8

--- a/solution.py
+++ b/solution.py
@@ -139,7 +139,7 @@
     product = jnp.concatenate(product, axis=1)
     push_ref[0:192, :] = dot(product.astype(BF), spread).astype(BF)
     padded = jnp.concatenate([product, jnp.zeros((256 - product.shape[0], leaf), F32)], axis=0)
-    back_ref[...] = padded.T.astype(BF)
+    back_ref[...] = padded.astype(BF).T
     cols = sinv_ref.shape[1]
     lane = lane_ids(cols, 256)
     source = jnp.where(
@@ -161,7 +161,7 @@
 def push_kernel(keep, tall, recv_ref, push_ref, side_ref, out_ref, wide_ref):
     sums = dot(push_ref[0:192, :], side_by_side(keep, tall, recv_ref, wide_ref))
     rows = jnp.concatenate([sums, side_ref[48:112, :].astype(F32)], axis=0)
-    turned = rows.T.astype(BF)
+    turned = rows.astype(BF).T
     meta = side_ref[0:48, :]
     for peer in range(TREE):
         out_ref[peer, 0:32, :] = turned[peer * COLS : (peer + 1) * COLS, :]
@@ -171,7 +171,7 @@
 def forward_kernel(leaf, keep, tall, place_ref, recv_ref, packed_ref, y_ref, wide_ref):
     slots = place_ref.shape[1]
     spread = hot(row_ids(leaf, slots) == place_ref[...])
-    owned = dot(spread, side_by_side(keep, tall, recv_ref, wide_ref)).T.astype(BF)
+    owned = dot(spread, side_by_side(keep, tall, recv_ref, wide_ref)).astype(BF).T
     cuts = column_cuts(leaf)
     y_t = []
     for low, high, _ in cuts:

time: 56.6 us -> 56.6 us (level)
  no operation moved by 1% of the time
where the time goes in v9:
time: 56.6 us; the launch traced here: 55.9 us
  starting transfers between devices  18.7 us (33%)
  Pallas kernels  14.1 us (25%)
  waiting for transfers between devices  10.6 us (19%)
  blocking collectives  7.83 us (14%)
  local copies, waits for them, and re-layouts  3.83 us (7%)
  between operations  0.83 us (1%)
    all_to_all x1, starting transfers between devices, on_device(): lax.all_to_all(sent.reshape(owners, tall // 4, 4, half), ('tree', 'peer')...  12 us
    all_to_all x1, blocking collectives, on_device(): lax.all_to_all(solved, 'peer', split_axis=0, concat_axis=0, tiled=True)  7.83 us
    all_to_all x1, waiting for transfers between devices, on_device(): lax.all_to_all(sent.reshape(owners, tall // 4, 4, half), ('tree', 'peer')...  6.23 us
    all_to_all x1, waiting for transfers between devices, on_device(): lax.all_to_all(chunks, 'peer', split_axis=0, concat_axis=0, tiled=True)  3.93 us
    unnamed x20, local copies, waits for them, and re-layouts  3.6 us
    all_to_all x1, starting transfers between devices, on_device(): lax.all_to_all(chunks, 'peer', split_axis=0, concat_axis=0, tiled=True)  3.43 us
    ppermute x1, starting transfers between devices, on_device(): other = lax.ppermute(got, 'front', [(0, 1), (1, 0)])  3.26 us
    pallas_call x1, Pallas kernels, on_device(): call(lambda *refs: send_kernel(keep, tall, *refs), 'send_rows', [HB, HB],...  3.14 us
  transfers between devices with their start and end apart: 3, of which 3 were waited for; matrix products, arithmetic and copies ran while one was open for 0% of the time, Pallas kernels for 11%

profile of v9, /device:TPU:1, one launch (start us, length us, event | category | flops | bytes accessed | tf_op | source)
XLA Modules:
  0.0 55.9 jit_solution(11309512055726682759)
XLA Ops:
  0.6 0.0 copy-start.9
  0.6 0.0 copy-start.4
  0.7 0.0 copy-start.5
  0.7 0.0 copy-start.6
  0.7 0.0 copy-start.7
  0.7 0.0 copy-start.8
  0.7 3.1 %send_rows.1 = bf16[2304,128]{1,0:T(8,128)(2,1)} custom-call(s32[1,1152]{1,0:T(1,128)} %bitcast.29, bf16[1152,256]{1,0:T(8,128)(2,1)} %bitcast.27), custom_call_target="tpu_custom_call" | custom-call | flops 679477248 | bytes 1179648 | tf_op jit(solution)/shard_map/send_rows/pallas_call | solution.py:365
  3.8 12.0 %all-to-all-start = ((bf16[64,9,4,128]{3,2,1,0:T(4,128)(2,1)}), bf16[64,9,4,128]{3,2,1,0:T(4,128)(2,1)S(1)}, u32[]{:S(2)}, u32[]{:S(2)}) async-start(bf16[64,9,4,128]{3,2,1,0:T(4,128)(2,1)} %bitcast.25), calls=%async_computation | async-start | bytes 1179648 | tf_op jit(solution)/shard_map/all_to_all | solution.py:382
  15.8 0.0 copy-done.9
  15.9 0.1 reshape_squeeze.6
  16.0 0.1 reshape.19.place_ref.refs_0_
  16.1 0.0 copy-done.4
  16.1 0.0 copy-done.5
  16.1 0.0 copy-done.6
  16.1 0.0 copy-done.7
  16.1 0.0 copy-done.8
  16.2 0.0 copy-start.2
  16.2 1.7 %copy-done.2 = bf16[1,1,1152,1152]{3,2,1,0:T(8,128)(2,1)S(1)} copy-done((bf16[1,1,1152,1152]{3,2,1,0:T(8,128)(2,1)S(1)}, bf16[1,1,1152,1152]{3,2,1,0:T(8,128)(2,1)}, u32[]{:S(2)}) %copy-start.2) | copy-done | bytes 2654232
  17.9 0.0 copy-start.3
  17.9 1.0 %copy-done.3 = bf16[1,1,3,64,1152]{4,3,2,1,0:T(8,128)(2,1)S(1)} copy-done((bf16[1,1,3,64,1152]{4,3,2,1,0:T(8,128)(2,1)S(1)}, bf16[1,1,3,64,1152]{4,3,2,1,0:T(8,128)(2,1)}, u32[]{:S(2)}) %copy-start.3) | copy-done | bytes 442392
  18.9 2.7 %factor_products.1 = (bf16[320,1536]{1,0:T(8,128)(2,1)S(1)}, bf16[1152,256]{1,0:T(8,128)(2,1)S(1)}, bf16[112,256]{1,0:T(8,128)(2,1)S(1)}, bf16[3200,256]{1,0:T(8,128)(2,1)S(1)}) custom-call(s32[1,1536]{1,0:T(1,128)S(1)} %reshape.19.place_ref.refs_0_, s32[3,1,64]{2,1,0:T(1,128)S(1)} %bitcast.23, s32[3,1,64]{2,1,0:T(1,128)S(1)} %bitcast.24, ...), custom_call_target="tpu_custom_call" | custom-call | flops 1189085184 | bytes 3833856 | tf_op jit(solution)/shard_map/factor_products/pallas_call | solution.py:391
  21.6 0.0 copy-start
  21.6 0.8 %copy-done = bf16[1152,256]{1,0:T(8,128)(2,1)} copy-done((bf16[1152,256]{1,0:T(8,128)(2,1)}, bf16[1152,256]{1,0:T(8,128)(2,1)S(1)}, u32[]{:S(2)}) %copy-start) | copy-done | bytes 589848
  22.4 6.2 %all-to-all-done = bf16[64,9,4,128]{3,2,1,0:T(4,128)(2,1)S(1)} async-done(((bf16[64,9,4,128]{3,2,1,0:T(4,128)(2,1)}), bf16[64,9,4,128]{3,2,1,0:T(4,128)(2,1)S(1)}, u32[]{:S(2)}, u32[]{:S(2)}) %all-to-all-start) | async-done | bytes 589856 | tf_op jit(solution)/shard_map/all_to_all | solution.py:382
  28.7 1.1 %push_updates.1 = bf16[8,80,256]{2,1,0:T(8,128)(2,1)} custom-call(bf16[2304,128]{1,0:T(8,128)(2,1)S(1)} %bitcast.16, bf16[320,1536]{1,0:T(8,128)(2,1)S(1)} %get-tuple-element.10.refs_1_, bf16[112,256]{1,0:T(8,128)(2,1)S(1)} %get-tuple-element.11.refs_2_), custom_call_target="tpu_custom_call" | custom-call | flops 150994944 | bytes 1703936 | tf_op jit(solution)/shard_map/push_updates/pallas_call | solution.py:420
  29.8 3.4 %all-to-all-start.1 = ((bf16[8,80,256]{2,1,0:T(8,128)(2,1)}), bf16[8,80,256]{2,1,0:T(8,128)(2,1)S(1)}, u32[]{:S(2)}, u32[]{:S(2)}) async-start(bf16[8,80,256]{2,1,0:T(8,128)(2,1)} %push_updates.1), calls=%async_computation.1 | async-start | bytes 655360 | tf_op jit(solution)/shard_map/all_to_all | solution.py:429
  33.3 2.5 %leaf_forward.1.y_ref = bf16[256,1152]{1,0:T(8,128)(2,1)S(1)} custom-call(s32[1,1536]{1,0:T(1,128)S(1)} %reshape.19.place_ref.refs_0_, bf16[2304,128]{1,0:T(8,128)(2,1)S(1)} %bitcast.17, bf16[3200,256]{1,0:T(8,128)(2,1)S(1)} %get-tuple-element.12.refs_2_.packed_ref), custom_call_target="tpu_custom_call" | custom-call | flops 1585446912 | bytes 4227072 | tf_op jit(solution)/shard_map/leaf_forward/pallas_call | solution.py:430
  35.8 3.9 %all-to-all-done.1.got_ref = bf16[8,80,256]{2,1,0:T(8,128)(2,1)S(1)} async-done(((bf16[8,80,256]{2,1,0:T(8,128)(2,1)}), bf16[8,80,256]{2,1,0:T(8,128)(2,1)S(1)}, u32[]{:S(2)}, u32[]{:S(2)}) %all-to-all-start.1) | async-done | bytes 327712 | tf_op jit(solution)/shard_map/all_to_all | solution.py:429
  39.7 3.3 %collective-permute-start = (bf16[8,80,256]{2,1,0:T(8,128)(2,1)S(1)}, bf16[8,80,256]{2,1,0:T(8,128)(2,1)S(1)}, u32[]{:S(2)}, u32[]{:S(2)}) collective-permute-start(bf16[8,80,256]{2,1,0:T(8,128)(2,1)S(1)} %all-to-all-done.1.got_ref), channel_id=1, source_target_pairs={{0,1},{1,0},{2,3},{3,2},{4,5},{5,4},{6,7},{7,6},{8,9},{9,8},{10,11... | collective-permute-start | bytes 983048 | tf_op jit(solution)/shard_map/ppermute | solution.py:440
  43.0 0.8 %leaf_backward.1.bare_hbm.leaf_ref = f32[1152,256]{1,0:T(8,128)S(1)} custom-call(bf16[256,1152]{1,0:T(8,128)(2,1)S(1)} %leaf_forward.1.y_ref, bf16[3200,256]{1,0:T(8,128)(2,1)S(1)} %get-tuple-element.12.refs_2_.packed_ref), custom_call_target="tpu_custom_call" | custom-call | flops 679477248 | bytes 4423680 | tf_op jit(solution)/shard_map/leaf_backward/pallas_call | solution.py:442
  43.8 0.0 copy-start.1
  43.8 0.5 collective-permute-done.other_ref
  44.3 2.4 %separator_tree.1 = bf16[8,32,256]{2,1,0:T(8,128)(2,1)S(1)} custom-call(s32[1]{0:T(128)} %bitcast.front_ref, bf16[8,80,256]{2,1,0:T(8,128)(2,1)S(1)} %all-to-all-done.1.got_ref, bf16[8,80,256]{2,1,0:T(8,128)(2,1)S(1)} %collective-permute-done.other_ref, f32[1152,256]{1,0:T(8,128)S(1)} %leaf_backward.1.bare_hbm.leaf_ref), custom_call_target="tpu_custom_call" | custom-call | flops 150994944 | bytes 786432 | tf_op jit(solution)/shard_map/separator_tree/pallas_call | solution.py:451
  46.7 7.8 %all_to_all.15.got_ref = bf16[8,32,256]{2,1,0:T(8,128)(2,1)S(1)} all-to-all(bf16[8,32,256]{2,1,0:T(8,128)(2,1)S(1)} %separator_tree.1), channel_id=1, replica_groups=mesh['tree'=8,'peer'=8,'front'=2] {'peer'}, dimensions={0} | all-to-all | bytes 262144 | tf_op jit(solution)/shard_map/all_to_all | solution.py:460
  54.5 0.0 copy-done.1
  54.5 1.4 %finish.1 = (f32[1152,256]{1,0:T(8,128)}, bf16[3,16,256]{2,1,0:T(8,128)(2,1)}) custom-call(bf16[8,32,256]{2,1,0:T(8,128)(2,1)S(1)} %all_to_all.15.got_ref, bf16[1152,256]{1,0:T(8,128)(2,1)S(1)} %copy-done.1, f32[1152,256]{1,0:T(8,128)S(1)} %leaf_backward.1.bare_hbm.leaf_ref), custom_call_target="tpu_custom_call" | custom-call | flops 150994944 | bytes 3080192 | tf_op jit(solution)/shard_map/finish/pallas_call | solution.py:462
  (2 shorter events, 0.0 us)
Async XLA Ops:
  0.6 15.2 %copy-start.9 = (s32[1,1,1152]{2,1,0:T(1,128)S(1)}, s32[1,1,1152]{2,1,0:T(1,128)}, u32[]{:S(2)}) copy-start(s32[1,1,1152]{2,1,0:T(1,128)} %param.12) | copy-start | bytes 13828
  0.6 15.5 %copy-start.4 = (bf16[1,1,3,16,256]{4,3,2,1,0:T(8,128)(2,1)S(1)}, bf16[1,1,3,16,256]{4,3,2,1,0:T(8,128)(2,1)}, u32[]{:S(2)}) copy-start(bf16[1,1,3,16,256]{4,3,2,1,0:T(8,128)(2,1)} %param.13) | copy-start | bytes 73732
  0.7 15.5 %copy-start.5 = (bf16[1,1,32,224]{3,2,1,0:T(8,128)(2,1)S(1)}, bf16[1,1,32,224]{3,2,1,0:T(8,128)(2,1)}, u32[]{:S(2)}) copy-start(bf16[1,1,32,224]{3,2,1,0:T(8,128)(2,1)} %param.17) | copy-start | bytes 43012
  0.7 15.5 %copy-start.6 = (bf16[1,1,3,64,16]{3,4,2,1,0:T(8,128)(2,1)S(1)}, bf16[1,1,3,64,16]{3,4,2,1,0:T(8,128)(2,1)}, u32[]{:S(2)}) copy-start(bf16[1,1,3,64,16]{3,4,2,1,0:T(8,128)(2,1)} %param.18) | copy-start | bytes 18436
  0.7 15.5 %copy-start.7 = (s32[1,1,3,64]{3,1,2,0:T(1,128)S(1)}, s32[1,1,3,64]{3,1,2,0:T(1,128)}, u32[]{:S(2)}) copy-start(s32[1,1,3,64]{3,1,2,0:T(1,128)} %param.16) | copy-start | bytes 2308
  0.7 15.5 %copy-start.8 = (s32[1,1,3,64]{3,1,2,0:T(1,128)S(1)}, s32[1,1,3,64]{3,1,2,0:T(1,128)}, u32[]{:S(2)}) copy-start(s32[1,1,3,64]{3,1,2,0:T(1,128)} %param.19) | copy-start | bytes 2308
  3.8 24.8 %all-to-all-start = ((bf16[64,9,4,128]{3,2,1,0:T(4,128)(2,1)}), bf16[64,9,4,128]{3,2,1,0:T(4,128)(2,1)S(1)}, u32[]{:S(2)}, u32[]{:S(2)}) async-start(bf16[64,9,4,128]{3,2,1,0:T(4,128)(2,1)} %bitcast.25), calls=%async_computation | async-start | bytes 1179648 | tf_op jit(solution)/shard_map/all_to_all | solution.py:382
  16.2 1.8 %copy-start.2 = (bf16[1,1,1152,1152]{3,2,1,0:T(8,128)(2,1)S(1)}, bf16[1,1,1152,1152]{3,2,1,0:T(8,128)(2,1)}, u32[]{:S(2)}) copy-start(bf16[1,1,1152,1152]{3,2,1,0:T(8,128)(2,1)} %param.14) | copy-start | bytes 7962628
  17.9 1.0 %copy-start.3 = (bf16[1,1,3,64,1152]{4,3,2,1,0:T(8,128)(2,1)S(1)}, bf16[1,1,3,64,1152]{4,3,2,1,0:T(8,128)(2,1)}, u32[]{:S(2)}) copy-start(bf16[1,1,3,64,1152]{4,3,2,1,0:T(8,128)(2,1)} %param.15) | copy-start | bytes 1327108
  21.6 0.8 %copy-start = (bf16[1152,256]{1,0:T(8,128)(2,1)}, bf16[1152,256]{1,0:T(8,128)(2,1)S(1)}, u32[]{:S(2)}) copy-start(bf16[1152,256]{1,0:T(8,128)(2,1)S(1)} %get-tuple-element.15.back_ref) | copy-start | bytes 1769476
  29.8 9.9 %all-to-all-start.1 = ((bf16[8,80,256]{2,1,0:T(8,128)(2,1)}), bf16[8,80,256]{2,1,0:T(8,128)(2,1)S(1)}, u32[]{:S(2)}, u32[]{:S(2)}) async-start(bf16[8,80,256]{2,1,0:T(8,128)(2,1)} %push_updates.1), calls=%async_computation.1 | async-start | bytes 655360 | tf_op jit(solution)/shard_map/all_to_all | solution.py:429
  39.7 4.5 %collective-permute-start = (bf16[8,80,256]{2,1,0:T(8,128)(2,1)S(1)}, bf16[8,80,256]{2,1,0:T(8,128)(2,1)S(1)}, u32[]{:S(2)}, u32[]{:S(2)}) collective-permute-start(bf16[8,80,256]{2,1,0:T(8,128)(2,1)S(1)} %all-to-all-done.1.got_ref), channel_id=1, source_target_pairs={{0,1},{1,0},{2,3},{3,2},{4,5},{5,4},{6,7},{7,6},{8,9},{9,8},{10,11... | collective-permute-start | bytes 983048 | tf_op jit(solution)/shard_map/ppermute | solution.py:440
  43.8 10.8 %copy-start.1 = (bf16[1152,256]{1,0:T(8,128)(2,1)S(1)}, bf16[1152,256]{1,0:T(8,128)(2,1)}, u32[]{:S(2)}) copy-start(bf16[1152,256]{1,0:T(8,128)(2,1)} %copy-done) | copy-start | bytes 1769476
